TPU v7x, 32 devices: a whole 2x2x4 slice. The times are simulated.
32 devices in a mesh: strata: 4 (over y, core), chain: 8 (over z, x).
Axes of the slice: x: 2, y: 2, z: 4, core: 2. Of those that a mesh axis runs over, the one named last changes fastest.
Arguments:
- features: bfloat16 [65536, 512], P(('strata', 'chain')), may hold values from -6 to 6
- events: int32 [65536, 35], P(('strata', 'chain')), may hold values from 0 to 32767, as said below
- tie_first: int32 [65536], P(('strata', 'chain')), may hold values from 0 to 16383, as said below
- entry_row: int32 [65536], P(('strata', 'chain')), may hold values from 0 to 16383, as said below
- w_in: bfloat16 [512, 512], replicated, may hold values from -0.25 to 0.25
- w_mid: bfloat16 [512, 512], replicated, may hold values from -0.25 to 0.25
- w_out: bfloat16 [512, 512], replicated, may hold values from -0.25 to 0.25
Outputs:
- endpoint_loss: float32 [512], replicated
- grad_x: bfloat16 [65536, 512], P(('strata', 'chain'))
- grad_in: float32 [512, 512], replicated
- grad_mid: float32 [512, 512], replicated
- grad_out: float32 [512, 512], replicated
Inputs may be any that keep to these rules, and one draw needn't show every extreme that they name: Bit b of events[i, k] is row i's event indicator for endpoint 15 k + b; bits 15 and above, and bits for endpoints 512 and beyond, are zero. Groups of equal stop time are runs of consecutive rows lying inside aligned blocks of 2048 rows; tie_first[i] is the first row of row i's run, counted within its stratum. An interval is at risk at the stop time of row k's group exactly when entry_row <= tie_first[k] and the interval's row is >= tie_first[k]. For every row, tie_first[i] - 2048 < entry_row[i] <= tie_first[i]; in every aligned block of 2048 rows some row has entry_row = max(tie_first - 1 * 2048 + 1, 0).
All inputs are finite; a program needn't handle non-finite values.
Results may differ from a plain program's by a relative error of at most 0.006.
The roundings to bfloat16 on the way count: a program that leaves them out, or rounds other values in their place, can miss the bound.
Values sent between devices are 32-bit elements; how exact they have to be, the bound alone decides.
No kernel may reach another device: no remote copies, remote signals or barrier semaphores. Data moves between devices by JAX's collectives and lax.ppermute only.
A program may use at most 128 MiB of HBM per device.

v0:
```python
import jax
import jax.numpy as jnp
from jax import lax
from jax.sharding import PartitionSpec as P

BACK = 1


def from_behind(block, axis, distance):
    devices = range(lax.axis_size(axis))
    route = [(i - distance, i) for i in devices if i - distance in devices]
    return lax.ppermute(block, axis, route)


def unpack_events(events, out_width):
    column = jnp.arange(out_width, dtype=jnp.int32)
    spread = jnp.repeat(events, 15, axis=1)[:, :out_width]
    return jnp.bitwise_and(jnp.right_shift(spread, column % 15), 1)


def silu_slope(value):
    sigma = jax.nn.sigmoid(value)
    return sigma * (1.0 + value * (1.0 - sigma))


def on_device(features, events, tie_first, entry_row, w_in, w_mid, w_out):
    block_rows = features.shape[0]
    out_width = w_out.shape[1]
    chain_len = lax.axis_size("chain")
    position = lax.axis_index("chain")
    total_rows = block_rows * chain_len * lax.axis_size("strata")
    block_start = position * block_rows
    look_back = BACK
    window = (look_back + 1) * block_rows
    device_ids = jnp.arange(chain_len, dtype=jnp.int32)[:, None]
    preact = jnp.dot(features, w_in, preferred_element_type=jnp.float32)
    first_hidden = jax.nn.silu(preact).astype(jnp.bfloat16)
    mid_pre = jnp.dot(first_hidden, w_mid, preferred_element_type=jnp.float32)
    hidden = jax.nn.silu(mid_pre).astype(jnp.bfloat16)
    log_hazard = jnp.dot(hidden, w_out, preferred_element_type=jnp.float32)
    weight = jnp.exp(log_hazard)
    indicator = unpack_events(events, out_width).astype(jnp.float32)
    target = entry_row - (position - look_back) * block_rows
    landed = jax.ops.segment_sum(weight, target, num_segments=window)
    entered = landed[look_back * block_rows :]
    distance = 1
    portion = landed[(look_back - distance) * block_rows : (look_back - distance + 1) * block_rows]
    entered = entered + from_behind(portion, "chain", -distance)
    local_suffix = lax.cumsum(weight - entered, axis=0, reverse=True)
    totals = lax.all_gather(local_suffix[0][None, :], "chain", axis=0, tiled=True)
    beyond = jnp.sum(jnp.where(device_ids > position, totals, 0.0), axis=0)
    at_risk = beyond + local_suffix + entered
    local_first = tie_first - block_start
    divisor = jnp.take(at_risk, local_first, axis=0)
    loss_part = jnp.sum(indicator * (jnp.log(divisor) - log_hazard), axis=0) / total_rows
    hazard = indicator / divisor
    grouped = jax.ops.segment_sum(hazard, local_first, num_segments=block_rows)
    inclusive = lax.cumsum(grouped, axis=0)
    totals = lax.all_gather(inclusive[-1][None, :], "chain", axis=0, tiled=True)
    before = jnp.sum(jnp.where(device_ids < position, totals, 0.0), axis=0)
    own_block = before + inclusive - grouped
    blocks = [own_block]
    distance = 1
    blocks = [from_behind(own_block, "chain", distance)] + blocks
    stacked = jnp.concatenate(blocks, axis=0)
    exposure = before + inclusive - jnp.take(stacked, target, axis=0)
    eta_grad = (weight * exposure - indicator).astype(jnp.bfloat16)
    factor = total_rows ** (-0.5)
    grad_out = (
        jnp.einsum("rh,re->he", hidden, eta_grad, preferred_element_type=jnp.float32) * factor
    )
    hidden_grad = jnp.einsum("re,he->rh", eta_grad, w_out, preferred_element_type=jnp.float32)
    mid_grad = (hidden_grad * silu_slope(mid_pre)).astype(jnp.bfloat16)
    grad_mid = (
        jnp.einsum("rg,rh->gh", first_hidden, mid_grad, preferred_element_type=jnp.float32) * factor
    )
    first_grad = jnp.einsum("rh,gh->rg", mid_grad, w_mid, preferred_element_type=jnp.float32)
    pre_grad = (first_grad * silu_slope(preact)).astype(jnp.bfloat16)
    grad_in = (
        jnp.einsum("rf,rh->fh", features, pre_grad, preferred_element_type=jnp.float32) * factor
    )
    grad_x = jnp.einsum("rh,fh->rf", pre_grad, w_in, preferred_element_type=jnp.float32).astype(
        jnp.bfloat16
    )
    grad_in, grad_mid, grad_out, endpoint_loss = lax.psum(
        (grad_in, grad_mid, grad_out, loss_part), ("strata", "chain")
    )
    return (endpoint_loss, grad_x, grad_in, grad_mid, grad_out)


def solution(mesh):
    placed = (
        P(("strata", "chain"), None),
        P(("strata", "chain"), None),
        P(("strata", "chain")),
        P(("strata", "chain")),
        P(),
        P(),
        P(),
    )
    return jax.shard_map(
        on_device,
        mesh=mesh,
        in_specs=placed,
        out_specs=(P(), P(("strata", "chain"), None), P(), P(), P()),
        check_vma=False,
    )
```

profile of v0, /device:TPU:0, one launch (start us, length us, event | category | flops | bytes accessed | tf_op | source)
XLA Modules:
  0.0 536.3 jit_solution(14117314422717302577)
XLA Ops:
  8.8 4.8 multiply_convert_fusion.3
  13.6 3.8 multiply_convert_fusion.2
  17.4 3.3 fusion.24
  20.7 17.5 %scatter_custom_fusion = f32[4096,512]{1,0:T(8,128)} fusion(s32[2048]{0:T(1024)S(1)} %get-tuple-element.24, f32[]{:T(128)} %constant.62.clone.1, f32[2048,512]{1,0:T(8,128)} %fusion.24), kind=kCustom, calls=%fused_computation.17 | custom fusion | flops 1048576 | bytes 12582916 | tf_op jit(solution)/shard_map/scatter-add | solution.py:44
  38.2 4.7 slice.42
  44.4 2.7 broadcast_in_dim.60
  47.1 4.0 reshape.64
  51.1 4.7 slice.40
  55.8 5.4 copy.32
  61.2 77.5 %collective-permute-done = f32[2048,512]{1,0:T(8,128)} collective-permute-done((f32[2048,512]{1,0:T(8,128)}, f32[2048,512]{1,0:T(8,128)}, u32[]{:S(2)}, u32[]{:S(2)}) %collective-permute-start) | collective-permute-done | bytes 4194336 | tf_op jit(solution)/shard_map/ppermute | solution.py:12
  138.6 6.2 %exponential_subtract_fusion = f32[2048,512]{1,0:T(8,128)S(1)} fusion(f32[2048,512]{1,0:T(8,128)} %fusion.24, f32[2048,512]{1,0:T(8,128)} %collective-permute-done, f32[4096,512]{1,0:T(8,128)} %scatter_custom_fusion), kind=kLoop, calls=%fused_computation.27 | loop fusion | flops 2097152 | bytes 16777216 | tf_op jit(solution)/shard_map/sub | solution.py:49
  144.9 10.1 %fusion.2 = f32[512,16,128]{0,1,2:T(8,128)S(1)} fusion(f32[512,16,128]{0,2,1:T(8,128)S(1)} %bitcast.58), kind=kOutput, calls=%fused_computation.8 | output fusion | flops 133169152 | bytes 8388608 | tf_op jit(solution)/shard_map/reduce-window
  157.1 2.9 broadcast_add_fusion.1
  160.0 2.4 copy.26
  162.4 26.8 %all-gather = f32[8,1,512]{2,1,0:T(1,128)S(1)} all-gather(f32[1,1,512]{2,1,0:T(1,128)S(1)} %slice_bitcast_fusion.3), channel_id=1, replica_groups=mesh['strata'=4,'chain'=8] {'chain'}, dimensions={0}, use_global_device_ids=true | all-gather | bytes 18432 | tf_op jit(solution)/shard_map/all_gather | solution.py:50
  189.3 5.6 %add_add_fusion = f32[2048,512]{1,0:T(8,128)} fusion(f32[512]{0:T(512)S(1)} %fusion.18, f32[2048,512]{1,0:T(8,128)} %collective-permute-done, f32[4096,512]{1,0:T(8,128)S(1)} %bitcast.54, f32[512,16,128]{0,2,1:T(8,128)S(1)} %copy.26), kind=kLoop, calls=%fused_computation.16 | loop fusion | flops 3145728 | bytes 16779264 | tf_op jit(solution)/shard_map/add | solution.py:52
  194.9 11.7 %gather_fusion = f32[2048,512]{1,0:T(8,128)} fusion(f32[2048,512]{1,0:T(8,128)} %add_add_fusion, s32[2048]{0:T(1024)S(1)} %fusion.19), kind=kCustom, calls=%fused_computation | custom fusion | bytes 8396800 | tf_op jit(solution)/shard_map/jit(_take)/gather | solution.py:54
  206.7 17.6 %scatter_custom_fusion.1 = f32[2048,512]{1,0:T(8,128)} fusion(s32[2048]{0:T(1024)S(1)} %get-tuple-element.26, f32[2048,512]{1,0:T(8,128)} %gather_fusion, s32[2048,512]{1,0:T(8,128)} %copy.32, f32[]{:T(128)} %constant.62.clone.1, f32[]{:T(128)} %constant.64.clone.1, s32[]{:T(128)} %constant.39.clone.1, s32[512]{0:T(512)S(1)} %add_select_fusion, ...), kind=kCustom, calls=%fused_computation.13 | custom fusion | flops 6291456 | bytes 12587020 | tf_op jit(solution)/shard_map/scatter-add | solution.py:57
  224.2 4.6 fusion
  230.9 2.7 broadcast_add_fusion
  233.6 2.4 copy.28
  236.0 26.0 %all-gather.1 = f32[8,1,512]{2,1,0:T(1,128)S(1)} all-gather(f32[1,1,512]{2,1,0:T(1,128)S(1)} %slice_bitcast_fusion.2), channel_id=1, replica_groups=mesh['strata'=4,'chain'=8] {'chain'}, dimensions={0}, use_global_device_ids=true | all-gather | bytes 18432 | tf_op jit(solution)/shard_map/all_gather | solution.py:59
  265.3 79.2 %collective-permute-done.1 = f32[2048,512]{1,0:T(8,128)S(1)} collective-permute-done((f32[2048,512]{1,0:T(8,128)S(1)}, f32[2048,512]{1,0:T(8,128)S(1)}, u32[]{:S(2)}, u32[]{:S(2)}) %collective-permute-start.1) | collective-permute-done | bytes 4194336 | tf_op jit(solution)/shard_map/ppermute | solution.py:12
  344.5 4.2 pad_maximum_fusion
  348.7 12.9 %gather_fusion.1 = f32[2048,512]{1,0:T(8,128)} fusion(f32[4096,512]{1,0:T(8,128)} %pad_maximum_fusion, s32[2048]{0:T(1024)S(1)} %fusion.20), kind=kCustom, calls=%fused_computation.1 | custom fusion | bytes 8396800 | tf_op jit(solution)/shard_map/jit(_take)/gather | solution.py:66
  361.6 8.5 %subtract_convert_fusion = (bf16[2048,512]{1,0:T(8,128)(2,1)S(1)}, f32[512]{0:T(512)S(1)}) fusion(f32[2048,512]{1,0:T(8,128)} %gather_fusion.1, f32[2048,512]{1,0:T(8,128)} %fusion.24, s32[2048,512]{1,0:T(8,128)} %copy.32, f32[512]{0:T(512)S(1)} %fusion.17, s32[512]{0:T(512)S(1)} %add_select_fusion, pred[2048]{0:T(1024)(128)(4,1)S(1)} %get-tuple-element.23, ...), kind=kLoop, calls=%fused_computation.12 | loop fusion | flops 13630976 | bytes 23078912 | tf_op jit(solution)/shard_map/convert_element_type | solution.py:67
  372.4 2.4 multiply_convert_fusion.1
  377.0 2.4 multiply_convert_fusion
  383.0 41.4 %psum.28 = f32[512]{0:T(512)} all-reduce(f32[512]{0:T(512)S(1)} %broadcast_multiply_fusion), channel_id=1, replica_groups=mesh['strata'=4,'chain'=8] {'strata','chain'}, use_global_device_ids=true, to_apply=%region_5.6 | all-reduce | flops 512 | bytes 4096 | tf_op jit(solution)/shard_map/psum | solution.py:85
  424.4 4.2 convolution_convert_fusion
  428.6 94.5 %all-reduce.3.cloned.1.call-done = (f32[512,512]{0,1:T(8,128)}, f32[512,512]{1,0:T(8,128)}, f32[512,512]{1,0:T(8,128)}) async-done(((f32[512,512]{0,1:T(8,128)}, f32[512,512]{1,0:T(8,128)}, f32[512,512]{1,0:T(8,128)}), (f32[512,512]{0,1:T(8,128)}, f32[512,512]{1,0:T(8,128)}, f32[512,512]{1,0:T(8,128)})) %all-reduce.3.cloned.1.call-update) | async-done | bytes 3145744 | tf_op jit(solution)/shard_map/psum | solution.py:85
  523.1 2.6 copy.29
  (69 shorter events, 21.8 us)
Async XLA Ops:
  7.2 1.6 copy-start
  7.2 515.9 %all-reduce.3.cloned.1.call-start = ((), (), s32[]{:S(2)}) async-start(), calls=%async_computation | async-start | bytes 6291456 | tf_op jit(solution)/shard_map/psum | solution.py:85
  8.8 4.8 copy-start.11
  13.6 3.8 copy-start.13
  13.6 3.8 copy-start.8
  17.4 3.3 copy-start.5
  38.2 6.2 %copy-start.9 = (s32[2048,35]{0,1:T(8,128)S(1)}, s32[2048,35]{0,1:T(8,128)}, u32[]{:S(2)}) copy-start(s32[2048,35]{0,1:T(8,128)} %param.8) | copy-start | bytes 860164
  42.9 95.7 %collective-permute-start = (f32[2048,512]{1,0:T(8,128)}, f32[2048,512]{1,0:T(8,128)}, u32[]{:S(2)}, u32[]{:S(2)}) collective-permute-start(f32[2048,512]{1,0:T(8,128)} %slice.42), channel_id=1, source_target_pairs={{1,0},{2,1},{3,2},{4,3},{5,4},{6,5},{7,6},{9,8},{10,9},{11,10},{12... | collective-permute-start | bytes 12582920 | tf_op jit(solution)/shard_map/ppermute | solution.py:12
  55.8 5.4 %copy-start.10 = (s32[2048]{0:T(1024)S(1)}, s32[2048]{0:T(1024)}, u32[]{:S(2)}) copy-start(s32[2048]{0:T(1024)} %param.9) | copy-start | bytes 24580
  155.0 1.9 copy-start.3
  157.0 32.2 %slice-start = ((s8[8388608]{0:T(1024)(128)(4,1)}), s8[4194304]{0:T(1024)(128)(4,1)S(1)}, s32[]{:S(2)}) async-start(s8[8388608]{0:T(1024)(128)(4,1)} %bitcast.53), calls=%async_computation.1 | async-start | bytes 8388608
  159.9 29.3 %slice-start.1 = ((s8[8388608]{0:T(1024)(128)(4,1)}), s8[4194304]{0:T(1024)(128)(4,1)S(1)}, s32[]{:S(2)}) async-start(s8[8388608]{0:T(1024)(128)(4,1)} %bitcast.53), calls=%async_computation.2 | async-start | bytes 8388608
  228.8 2.0 copy-start.4
  233.6 28.6 %copy-start.2 = (f32[2048,512]{1,0:T(8,128)S(1)}, f32[2048,512]{1,0:T(8,128)}, u32[]{:S(2)}) copy-start(f32[2048,512]{1,0:T(8,128)} %scatter_custom_fusion.1) | copy-start | bytes 12582916
  236.0 27.2 %copy-start.1 = (f32[512,16,128]{0,2,1:T(8,128)}, f32[512,16,128]{0,2,1:T(8,128)S(1)}, u32[]{:S(2)}) copy-start(f32[512,16,128]{0,2,1:T(8,128)S(1)} %copy.28) | copy-start | bytes 12582916
  263.2 81.3 %collective-permute-start.1 = (f32[2048,512]{1,0:T(8,128)S(1)}, f32[2048,512]{1,0:T(8,128)S(1)}, u32[]{:S(2)}, u32[]{:S(2)}) collective-permute-start(f32[2048,512]{1,0:T(8,128)S(1)} %add_subtract_fusion), channel_id=1, source_target_pairs={{0,1},{1,2},{2,3},{3,4},{4,5},{5,6},{6,7},{8,9},{9,10},{10,11},{11... | collective-permute-start | bytes 12582920 | tf_op jit(solution)/shard_map/ppermute | solution.py:12
  361.6 8.6 %copy-start.6 = (bf16[2048,512]{1,0:T(8,128)(2,1)S(1)}, bf16[2048,512]{1,0:T(8,128)(2,1)}, u32[]{:S(2)}) copy-start(bf16[2048,512]{1,0:T(8,128)(2,1)} %copy-done.5) | copy-start | bytes 6291460
  370.1 2.3 copy-start.17
  372.4 2.4 copy-start.14
  374.8 2.3 copy-start.16
  379.4 1.3 copy-start.15
  380.7 43.7 %copy-start.12 = (bf16[512,512]{1,0:T(8,128)(2,1)S(1)}, bf16[512,512]{1,0:T(8,128)(2,1)}, u32[]{:S(2)}) copy-start(bf16[512,512]{1,0:T(8,128)(2,1)} %param.11) | copy-start | bytes 1572868
  523.1 4.9 copy-start.7
Sparse Core Ops, SparseCore 0:
  383.1 139.9 all-reduce.2
where the time goes:
time: 543 us; the launch traced here: 536 us
  waiting for transfers between devices  251 us (46%)
  blocking collectives  94.2 us (17%)
  other arithmetic  82.2 us (15%)
  local copies, waits for them, and re-layouts  62.8 us (12%)
  matrix products  27.5 us (5%)
  between operations  14.8 us (3%)
    ppermute x2, waiting for transfers between devices, from_behind(): return lax.ppermute(block, axis, route)  157 us
    psum x1, waiting for transfers between devices, on_device(): lax.psum((grad_in, grad_mid, grad_out, loss_part), ('strata', 'chain'))  94.5 us
    psum x1, blocking collectives, on_device(): lax.psum((grad_in, grad_mid, grad_out, loss_part), ('strata', 'chain'))  41.4 us
    all_gather x1, blocking collectives, on_device(): lax.all_gather(local_suffix[0][None, :], 'chain', axis=0, tiled=True)  26.8 us
    all_gather x1, blocking collectives, on_device(): totals = lax.all_gather(inclusive[-1][None, :], 'chain', axis=0, tiled=True)  26 us
    scatter-add x1, other arithmetic, on_device(): grouped = jax.ops.segment_sum(hazard, local_first, num_segments=block_rows)  17.6 us
    scatter-add x1, other arithmetic, on_device(): landed = jax.ops.segment_sum(weight, target, num_segments=window)  17.5 us
    unnamed x46, local copies, waits for them, and re-layouts  17.2 us
  transfers between devices with their start and end apart: 3, of which 3 were waited for; matrix products, arithmetic and copies ran while one was open for 4% of the time, Pallas kernels for 0%

commit v1 on v0

v1 whole, which is shorter than its diff:
```python
from functools import partial

import jax
import jax.numpy as jnp
import numpy as np
from jax import lax
from jax.experimental import pallas as pl
from jax.experimental.pallas import tpu as pltpu
from jax.sharding import PartitionSpec as P

BITS = 15
LANES = 128
TILE = 256
DEPTH = 512
GROUP = 256
VMEM_BYTES = 48 * 1024 * 1024
F32 = jnp.float32
BF16 = jnp.bfloat16
I32 = jnp.int32


def two_parts(value):
    top = value.astype(BF16)
    return top, (value - top.astype(F32)).astype(BF16)


def iota(shape, dim):
    return lax.broadcasted_iota(I32, shape, dim)


def ones_where(mask):
    return jnp.where(mask, 1.0, 0.0).astype(BF16)


def dot(a, b, ca=1, cb=0):
    return lax.dot_general(a, b, (((ca,), (cb,)), ((), ())), preferred_element_type=F32)


def widen(column, width):
    return jnp.concatenate([column] * (width // column.shape[1]), axis=1)


def as_column(row):
    parts = [
        jnp.broadcast_to(row[:, k : k + LANES], (LANES, LANES)).T
        for k in range(0, row.shape[1], LANES)
    ]
    return jnp.concatenate(parts, axis=0)


def whole(shape):
    return pl.BlockSpec(shape, lambda i: (0,) * len(shape))


def rows_of(tile, width):
    return pl.BlockSpec((tile, width), lambda i: (i, 0))


def params():
    return pltpu.CompilerParams(vmem_limit_bytes=VMEM_BYTES)


def rank_entries(entry_ref, first_ref, entry_col, first_col, rank_col, rank_row, send, note, cap):
    rows = entry_ref.shape[1]
    high = rows // LANES
    entry_col[...] = as_column(entry_ref[...])
    first_col[...] = as_column(first_ref[...])
    row = entry_ref[...]
    col = entry_col[...]
    crosses_row = row < 0
    crosses = col < 0
    place_row = row + rows
    place = col + rows
    high_row = ones_where((iota((high, rows), 0) == (place_row >> 7)) & crosses_row)
    lane = iota((rows, LANES), 1)
    low_col = jnp.where((lane == (place & (LANES - 1))) & crosses, 1.0, 0.0)
    high_col = ones_where((lane == (place >> 7)) & crosses)
    present = ones_where(dot(high_row, low_col.astype(BF16)) > 0.5)
    square = (LANES, LANES)
    within = dot(present, ones_where(iota(square, 0) < iota(square, 1)))
    small = (high, high)
    ahead = dot(ones_where(iota(small, 1) < iota(small, 0)), present)
    table = within + jnp.sum(ahead, axis=1, keepdims=True)
    table = jnp.concatenate([table, jnp.zeros((LANES - high, LANES), F32)], axis=0)
    table_high = jnp.floor(table * (1.0 / 256.0))
    table_low = table - 256.0 * table_high
    ones = jnp.ones(square, BF16)
    found_high = dot(high_col, table_high.astype(BF16)) * low_col
    found_low = dot(high_col, table_low.astype(BF16)) * low_col
    rank = 256.0 * dot(found_high.astype(BF16), ones) + dot(found_low.astype(BF16), ones)
    rank_col[...] = jnp.where(crosses, rank.astype(I32), -1)
    for k in range(0, rows, LANES):
        rank_row[:, k : k + LANES] = rank_col[k : k + LANES, :].T[0:8]
    count = jnp.sum(present.astype(F32))
    note[...] = jnp.where(iota(note.shape, 0) == 1, jnp.where(count > cap, 1.0, 0.0), 0.0)
    send[cap:, :] = jnp.zeros((send.shape[0] - cap, send.shape[1]), F32)

    def entries(t, _):
        hit = widen(rank_col[...], GROUP) == iota((rows, GROUP), 1) + t * GROUP
        found = jnp.max(jnp.where(hit, widen(entry_col[...] + rows, GROUP), 0), axis=0, keepdims=True)
        send[pl.ds(cap + t, 1), 0:GROUP] = found.astype(F32)
        return 0

    lax.fori_loop(0, cap // GROUP, entries, 0)


def trunk_kernel(
    cap, entry_ref, first_ref, x_ref, events_ref, low_ref, high_ref, shift_ref, w_in, w_mid, w_out,
    first_hidden, hidden, slope_in, slope_mid, weight_out, indicator_out, weight_top, weight_rest,
    send, note, entry_col, first_col, rank_col, rank_row,
):
    step = pl.program_id(0)
    tile = x_ref.shape[0]

    @pl.when(step == 0)
    def _():
        rank_entries(entry_ref, first_ref, entry_col, first_col, rank_col, rank_row, send, note, cap)

    events = events_ref[...]
    spread = dot((events & 255).astype(F32).astype(BF16), low_ref[...])
    spread = spread + dot((events >> 8).astype(F32).astype(BF16), high_ref[...])
    bits = jnp.bitwise_and(jnp.right_shift(spread.astype(I32), shift_ref[...]), 1)
    indicator = bits.astype(F32)
    indicator_out[...] = indicator.astype(BF16)

    preact = dot(x_ref[...], w_in[...])
    sigma = jax.nn.sigmoid(preact)
    first = (preact * sigma).astype(BF16)
    first_hidden[...] = first
    slope_in[...] = sigma * (1.0 + preact * (1.0 - sigma))
    mid_pre = dot(first, w_mid[...])
    sigma = jax.nn.sigmoid(mid_pre)
    second = (mid_pre * sigma).astype(BF16)
    hidden[...] = second
    slope_mid[...] = sigma * (1.0 + mid_pre * (1.0 - sigma))
    log_hazard = dot(second, w_out[...])
    weight = jnp.exp(log_hazard)
    weight_out[...] = weight
    at = pl.ds(pl.multiple_of(step * tile, tile), tile)
    weight_top[at, :], weight_rest[at, :] = two_parts(weight)
    note[0:1, :] -= jnp.sum(indicator * log_hazard, axis=0, keepdims=True)

    @pl.when(step == pl.num_programs(0) - 1)
    def _():
        rows = rank_row.shape[1]

        def total(t, _):
            hit = ones_where(iota((GROUP, rows), 0) + t * GROUP == rank_row[0:1, :])
            at = pl.ds(pl.multiple_of(t * GROUP, GROUP), GROUP)
            send[at, :] = dot(hit, weight_top[...]) + dot(hit, weight_rest[...])
            return 0

        lax.fori_loop(0, cap // GROUP, total, 0)


def trunk(cap, entry, first, features, events, w_in, w_mid, w_out):
    rows, width = features.shape
    mid = w_in.shape[1]
    wide = w_mid.shape[1]
    out_width = w_out.shape[1]
    words = events.shape[1]
    column = np.arange(out_width)
    owner = (np.arange(words)[:, None] == column // BITS).astype(np.float32)
    bit = column % BITS
    low = jnp.asarray(owner * (bit < 8), BF16)
    high = jnp.asarray(owner * (bit >= 8), BF16)
    shift = jnp.asarray((bit % 8)[None, :], I32)
    sent_rows = cap + -(-(cap // GROUP) // 8) * 8
    like = jax.ShapeDtypeStruct
    return pl.pallas_call(
        partial(trunk_kernel, cap),
        grid=(rows // TILE,),
        in_specs=[
            whole((1, rows)), whole((1, rows)), rows_of(TILE, width), rows_of(TILE, words),
            whole((words, out_width)), whole((words, out_width)), whole((1, out_width)),
            whole(w_in.shape), whole(w_mid.shape), whole(w_out.shape),
        ],
        out_specs=[
            rows_of(TILE, mid), rows_of(TILE, wide), rows_of(TILE, mid), rows_of(TILE, wide),
            rows_of(TILE, out_width), rows_of(TILE, out_width), whole((rows, out_width)),
            whole((rows, out_width)), whole((sent_rows, out_width)), whole((8, out_width)),
            whole((rows, LANES)), whole((rows, LANES)), whole((rows, LANES)),
        ],
        out_shape=[
            like((rows, mid), BF16), like((rows, wide), BF16),
            like((rows, mid), F32), like((rows, wide), F32),
            like((rows, out_width), F32), like((rows, out_width), BF16),
            like((rows, out_width), BF16), like((rows, out_width), BF16), like((sent_rows, out_width), F32),
            like((8, out_width), F32), like((rows, LANES), I32),
            like((rows, LANES), I32), like((rows, LANES), I32),
        ],
        scratch_shapes=[pltpu.VMEM((8, rows), I32)],
        compiler_params=params(),
        name="trunk",
    )(entry, first, features, events, low, high, shift, w_in, w_mid, w_out)


def own_risk_kernel(starts, entry_ref, first_col, weight_top, weight_rest, out):
    step = pl.program_id(0)
    tile = out.shape[0]
    rows = weight_top.shape[0]
    first = widen(first_col[...], DEPTH)
    out[...] = jnp.zeros_like(out)

    def part(k, _):
        at = pl.multiple_of(k * DEPTH, DEPTH)
        row = iota((tile, DEPTH), 1) + at
        entry = entry_ref[pl.ds(k, 1), :]
        mask = ones_where((row >= first) & (entry <= first))
        at = pl.ds(at, DEPTH)
        out[...] += dot(mask, weight_top[at, :]) + dot(mask, weight_rest[at, :])
        return 0

    lax.fori_loop(starts[step] // DEPTH, rows // DEPTH, part, 0)


def own_risk(starts, entry, first_col, weight_top, weight_rest):
    rows, width = weight_top.shape
    split = entry.reshape(rows // DEPTH, DEPTH)
    return pl.pallas_call(
        own_risk_kernel,
        grid_spec=pltpu.PrefetchScalarGridSpec(
            num_scalar_prefetch=1,
            grid=(rows // TILE,),
            in_specs=[
                pl.BlockSpec(split.shape, lambda i, s: (0, 0)),
                pl.BlockSpec((TILE, LANES), lambda i, s: (i, 0)),
                pl.BlockSpec((rows, width), lambda i, s: (0, 0)),
                pl.BlockSpec((rows, width), lambda i, s: (0, 0)),
            ],
            out_specs=pl.BlockSpec((TILE, width), lambda i, s: (i, 0)),
        ),
        out_shape=jax.ShapeDtypeStruct((rows, width), F32),
        compiler_params=params(),
        cost_estimate=pl.CostEstimate(
            flops=rows * rows * width * 2, bytes_accessed=rows * width * 8, transcendentals=0
        ),
        name="own_risk",
    )(starts, split, first_col, weight_top, weight_rest)


def own_exposure_kernel(starts, first_ref, entry_col, hazard_top, hazard_rest, out):
    step = pl.program_id(0)
    tile = out.shape[0]
    entry = widen(entry_col[...], DEPTH)
    row = iota((tile, DEPTH), 0) + step * tile
    out[...] = jnp.zeros_like(out)
    last = step * tile + tile - 1
    parts = jnp.int32(0)
    per = DEPTH // tile
    for k in range(first_ref.shape[0]):
        parts += jnp.where(starts[k * per] <= last, 1, 0).astype(I32)

    def part(k, _):
        at = pl.multiple_of(k * DEPTH, DEPTH)
        first = first_ref[pl.ds(k, 1), :]
        mask = ones_where((first >= entry) & (first <= row))
        at = pl.ds(at, DEPTH)
        out[...] += dot(mask, hazard_top[at, :]) + dot(mask, hazard_rest[at, :])
        return 0

    lax.fori_loop(0, parts, part, 0)


def own_exposure(starts, first, entry_col, hazard_top, hazard_rest):
    rows, width = hazard_top.shape
    split = first.reshape(rows // DEPTH, DEPTH)
    return pl.pallas_call(
        own_exposure_kernel,
        grid_spec=pltpu.PrefetchScalarGridSpec(
            num_scalar_prefetch=1,
            grid=(rows // TILE,),
            in_specs=[
                pl.BlockSpec(split.shape, lambda i, s: (0, 0)),
                pl.BlockSpec((TILE, LANES), lambda i, s: (i, 0)),
                pl.BlockSpec((rows, width), lambda i, s: (0, 0)),
                pl.BlockSpec((rows, width), lambda i, s: (0, 0)),
            ],
            out_specs=pl.BlockSpec((TILE, width), lambda i, s: (i, 0)),
        ),
        out_shape=jax.ShapeDtypeStruct((rows, width), F32),
        compiler_params=params(),
        cost_estimate=pl.CostEstimate(
            flops=rows * rows * width * 2, bytes_accessed=rows * width * 8, transcendentals=0
        ),
        name="own_exposure",
    )(starts, split, entry_col, hazard_top, hazard_rest)


def split_sum(source, high, low, cap):
    for t in range(0, cap, GROUP):
        high[t : t + GROUP, :], low[t : t + GROUP, :] = two_parts(source[t : t + GROUP, :])


def hazard_kernel(
    cap, first_ref, first_col, risk, indicator_ref, got, hazard_top, hazard_rest,
    sums, note, high, low,
):
    step = pl.program_id(0)
    tile = risk.shape[0]
    rows = hazard_top.shape[0]

    @pl.when(step == 0)
    def _():
        split_sum(got, high, low, cap)
        note[...] = jnp.zeros_like(note)

    first = widen(first_col[...].astype(F32), GROUP)
    divisor = risk[...]

    def beyond(t, total):
        entry = got[pl.ds(cap + t, 1), 0:GROUP]
        mask = ones_where(entry <= first)
        at = pl.ds(pl.multiple_of(t * GROUP, GROUP), GROUP)
        return total + dot(mask, high[at, :]) + dot(mask, low[at, :])

    divisor = lax.fori_loop(0, cap // GROUP, beyond, divisor)
    indicator = indicator_ref[...].astype(F32)
    note[0:1, :] += jnp.sum(indicator * jnp.log(divisor), axis=0, keepdims=True)
    at = pl.ds(pl.multiple_of(step * tile, tile), tile)
    hazard_top[at, :], hazard_rest[at, :] = two_parts(indicator / divisor)

    @pl.when(step == pl.num_programs(0) - 1)
    def _():
        def total(t, _):
            entry = widen(as_column(got[pl.ds(cap + t, 1), 0:GROUP]), rows)
            mask = ones_where(first_ref[...].astype(F32) >= entry)
            at = pl.ds(pl.multiple_of(t * GROUP, GROUP), GROUP)
            sums[at, :] = dot(mask, hazard_top[...]) + dot(mask, hazard_rest[...])
            return 0

        lax.fori_loop(0, cap // GROUP, total, 0)


def hazards(cap, first, first_col, risk, indicator, got):
    rows, width = risk.shape
    like = jax.ShapeDtypeStruct
    return pl.pallas_call(
        partial(hazard_kernel, cap),
        grid=(rows // TILE,),
        in_specs=[
            whole((1, rows)), rows_of(TILE, LANES), rows_of(TILE, width), rows_of(TILE, width),
            whole(got.shape),
        ],
        out_specs=[
            whole((rows, width)), whole((rows, width)), whole((cap, width)), whole((8, width)),
        ],
        out_shape=[
            like((rows, width), BF16), like((rows, width), BF16),
            like((cap, width), F32), like((8, width), F32),
        ],
        scratch_shapes=[pltpu.VMEM((cap, width), BF16), pltpu.VMEM((cap, width), BF16)],
        compiler_params=params(),
        name="hazards",
    )(first, first_col, risk, indicator, got)


def backward_kernel(
    cap, factor, rank_col, exposure_ref, got, weight, indicator, hidden, slope_mid, first_hidden,
    slope_in, x_ref, w_in, w_mid, w_out, grad_x, grad_in, grad_mid, grad_out, high, low,
):
    step = pl.program_id(0)
    tile = weight.shape[0]

    @pl.when(step == 0)
    def _():
        split_sum(got, high, low, cap)
        grad_in[...] = jnp.zeros_like(grad_in)
        grad_mid[...] = jnp.zeros_like(grad_mid)
        grad_out[...] = jnp.zeros_like(grad_out)

    rank = widen(rank_col[...], GROUP)

    def behind(t, total):
        mask = ones_where(rank == iota((tile, GROUP), 1) + t * GROUP)
        at = pl.ds(pl.multiple_of(t * GROUP, GROUP), GROUP)
        return total + dot(mask, high[at, :]) + dot(mask, low[at, :])

    exposure = lax.fori_loop(0, cap // GROUP, behind, exposure_ref[...])
    eta = (weight[...] * exposure - indicator[...].astype(F32)).astype(BF16)
    grad_out[...] += dot(hidden[...], eta, 0, 0)
    mid = (dot(eta, w_out[...], 1, 1) * slope_mid[...]).astype(BF16)
    grad_mid[...] += dot(first_hidden[...], mid, 0, 0)
    pre = (dot(mid, w_mid[...], 1, 1) * slope_in[...]).astype(BF16)
    grad_in[...] += dot(x_ref[...], pre, 0, 0)
    grad_x[...] = dot(pre, w_in[...], 1, 1).astype(BF16)

    @pl.when(step == pl.num_programs(0) - 1)
    def _():
        grad_in[...] = grad_in[...] * factor
        grad_mid[...] = grad_mid[...] * factor
        grad_out[...] = grad_out[...] * factor


def backward(cap, factor, rank_col, exposure, got, kept, features, w_in, w_mid, w_out):
    weight, indicator, hidden, slope_mid, first_hidden, slope_in = kept
    rows, width = features.shape
    out_width = weight.shape[1]
    like = jax.ShapeDtypeStruct
    tiles = (weight, indicator, hidden, slope_mid, first_hidden, slope_in, features)
    return pl.pallas_call(
        partial(backward_kernel, cap, factor),
        grid=(rows // TILE,),
        in_specs=[rows_of(TILE, LANES), rows_of(TILE, out_width), whole(got.shape)]
        + [rows_of(TILE, a.shape[1]) for a in tiles]
        + [whole(w.shape) for w in (w_in, w_mid, w_out)],
        out_specs=[rows_of(TILE, width), whole(w_in.shape), whole(w_mid.shape), whole(w_out.shape)],
        out_shape=[like((rows, width), BF16)] + [like(w.shape, F32) for w in (w_in, w_mid, w_out)],
        scratch_shapes=[pltpu.VMEM((cap, out_width), BF16), pltpu.VMEM((cap, out_width), BF16)],
        compiler_params=params(),
        name="backward",
    )(rank_col, exposure, got, *tiles, w_in, w_mid, w_out)


def from_behind(block, axis, distance):
    devices = range(lax.axis_size(axis))
    route = [(i - distance, i) for i in devices if i - distance in devices]
    return lax.ppermute(block, axis, route)


def pipeline(cap, total_rows, features, events, first, entry, w_in, w_mid, w_out):
    rows = features.shape[0]
    first_row = first.reshape(1, rows)
    entry_row = entry.reshape(1, rows)
    starts = first[::TILE]
    (
        first_hidden, hidden, slope_in, slope_mid, weight, indicator, weight_top, weight_rest,
        send, note, entry_col, first_col, rank_col,
    ) = trunk(cap, entry_row, first_row, features, events, w_in, w_mid, w_out)
    got = from_behind(send, "chain", -1)
    risk = own_risk(starts, entry, first_col, weight_top, weight_rest)
    hazard_top, hazard_rest, sums, log_part = hazards(cap, first_row, first_col, risk, indicator, got)
    got_sums = from_behind(sums, "chain", 1)
    exposure = own_exposure(starts, first, entry_col, hazard_top, hazard_rest)
    kept = (weight, indicator, hidden, slope_mid, first_hidden, slope_in)
    factor = total_rows ** (-0.5)
    grads = backward(
        cap, factor, rank_col, exposure, got_sums, kept, features, w_in, w_mid, w_out
    )
    return grads, note + log_part


def on_device(features, events, tie_first, entry_row, w_in, w_mid, w_out):
    rows = features.shape[0]
    total_rows = rows * lax.axis_size("chain") * lax.axis_size("strata")
    block_start = lax.axis_index("chain") * rows
    first = tie_first - block_start
    entry = entry_row - block_start
    args = (features, events, first, entry, w_in, w_mid, w_out)

    def run(cap):
        (grad_x, grad_in, grad_mid, grad_out), note = pipeline(cap, total_rows, *args)
        grad_in, grad_mid, grad_out, note = lax.psum(
            (grad_in, grad_mid, grad_out, note), ("strata", "chain")
        )
        return note[1, 0], (note[0] / total_rows, grad_x, grad_in, grad_mid, grad_out)

    over, out = run(min(GROUP, rows))
    return lax.cond(over > 0, lambda _: run(rows)[1], lambda kept: kept, out)


def solution(mesh):
    placed = (
        P(("strata", "chain"), None),
        P(("strata", "chain"), None),
        P(("strata", "chain")),
        P(("strata", "chain")),
        P(),
        P(),
        P(),
    )
    return jax.shard_map(
        on_device,
        mesh=mesh,
        in_specs=placed,
        out_specs=(P(), P(("strata", "chain"), None), P(), P(), P()),
        check_vma=False,
    )
```

time: 543 us -> 248 us (0.46); the launches traced: 536 us -> 247 us
  waiting for transfers between devices: 251 us -> 98.1 us
  other arithmetic: 82.2 us -> 1.31 us
  Pallas kernels: 0 us -> 68.7 us
  blocking collectives: 94.2 us -> 42.4 us
  local copies, waits for them, and re-layouts: 62.8 us -> 16.1 us
  matrix products: 27.5 us -> 0 us
    ppermute x2, waiting for transfers between devices: 157 us -> 0.88 us  [from_behind(): return lax.ppermute(block, axis, route)]
    pallas_call x0 -> x5, Pallas kernels: none -> 68.7 us  [the longest x1 17.5 us: backward(): pl.pallas_call(partial(backward_kernel, cap, factor), grid=(rows // TILE,...]
    all_gather x2 -> x0, blocking collectives: 52.8 us -> none  [the longest x1 26.8 us: on_device(): lax.all_gather(local_suffix[0][None, :], 'chain', axis=0, tiled=True)]
    scatter-add x2 -> x0, other arithmetic: 35.1 us -> none  [the longest x1 17.6 us: on_device(): grouped = jax.ops.segment_sum(hazard, local_first, num_segments=block_rows)]
    dot_general x9 -> x0, matrix products: 27.5 us -> none  [the longest x1 4.81 us: on_device(): preact = jnp.dot(features, w_in, preferred_element_type=jnp.float32)]
    gather x2 -> x0, local copies, waits for them, and re-layouts: 24.6 us -> none  [the longest x1 12.9 us: on_device(): exposure = before + inclusive - jnp.take(stacked, target, axis=0)]
    another operation x6 -> x0, other arithmetic: 20.4 us -> none
    slice x2, local copies, waits for them, and re-layouts: 9.42 us -> 0.6 us  [the longest x1 0.51 us: run(): note[1, 0]]
  transfers between devices with their start and end apart: 3 -> 3, of which waited for: 3 -> 2; matrix products, arithmetic and copies ran while one was open for 4% -> 0% of each run, Pallas kernels for 0% -> 10%
where the time goes in v1:
time: 248 us; the launch traced here: 247 us
  waiting for transfers between devices  98.1 us (40%)
  Pallas kernels  68.7 us (28%)
  blocking collectives  42.4 us (17%)
  local copies, waits for them, and re-layouts  16.1 us (6%)
  between operations  14.8 us (6%)
  starting transfers between devices  5.9 us (2%)
    psum x1, waiting for transfers between devices, run(): lax.psum((grad_in, grad_mid, grad_out, note), ('strata', 'chain'))  97.2 us
    psum x1, blocking collectives, run(): lax.psum((grad_in, grad_mid, grad_out, note), ('strata', 'chain'))  42.4 us
    pallas_call x1, Pallas kernels, backward(): pl.pallas_call(partial(backward_kernel, cap, factor), grid=(rows // TILE,...  17.5 us
    pallas_call x1, Pallas kernels, trunk(): pl.pallas_call(partial(trunk_kernel, cap), grid=(rows // TILE,), in_specs...  17.2 us
    unnamed x34, local copies, waits for them, and re-layouts  15.5 us
    pallas_call x1, Pallas kernels, own_exposure(): pl.pallas_call(own_exposure_kernel, grid_spec=pltpu.PrefetchScalarGridSpe...  12.1 us
    pallas_call x1, Pallas kernels, own_risk(): pl.pallas_call(own_risk_kernel, grid_spec=pltpu.PrefetchScalarGridSpec(nu...  11.9 us
    pallas_call x1, Pallas kernels, hazards(): pl.pallas_call(partial(hazard_kernel, cap), grid=(rows // TILE,), in_spec...  9.93 us
  transfers between devices with their start and end apart: 3, of which 2 were waited for; matrix products, arithmetic and copies ran while one was open for 0% of the time, Pallas kernels for 10%

profile of v1, /device:TPU:0, one launch (start us, length us, event | category | flops | bytes accessed | tf_op | source)
XLA Modules:
  0.0 247.3 jit_solution(18161230528946619793)
XLA Ops:
  7.2 0.0 all-reduce.7.cloned.1.call-start
  7.2 1.3 copy.18.events_ref
  8.6 0.7 broadcast_subtract_fusion
  9.3 17.2 %trunk.3 = (bf16[2048,512]{1,0:T(8,128)(2,1)}, bf16[2048,512]{1,0:T(8,128)(2,1)}, f32[2048,512]{1,0:T(8,128)}, f32[2048,512]{1,0:T(8,128)}, f32[2048,512]{1,0:T(...) custom-call(s32[1,2048]{1,0:T(1,128)S(1)} %bitcast.10, ...), custom_call_target="tpu_custom_call" | custom-call | tf_op jit(solution)/shard_map/trunk/pallas_call | solution.py:170
  26.5 0.0 copy-start.11
  26.5 1.0 copy-done.11
  27.5 1.3 collective-permute-start.2
  28.8 0.1 slice.16.starts
  28.9 1.6 copy-done
  30.5 1.6 copy-done.1
  32.1 11.9 %own_risk.3.risk = f32[2048,512]{1,0:T(8,128)} custom-call(s32[8]{0:T(128)S(1)} %slice.16.starts, s32[4,512]{1,0:T(4,128)S(1)} %reshape.44.entry_ref, s32[2048,128]{1,0:T(8,128)S(1)} %get-tuple-element.103.first_col, bf16[2048,512]{1,0:T(8,128)(2,1)S(1)} %copy-done, bf16[2048,512]{1,0:T(8,128)(2,1)S(1)} %copy-done.1), custom_call_target="tpu_custom_call" | custom-call | flops 4294967296 | bytes 8388608 | tf_op jit(solution)/shard_map/own_risk/pallas_call | solution.py:220
  43.9 0.9 collective-permute-done.2.got
  44.8 9.9 %hazards.3 = (bf16[2048,512]{1,0:T(8,128)(2,1)S(1)}, bf16[2048,512]{1,0:T(8,128)(2,1)}, f32[256,512]{1,0:T(8,128)}, f32[8,512]{1,0:T(8,128)S(1)}) custom-call(s32[1,2048]{1,0:T(1,128)S(1)} %bitcast.7, s32[2048,128]{1,0:T(8,128)S(1)} %get-tuple-element.103.first_col, f32[2048,512]{1,0:T(8,128)} %own_risk.3.risk, ...), custom_call_target="tpu_custom_call" | custom-call | tf_op jit(solution)/shard_map/hazards/pallas_call | solution.py:338
  54.7 1.3 copy-done.4
  56.0 4.6 %collective-permute-start.3 = (f32[256,512]{1,0:T(8,128)}, f32[256,512]{1,0:T(8,128)S(1)}, u32[]{:S(2)}, u32[]{:S(2)}) collective-permute-start(f32[256,512]{1,0:T(8,128)} %get-tuple-element.113), channel_id=1, source_target_pairs={{0,1},{1,2},{2,3},{3,4},{4,5},{5,6},{6,7},{8,9},{9,10},{10,11},{11... | collective-permute-start | bytes 1572872 | tf_op jit(solution)/shard_map/ppermute | solution.py:418
  60.7 1.6 copy-done.5
  62.3 1.6 copy-done.6
  63.8 1.2 copy-done.12
  65.1 12.1 %own_exposure.3.exposure_ref = f32[2048,512]{1,0:T(8,128)} custom-call(s32[8]{0:T(128)S(1)} %slice.16.starts, s32[4,512]{1,0:T(4,128)S(1)} %reshape.45.first_ref, s32[2048,128]{1,0:T(8,128)S(1)} %copy-done.12, bf16[2048,512]{1,0:T(8,128)(2,1)S(1)} %copy-done.5, bf16[2048,512]{1,0:T(8,128)(2,1)S(1)} %copy-done.6), custom_call_target="tpu_custom_call" | custom-call | flops 4294967296 | bytes 8388608 | tf_op jit(solution)/shard_map/own_exposure/pallas_call | solution.py:268
  77.2 0.0 collective-permute-done.3.got
  77.2 0.0 copy-done.15
  77.2 17.5 %backward.3 = (bf16[2048,512]{1,0:T(8,128)(2,1)}, f32[512,512]{1,0:T(8,128)}, f32[512,512]{1,0:T(8,128)}, f32[512,512]{1,0:T(8,128)}) custom-call(s32[2048,128]{1,0:T(8,128)S(1)} %get-tuple-element.109.rank_col, f32[2048,512]{1,0:T(8,128)} %own_exposure.3.exposure_ref, f32[256,512]{1,0:T(8,128)S(1)} %collective-permute-done.3.got, ...), custom_call_target="tpu_custom_call" | custom-call | tf_op jit(solution)/shard_map/backward/pallas_call | solution.py:401
  94.7 0.0 copy-start.26
  94.8 0.0 all-reduce.7.cloned.1.call-update
  94.8 42.4 %psum.56 = f32[8,512]{1,0:T(8,128)S(1)} all-reduce(f32[8,512]{1,0:T(8,128)S(1)} %add.22), channel_id=1, replica_groups=mesh['strata'=4,'chain'=8] {'strata','chain'}, use_global_device_ids=true, to_apply=%region_0.0 | all-reduce | flops 4096 | bytes 32768 | tf_op jit(solution)/shard_map/psum | solution.py:453
  137.2 0.5 slice.19
  138.3 97.2 %all-reduce.7.cloned.1.call-done = (f32[512,512]{1,0:T(8,128)}, f32[512,512]{1,0:T(8,128)}, f32[512,512]{1,0:T(8,128)}) async-done(((f32[512,512]{1,0:T(8,128)}, f32[512,512]{1,0:T(8,128)}, f32[512,512]{1,0:T(8,128)}), (f32[512,512]{1,0:T(8,128)}, f32[512,512]{1,0:T(8,128)}, f32[512,512]{1,0:T(8,128)})) %all-reduce.7.cloned.1.call-update) | async-done | bytes 3145744 | tf_op jit(solution)/shard_map/psum | solution.py:453
  235.6 0.6 slice_multiply_fusion
  236.2 2.4 copy.36
  238.5 0.0 copy-done.24
  238.5 1.0 copy.37
  239.5 1.0 copy.38
  (23 shorter events, 0.1 us)
Async XLA Ops:
  7.2 228.4 %all-reduce.7.cloned.1.call-start = ((), (), s32[]{:S(2)}) async-start(), calls=%async_computation.1 | async-start | bytes 6291456 | tf_op jit(solution)/shard_map/psum | solution.py:453
  26.5 1.0 copy-start.11
  27.5 17.3 %collective-permute-start.2 = (f32[264,512]{1,0:T(8,128)}, f32[264,512]{1,0:T(8,128)S(1)}, u32[]{:S(2)}, u32[]{:S(2)}) collective-permute-start(f32[264,512]{1,0:T(8,128)} %get-tuple-element.107), channel_id=1, source_target_pairs={{1,0},{2,1},{3,2},{4,3},{5,4},{6,5},{7,6},{9,8},{10,9},{11,10},{12... | collective-permute-start | bytes 1622024 | tf_op jit(solution)/shard_map/ppermute | solution.py:418
  28.9 1.6 copy-start
  30.5 1.6 copy-start.1
  54.7 1.3 copy-start.4
  56.0 21.1 %collective-permute-start.3 = (f32[256,512]{1,0:T(8,128)}, f32[256,512]{1,0:T(8,128)S(1)}, u32[]{:S(2)}, u32[]{:S(2)}) collective-permute-start(f32[256,512]{1,0:T(8,128)} %get-tuple-element.113), channel_id=1, source_target_pairs={{0,1},{1,2},{2,3},{3,4},{4,5},{5,6},{6,7},{8,9},{9,10},{10,11},{11... | collective-permute-start | bytes 1572872 | tf_op jit(solution)/shard_map/ppermute | solution.py:418
  60.7 1.6 copy-start.5
  62.2 1.6 copy-start.6
  63.8 1.2 copy-start.12
  65.1 12.1 %copy-start.15 = (bf16[2048,512]{1,0:T(8,128)(2,1)S(1)}, bf16[2048,512]{1,0:T(8,128)(2,1)}, u32[]{:S(2)}) copy-start(bf16[2048,512]{1,0:T(8,128)(2,1)} %x_ref.3) | copy-start | bytes 6291460
  65.1 12.1 %copy-start.17 = (bf16[512,512]{1,0:T(8,128)(2,1)S(1)}, bf16[512,512]{1,0:T(8,128)(2,1)}, u32[]{:S(2)}) copy-start(bf16[512,512]{1,0:T(8,128)(2,1)} %w_in.3) | copy-start | bytes 1572868
  65.1 12.1 %copy-start.19 = (bf16[512,512]{1,0:T(8,128)(2,1)S(1)}, bf16[512,512]{1,0:T(8,128)(2,1)}, u32[]{:S(2)}) copy-start(bf16[512,512]{1,0:T(8,128)(2,1)} %w_mid.3) | copy-start | bytes 1572868
  65.1 12.1 %copy-start.21 = (bf16[512,512]{1,0:T(8,128)(2,1)S(1)}, bf16[512,512]{1,0:T(8,128)(2,1)}, u32[]{:S(2)}) copy-start(bf16[512,512]{1,0:T(8,128)(2,1)} %w_out.3) | copy-start | bytes 1572868
  94.7 140.9 %copy-start.23 = (s32[2048,35]{0,1:T(8,128)S(1)}, s32[2048,35]{0,1:T(8,128)}, u32[]{:S(2)}) copy-start(s32[2048,35]{0,1:T(8,128)} %param.16) | copy-start | bytes 860164
  94.7 140.9 %copy-start.26 = (s32[1,512]{1,0:T(1,128)S(1)}, s32[1,512]{1,0:T(1,128)}, u32[]{:S(2)}) copy-start(s32[1,512]{1,0:T(1,128)} %constant.24.clone.shift_ref) | copy-start | bytes 6148
  235.6 2.9 %copy-start.24 = (f32[512,512]{1,0:T(8,128)S(1)}, f32[512,512]{1,0:T(8,128)}, u32[]{:S(2)}) copy-start(f32[512,512]{1,0:T(8,128)} %get-tuple-element.159) | copy-start | bytes 3145732
  236.2 3.3 %copy-start.25 = (f32[512,512]{1,0:T(8,128)S(1)}, f32[512,512]{1,0:T(8,128)}, u32[]{:S(2)}) copy-start(f32[512,512]{1,0:T(8,128)} %get-tuple-element.160) | copy-start | bytes 3145732
Sparse Core Ops, SparseCore 0:
  94.9 140.6 all-reduce.6

commit v2 on v1

v2 whole, which is shorter than its diff:
```python
from functools import partial

import jax
import jax.numpy as jnp
import numpy as np
from jax import lax
from jax.experimental import pallas as pl
from jax.experimental.pallas import tpu as pltpu
from jax.sharding import PartitionSpec as P

BITS = 15
LANES = 128
TILE = 512
DEPTH = 512
GROUP = 256
MIB = 1024 * 1024
F32 = jnp.float32
BF16 = jnp.bfloat16
I32 = jnp.int32


def two_parts(value):
    top = value.astype(BF16)
    return top, (value - top.astype(F32)).astype(BF16)


def iota(shape, dim):
    return lax.broadcasted_iota(I32, shape, dim)


def ones_where(mask):
    return jnp.where(mask, 1.0, 0.0).astype(BF16)


def dot(a, b, ca=1, cb=0):
    return lax.dot_general(a, b, (((ca,), (cb,)), ((), ())), preferred_element_type=F32)


def widen(column, width):
    return jnp.concatenate([column] * (width // column.shape[1]), axis=1)


def as_column(row):
    parts = [
        jnp.broadcast_to(row[:, k : k + LANES], (LANES, LANES)).T
        for k in range(0, row.shape[1], LANES)
    ]
    return jnp.concatenate(parts, axis=0)


def whole():
    return pl.BlockSpec(memory_space=pltpu.VMEM)


def rows_of(tile, width):
    return pl.BlockSpec((tile, width), lambda i: (i, 0))


def lanes_of(height, tile):
    return pl.BlockSpec((height, tile), lambda i: (0, i))


def in_hbm(array):
    return pltpu.with_memory_space_constraint(array, pltpu.HBM)


def params(mib):
    return pltpu.CompilerParams(vmem_limit_bytes=mib * MIB)


def rank_entries(entry_ref, rank_ref, note, cap):
    rows = entry_ref.shape[1]
    high = rows // LANES
    place = entry_ref[...] + rows
    crosses = place < rows
    high_hit = ones_where((iota((high, rows), 0) == (place >> 7)) & crosses)
    low_hit = jnp.where((iota((LANES, rows), 0) == (place & (LANES - 1))) & crosses, 1.0, 0.0)
    present = ones_where(dot(high_hit, low_hit.astype(BF16), 1, 1) > 0.5)
    square = (LANES, LANES)
    within = dot(present, ones_where(iota(square, 0) < iota(square, 1)))
    small = (high, high)
    ahead = dot(ones_where(iota(small, 1) < iota(small, 0)), present)
    table = within + jnp.sum(ahead, axis=1, keepdims=True)
    table_high = jnp.floor(table * (1.0 / 256.0))
    table_low = table - 256.0 * table_high
    found = 256.0 * dot(table_high.astype(BF16), high_hit, 0, 0)
    found = found + dot(table_low.astype(BF16), high_hit, 0, 0)
    rank = jnp.sum(found * low_hit, axis=0, keepdims=True)
    rank_ref[...] = jnp.where(crosses, rank.astype(I32), -1)
    count = jnp.sum(present.astype(F32))
    note[...] = jnp.where(iota(note.shape, 0) == 1, jnp.where(count > cap, 1.0, 0.0), 0.0)


def trunk_kernel(
    cap, entry_ref, x_ref, events_ref, low_ref, high_ref, shift_ref, w_in, w_mid, w_out,
    first_hidden, hidden, slope_in, slope_mid, indicator_out, weight_out, weight_top, weight_rest,
    send, note, rank_ref,
):
    step = pl.program_id(0)
    tile = x_ref.shape[0]

    @pl.when(step == 0)
    def _():
        rank_entries(entry_ref, rank_ref, note, cap)

    at = pl.ds(pl.multiple_of(step * tile, tile), tile)
    events = events_ref[...]
    spread = dot((events & 255).astype(F32).astype(BF16), low_ref[...], 0, 0)
    spread = spread + dot((events >> 8).astype(F32).astype(BF16), high_ref[...], 0, 0)
    bits = jnp.bitwise_and(jnp.right_shift(spread.astype(I32), shift_ref[...]), 1)
    indicator = bits.astype(F32)
    indicator_out[...] = indicator.astype(BF16)

    preact = dot(x_ref[...], w_in[...])
    sigma = jax.nn.sigmoid(preact)
    first = (preact * sigma).astype(BF16)
    first_hidden[...] = first
    slope_in[...] = sigma * (1.0 + preact * (1.0 - sigma))
    mid_pre = dot(first, w_mid[...])
    sigma = jax.nn.sigmoid(mid_pre)
    second = (mid_pre * sigma).astype(BF16)
    hidden[...] = second
    slope_mid[...] = sigma * (1.0 + mid_pre * (1.0 - sigma))
    log_hazard = dot(second, w_out[...])
    weight = jnp.exp(log_hazard)
    weight_out[...] = weight
    weight_top[at, :], weight_rest[at, :] = two_parts(weight)
    note[0:1, :] -= jnp.sum(indicator * log_hazard, axis=0, keepdims=True)

    @pl.when(step == pl.num_programs(0) - 1)
    def _():
        rows = rank_ref.shape[1]
        send[cap:, :] = jnp.zeros((send.shape[0] - cap, send.shape[1]), F32)

        def total(t, _):
            hit = iota((GROUP, rows), 0) + t * GROUP == rank_ref[...]
            place = jnp.where(hit, (entry_ref[...] + rows).astype(F32), 0.0)
            place = jnp.max(place, axis=1, keepdims=True)
            place = jnp.broadcast_to(place, (GROUP, LANES))
            parts = [place[k : k + LANES, :].T[0:1] for k in range(0, GROUP, LANES)]
            spot = (send.shape[0] - cap, GROUP)
            place = jnp.broadcast_to(jnp.concatenate(parts, axis=1), spot)
            send[cap:, 0:GROUP] = jnp.where(iota(spot, 0) == t, place, send[cap:, 0:GROUP])
            hit = ones_where(hit)
            at = pl.ds(pl.multiple_of(t * GROUP, GROUP), GROUP)
            send[at, :] = dot(hit, weight_top[...]) + dot(hit, weight_rest[...])
            return 0

        lax.fori_loop(0, cap // GROUP, total, 0)


def trunk(cap, entry, features, events, w_in, w_mid, w_out):
    rows, width = features.shape
    mid = w_in.shape[1]
    wide = w_mid.shape[1]
    out_width = w_out.shape[1]
    words = events.shape[1]
    column = np.arange(out_width)
    owner = (np.arange(words)[:, None] == column // BITS).astype(np.float32)
    bit = column % BITS
    low = jnp.asarray(owner * (bit < 8), BF16)
    high = jnp.asarray(owner * (bit >= 8), BF16)
    shift = jnp.asarray((bit % 8)[None, :], I32)
    sent_rows = cap + -(-(cap // GROUP) // 8) * 8
    like = jax.ShapeDtypeStruct
    return pl.pallas_call(
        partial(trunk_kernel, cap),
        grid=(rows // TILE,),
        in_specs=[whole(), rows_of(TILE, width), lanes_of(words, TILE)] + [whole()] * 6,
        out_specs=[
            rows_of(TILE, mid), rows_of(TILE, wide), rows_of(TILE, mid), rows_of(TILE, wide),
            rows_of(TILE, out_width), rows_of(TILE, out_width),
        ]
        + [whole()] * 5,
        out_shape=[
            pltpu.HBM((rows, mid), BF16), pltpu.HBM((rows, wide), BF16),
            pltpu.HBM((rows, mid), F32), pltpu.HBM((rows, wide), F32),
            pltpu.HBM((rows, out_width), BF16), pltpu.HBM((rows, out_width), F32),
            like((rows, out_width), BF16), like((rows, out_width), BF16), like((sent_rows, out_width), F32),
            like((8, out_width), F32), like((1, rows), I32),
        ],
        compiler_params=params(28),
        name="trunk",
    )(entry, features, events.T, low, high, shift, w_in, w_mid, w_out)


def own_risk_kernel(starts, entry_ref, first_ref, weight_top, weight_rest, out):
    step = pl.program_id(0)
    tile = first_ref.shape[1]
    rows = weight_top.shape[0]
    first = widen(as_column(first_ref[...]), DEPTH)
    own = pl.ds(pl.multiple_of(step * tile, tile), tile)
    out[own, :] = jnp.zeros((tile, out.shape[1]), F32)

    def part(k, _):
        at = pl.multiple_of(k * DEPTH, DEPTH)
        row = iota((tile, DEPTH), 1) + at
        entry = entry_ref[pl.ds(k, 1), :]
        mask = ones_where((row >= first) & (entry <= first))
        at = pl.ds(at, DEPTH)
        out[own, :] += dot(mask, weight_top[at, :]) + dot(mask, weight_rest[at, :])
        return 0

    lax.fori_loop(starts[step] // DEPTH, rows // DEPTH, part, 0)


def block_sum(flops):
    return pl.CostEstimate(flops=flops, bytes_accessed=flops // 256, transcendentals=0)


def own_risk(starts, entry, first, weight_top, weight_rest):
    rows, width = weight_top.shape
    return pl.pallas_call(
        own_risk_kernel,
        grid=(rows // TILE,),
        in_specs=[
            pl.BlockSpec(memory_space=pltpu.SMEM), whole(), lanes_of(1, TILE), whole(), whole()
        ],
        out_specs=whole(),
        out_shape=jax.ShapeDtypeStruct((rows, width), F32),
        compiler_params=params(12),
        cost_estimate=block_sum(rows * rows * width * 4),
        name="own_risk",
    )(starts, entry.reshape(rows // DEPTH, DEPTH), first, weight_top, weight_rest)


def own_exposure_kernel(starts, first_ref, entry_ref, hazard_top, hazard_rest, out, note):
    step = pl.program_id(0)
    tile = entry_ref.shape[1]

    @pl.when(step == 0)
    def _():
        note[...] = jnp.zeros_like(note)

    entry = widen(as_column(entry_ref[...]), DEPTH)
    row = iota((tile, DEPTH), 0) + step * tile
    own = pl.ds(pl.multiple_of(step * tile, tile), tile)
    out[own, :] = jnp.zeros((tile, out.shape[1]), F32)
    last = step * tile + tile - 1
    parts = jnp.int32(0)
    for k in range(first_ref.shape[0]):
        parts += jnp.where(starts[k * (DEPTH // TILE)] <= last, 1, 0).astype(I32)

    def part(k, _):
        at = pl.multiple_of(k * DEPTH, DEPTH)
        first = first_ref[pl.ds(k, 1), :]
        mask = ones_where((first >= entry) & (first <= row))
        at = pl.ds(at, DEPTH)
        out[own, :] += dot(mask, hazard_top[at, :]) + dot(mask, hazard_rest[at, :])
        return 0

    lax.fori_loop(0, parts, part, 0)
    hazard = hazard_top[own, :].astype(F32) + hazard_rest[own, :].astype(F32)
    logs = jnp.where(hazard > 0.0, jnp.log(hazard), 0.0)
    note[0:1, :] -= jnp.sum(logs, axis=0, keepdims=True)


def own_exposure(starts, first, entry, hazard_top, hazard_rest):
    rows, width = hazard_top.shape
    like = jax.ShapeDtypeStruct
    return pl.pallas_call(
        own_exposure_kernel,
        grid=(rows // TILE,),
        in_specs=[
            pl.BlockSpec(memory_space=pltpu.SMEM), whole(), lanes_of(1, TILE), whole(), whole()
        ],
        out_specs=[whole(), whole()],
        out_shape=[like((rows, width), F32), like((8, width), F32)],
        compiler_params=params(12),
        cost_estimate=block_sum(rows * rows * width * 4),
        name="own_exposure",
    )(starts, first.reshape(rows // DEPTH, DEPTH), entry, hazard_top, hazard_rest)


def split_sum(source, high, low, cap):
    for t in range(0, cap, GROUP):
        high[t : t + GROUP, :], low[t : t + GROUP, :] = two_parts(source[t : t + GROUP, :])


def hazard_kernel(
    cap, first_all, first_ref, risk, indicator_ref, got, hazard_top, hazard_rest, sums, high, low
):
    step = pl.program_id(0)
    tile = first_ref.shape[1]
    rows = hazard_top.shape[0]
    own = pl.ds(pl.multiple_of(step * tile, tile), tile)

    @pl.when(step == 0)
    def _():
        split_sum(got, high, low, cap)

    first = widen(as_column(first_ref[...]).astype(F32), GROUP)
    divisor = risk[own, :]

    def beyond(t, total):
        entry = got[pl.ds(cap + t, 1), 0:GROUP]
        mask = ones_where(entry <= first)
        at = pl.ds(pl.multiple_of(t * GROUP, GROUP), GROUP)
        return total + dot(mask, high[at, :]) + dot(mask, low[at, :])

    divisor = lax.fori_loop(0, cap // GROUP, beyond, divisor)
    hazard = indicator_ref[...].astype(F32) / divisor
    hazard_top[own, :], hazard_rest[own, :] = two_parts(hazard)

    @pl.when(step == pl.num_programs(0) - 1)
    def _():
        def total(t, _):
            entry = widen(as_column(got[pl.ds(cap + t, 1), 0:GROUP]), rows)
            mask = ones_where(first_all[...].astype(F32) >= entry)
            at = pl.ds(pl.multiple_of(t * GROUP, GROUP), GROUP)
            sums[at, :] = dot(mask, hazard_top[...]) + dot(mask, hazard_rest[...])
            return 0

        lax.fori_loop(0, cap // GROUP, total, 0)


def hazards(cap, first, risk, indicator, got):
    rows, width = risk.shape
    like = jax.ShapeDtypeStruct
    return pl.pallas_call(
        partial(hazard_kernel, cap),
        grid=(rows // TILE,),
        in_specs=[
            whole(), lanes_of(1, TILE), whole(), rows_of(TILE, width), whole()
        ],
        out_specs=[whole(), whole(), whole()],
        out_shape=[
            like((rows, width), BF16), like((rows, width), BF16), like((cap, width), F32)
        ],
        scratch_shapes=[pltpu.VMEM((cap, width), BF16), pltpu.VMEM((cap, width), BF16)],
        compiler_params=params(20),
        name="hazards",
    )(first, first, risk, in_hbm(indicator), got)


def backward_kernel(
    cap, factor, half, rank_ref, exposure_ref, got, note, log_part, weight, indicator, hidden, slope_mid, first_hidden, slope_in, x_ref, w_in, w_mid, w_out, grad_x, keep, send,
    high, low, grad_in, grad_mid, grad_out,
):
    step = pl.program_id(0)
    tile = rank_ref.shape[1]
    own = pl.ds(pl.multiple_of(step * tile, tile), tile)

    @pl.when(step == 0)
    def _():
        split_sum(got, high, low, cap)
        grad_in[...] = jnp.zeros_like(grad_in)
        grad_mid[...] = jnp.zeros_like(grad_mid)
        grad_out[...] = jnp.zeros_like(grad_out)

    rank = widen(as_column(rank_ref[...]), GROUP)

    def behind(t, total):
        mask = ones_where(rank == iota((tile, GROUP), 1) + t * GROUP)
        at = pl.ds(pl.multiple_of(t * GROUP, GROUP), GROUP)
        return total + dot(mask, high[at, :]) + dot(mask, low[at, :])

    exposure = lax.fori_loop(0, cap // GROUP, behind, exposure_ref[own, :])
    eta = (weight[...] * exposure - indicator[...].astype(F32)).astype(BF16)
    grad_out[...] += dot(hidden[...], eta, 0, 0)
    mid = (dot(eta, w_out[...], 1, 1) * slope_mid[...]).astype(BF16)
    grad_mid[...] += dot(first_hidden[...], mid, 0, 0)
    pre = (dot(mid, w_mid[...], 1, 1) * slope_in[...]).astype(BF16)
    grad_in[...] += dot(x_ref[...], pre, 0, 0)
    grad_x[...] = dot(pre, w_in[...], 1, 1).astype(BF16)

    @pl.when(step == pl.num_programs(0) - 1)
    def _():
        body, rest = grad_mid.shape[0], grad_out.shape[0] // 2
        end = body + rest

        def write(out, block, at):
            out[0:body, :] = block[...] * factor
            out[body:end, :] = grad_out[at : at + rest, :] * factor
            out[end:, :] = note[...] + log_part[...]

        @pl.when(half[0] == 0)
        def _():
            write(keep, grad_mid, 0)
            write(send, grad_in, rest)

        @pl.when(half[0] != 0)
        def _():
            write(keep, grad_in, rest)
            write(send, grad_mid, 0)


def backward(cap, factor, half, rank, exposure, got, notes, kept, features, w_in, w_mid, w_out):
    rows, width = features.shape
    out_width = exposure.shape[1]
    like = jax.ShapeDtypeStruct
    tiles = [in_hbm(a) for a in (*kept, features)]
    weights = (w_in, w_mid, w_out)
    halves = (w_mid.shape[0] + w_out.shape[0] // 2 + 8, out_width)
    return pl.pallas_call(
        partial(backward_kernel, cap, factor),
        grid=(rows // TILE,),
        in_specs=[pl.BlockSpec(memory_space=pltpu.SMEM)]
        + [lanes_of(1, TILE)]
        + [whole()] * (2 + len(notes))
        + [rows_of(TILE, a.shape[1]) for a in tiles]
        + [whole()] * len(weights),
        out_specs=[rows_of(TILE, width), whole(), whole()],
        out_shape=[
            pltpu.HBM((rows, width), BF16), pltpu.HBM(halves, F32), like(halves, F32)
        ],
        scratch_shapes=[pltpu.VMEM((cap, out_width), BF16), pltpu.VMEM((cap, out_width), BF16)]
        + [pltpu.VMEM(w.shape, F32) for w in weights],
        compiler_params=params(28),
        name="backward",
    )(half, rank, exposure, got, *notes, *tiles, *weights)


def spread_kernel(sizes, streams, me, *refs):
    count = sum(sizes)
    outs = iter(refs[count : len(refs) - len(sizes)])
    totals = refs[len(refs) - len(sizes) :]
    start = 0
    for size, total in zip(sizes, totals):
        value = refs[start][...]
        for ref in refs[start + 1 : start + size]:
            value = value + ref[...]
        total[...] = value
        start += size
    for i, (which, at, rows, tail_at, tail, groups) in enumerate(streams):
        total, piece = totals[which], rows // groups
        for m in range(groups):
            out = next(outs)
            begin = pl.multiple_of(at + jnp.bitwise_xor(me[i], m) * piece, 8)
            out[0:piece, :] = total[pl.ds(begin, piece), :]
            if tail:
                out[piece : piece + tail, :] = total[tail_at : tail_at + tail, :]


def spread(terms, streams, me, name):
    width = terms[0][0].shape[1]
    shapes = []
    for _, _, rows, _, tail, groups in streams:
        shapes += [jax.ShapeDtypeStruct((rows // groups + tail, width), F32)] * groups
    flat = [a for term in terms for a in term]
    out = pl.pallas_call(
        partial(spread_kernel, [len(term) for term in terms], streams),
        in_specs=[pl.BlockSpec(memory_space=pltpu.SMEM)]
        + [pl.BlockSpec(memory_space=pltpu.VMEM)] * len(flat),
        out_specs=[pl.BlockSpec(memory_space=pltpu.VMEM)] * len(shapes),
        out_shape=shapes,
        scratch_shapes=[pltpu.VMEM(term[0].shape, F32) for term in terms],
        compiler_params=params(16),
        name=name,
    )(me, *flat)
    parts = []
    for stream in streams:
        parts.append(out[: stream[-1]])
        out = out[stream[-1] :]
    return parts


def collect_kernel(places, me, *refs):
    count = sum(groups for groups, _, _ in places)
    outs = refs[count:]
    start = 0
    for i, (groups, which, at) in enumerate(places):
        piece = refs[start].shape[0]
        for m in range(groups):
            begin = pl.multiple_of(at + jnp.bitwise_xor(me[i], m) * piece, 8)
            outs[which][pl.ds(begin, piece), :] = refs[start + m][...]
        start += groups


def collect(streams, out_rows, me, name):
    flat = [a for pieces, _, _ in streams for a in pieces]
    width = flat[0].shape[1]
    return pl.pallas_call(
        partial(collect_kernel, [(len(pieces), which, at) for pieces, which, at in streams]),
        in_specs=[pl.BlockSpec(memory_space=pltpu.SMEM)]
        + [pl.BlockSpec(memory_space=pltpu.VMEM)] * len(flat),
        out_specs=[pl.BlockSpec(memory_space=pltpu.VMEM)] * len(out_rows),
        out_shape=[jax.ShapeDtypeStruct((rows, width), F32) for rows in out_rows],
        compiler_params=params(16),
        name=name,
    )(me, *flat)


def plan(body, rest):
    strata, chain = lax.axis_size("strata"), lax.axis_size("chain")
    if strata % 2 or chain % 4 or strata & (strata - 1) or chain & (chain - 1):
        return None
    across = chain // 4
    plane, line = strata // 2 * across, 4
    if body % (8 * plane * line) or rest % (8 * plane * line):
        return None
    return across, plane, line


def hop(block, strata_flip, chain_flip):
    strata, chain = lax.axis_size("strata"), lax.axis_size("chain")
    route = [
        (s * chain + c, (s ^ strata_flip) * chain + (c ^ chain_flip))
        for s in range(strata)
        for c in range(chain)
    ]
    return lax.ppermute(block, ("strata", "chain"), route)


def total_by_hops(keep, send, body, rest, groups):
    across, plane, line = groups
    strata, chain = lax.axis_index("strata"), lax.axis_index("chain")
    in_plane = strata // 2 * across + chain % across
    in_line = chain // across
    zero = jnp.int32(0)

    def plane_hops(pieces):
        return [pieces[0]] + [
            hop(pieces[m], m // across * 2, m % across) for m in range(1, plane)
        ]

    def line_hops(pieces):
        return [pieces[0]] + [hop(pieces[m], 0, m * across) for m in range(1, line)]

    end = body + rest
    tail = keep.shape[0] - end
    first_me = jnp.stack([in_plane, in_line])
    second_me = jnp.stack([in_line, in_plane])
    a, b = spread(
        [[keep, hop(send, 1, 0)]],
        [(0, 0, body, end, tail, plane), (0, body, rest, 0, 0, line)],
        first_me, "spread_first",
    )
    a, b = plane_hops(a), line_hops(b)
    body_a, body_b = body // plane, rest // line
    a, b = spread(
        [a, b],
        [(0, 0, body_a, body_a, tail, line), (1, 0, body_b, 0, 0, plane)],
        second_me, "spread_second",
    )
    a, b = line_hops(a), plane_hops(b)
    size_a, size_b = body_a // line, body_b // plane
    (a,), (note,), (b,) = spread(
        [a, b],
        [(0, 0, size_a, 0, 0, 1), (0, size_a, tail, 0, 0, 1), (1, 0, size_b, 0, 0, 1)],
        jnp.stack([zero, zero, zero]), "sums",
    )
    a, b = line_hops([a] * line), plane_hops([b] * plane)
    a, b = collect([(a, 0, 0), (b, 1, 0)], [body_a, body_b], second_me, "collect_first")
    a, b = plane_hops([a] * plane), line_hops([b] * line)
    (own,) = collect([(a, 0, 0), (b, 0, body)], [end], first_me, "collect_second")
    return own, hop(own, 1, 0), note


def finish_kernel(half, own, got, grad_in, grad_mid, grad_out):
    body, rest = grad_mid.shape[0], grad_out.shape[0] // 2

    def write(top, bottom):
        grad_mid[...] = top[0:body, :]
        grad_in[...] = bottom[0:body, :]
        grad_out[0:rest, :] = top[body:, :]
        grad_out[rest:, :] = bottom[body:, :]

    @pl.when(half[0] == 0)
    def _():
        write(own, got)

    @pl.when(half[0] != 0)
    def _():
        write(got, own)


def finish(half, own, got, shapes):
    return pl.pallas_call(
        finish_kernel,
        in_specs=[pl.BlockSpec(memory_space=pltpu.SMEM)]
        + [pl.BlockSpec(memory_space=pltpu.VMEM)] * 2,
        out_specs=[pl.BlockSpec(memory_space=pltpu.VMEM)] * 3,
        out_shape=[pltpu.HBM(shape, F32) for shape in shapes],
        compiler_params=params(16),
        name="finish",
    )(half, own, got)


def from_behind(block, axis, distance):
    devices = range(lax.axis_size(axis))
    route = [(i - distance, i) for i in devices if i - distance in devices]
    return lax.ppermute(block, axis, route)


def pipeline(cap, total_rows, half, features, events, first, entry, w_in, w_mid, w_out):
    rows = features.shape[0]
    first_row = first.reshape(1, rows)
    entry_row = entry.reshape(1, rows)
    starts = first[::TILE]
    (
        first_hidden, hidden, slope_in, slope_mid, indicator, weight, weight_top, weight_rest,
        send, note, rank,
    ) = trunk(cap, entry_row, features, events, w_in, w_mid, w_out)
    got = from_behind(send, "chain", -1)
    risk = own_risk(starts, entry, first_row, weight_top, weight_rest)
    hazard_top, hazard_rest, sums = hazards(cap, first_row, risk, indicator, got)
    got_sums = from_behind(sums, "chain", 1)
    exposure, log_part = own_exposure(starts, first, entry_row, hazard_top, hazard_rest)
    kept = (weight, indicator, hidden, slope_mid, first_hidden, slope_in)
    return backward(
        cap, total_rows ** (-0.5), half, rank, exposure, got_sums, (note, log_part), kept,
        features, w_in, w_mid, w_out,
    )


def on_device(features, events, tie_first, entry_row, w_in, w_mid, w_out):
    rows = features.shape[0]
    total_rows = rows * lax.axis_size("chain") * lax.axis_size("strata")
    block_start = lax.axis_index("chain") * rows
    first = tie_first - block_start
    entry = entry_row - block_start
    args = (features, events, first, entry, w_in, w_mid, w_out)
    shapes = (w_in.shape, w_mid.shape, w_out.shape)
    body, rest = w_mid.shape[0], w_out.shape[0] // 2
    groups = plan(body, rest)
    half = jnp.zeros((1,), I32)
    if groups:
        half = half + lax.axis_index("strata") % 2

    def run(cap):
        grad_x, keep, send = pipeline(cap, total_rows, half, *args)
        if groups:
            own, other, note = total_by_hops(keep, send, body, rest, groups)
        else:
            own, other = lax.psum((keep, send[: body + rest]), ("strata", "chain"))
            own, note = own[: body + rest], own[body + rest :]
        return note, (note[0] / total_rows, grad_x, own, other)

    def complete(kept):
        loss, grad_x, own, other = kept
        return (loss, grad_x, *finish(half, own, other, shapes))

    note, kept = run(min(GROUP, rows))
    return lax.cond(note[1, 0] > 0, lambda _: complete(run(rows)[1]), complete, kept)


def solution(mesh):
    placed = (
        P(("strata", "chain"), None),
        P(("strata", "chain"), None),
        P(("strata", "chain")),
        P(("strata", "chain")),
        P(),
        P(),
        P(),
    )
    return jax.shard_map(
        on_device,
        mesh=mesh,
        in_specs=placed,
        out_specs=(P(), P(("strata", "chain"), None), P(), P(), P()),
        check_vma=False,
    )
```

time: 248 us -> 145 us (0.58)
  waiting for transfers between devices: 98.1 us -> 30.6 us
  blocking collectives: 42.4 us -> 0 us
  starting transfers between devices: 5.9 us -> 42.5 us
  between operations: 14.8 us -> 1.67 us
  Pallas kernels: 68.7 us -> 59.8 us
  local copies, waits for them, and re-layouts: 16.1 us -> 8.9 us
    psum x1 -> x0, waiting for transfers between devices: 97.2 us -> none  [run(): lax.psum((grad_in, grad_mid, grad_out, note), ('strata', 'chain'))]
    psum x1 -> x0, blocking collectives: 42.4 us -> none  [run(): lax.psum((grad_in, grad_mid, grad_out, note), ('strata', 'chain'))]
    ppermute x0 -> x26, starting transfers between devices: none -> 36.4 us  [hop(): return lax.ppermute(block, ('strata', 'chain'), route)]
    ppermute x0 -> x26, waiting for transfers between devices: none -> 26.4 us  [hop(): return lax.ppermute(block, ('strata', 'chain'), route)]
    unnamed x34 -> x36, local copies, waits for them, and re-layouts: 15.5 us -> 5.44 us
    pallas_call x1, Pallas kernels: 9.93 us -> 5.39 us  [hazards(): pl.pallas_call(partial(hazard_kernel, cap), grid=(rows // TILE,), in_spec...]
    pallas_call x1, Pallas kernels: 17.2 us -> 13.8 us  [trunk(): pl.pallas_call(partial(trunk_kernel, cap), grid=(rows // TILE,), in_specs...]
    pallas_call x1, Pallas kernels: 17.5 us -> 14.2 us  [backward(): pl.pallas_call(partial(backward_kernel, cap, factor), grid=(rows // TILE,...]
  transfers between devices with their start and end apart: 3 -> 28, of which waited for: 2 -> 12; matrix products, arithmetic and copies ran while one was open for 0% -> 1% of each run, Pallas kernels for 10% -> 15%
where the time goes in v2:
time: 145 us
  Pallas kernels  59.8 us (41%)
  starting transfers between devices  42.5 us (29%)
  waiting for transfers between devices  30.6 us (21%)
  local copies, waits for them, and re-layouts  8.9 us (6%)
  between operations  1.67 us (1%)
  other arithmetic  1.47 us (1%)
    ppermute x26, starting transfers between devices, hop(): return lax.ppermute(block, ('strata', 'chain'), route)  36.4 us
    ppermute x26, waiting for transfers between devices, hop(): return lax.ppermute(block, ('strata', 'chain'), route)  26.4 us
    pallas_call x1, Pallas kernels, backward(): pl.pallas_call(partial(backward_kernel, cap, factor), grid=(rows // TILE,...  14.2 us
    pallas_call x1, Pallas kernels, trunk(): pl.pallas_call(partial(trunk_kernel, cap), grid=(rows // TILE,), in_specs...  13.8 us
    pallas_call x1, Pallas kernels, own_exposure(): pl.pallas_call(own_exposure_kernel, grid=(rows // TILE,), in_specs=[pl.Bl...  11.3 us
    pallas_call x1, Pallas kernels, own_risk(): pl.pallas_call(own_risk_kernel, grid=(rows // TILE,), in_specs=[pl.BlockS...  9.94 us
    ppermute x2, starting transfers between devices, from_behind(): return lax.ppermute(block, axis, route)  6.03 us
    unnamed x36, local copies, waits for them, and re-layouts  5.44 us
  transfers between devices with their start and end apart: 28, of which 12 were waited for; matrix products, arithmetic and copies ran while one was open for 1% of the time, Pallas kernels for 15%

profile of v2, /device:TPU:0, one launch (start us, length us, event | category | flops | bytes accessed | tf_op | source)
XLA Modules:
  0.0 144.9 jit_solution(9853215211790043023)
XLA Ops:
  1.3 13.8 %trunk.3 = (bf16[2048,512]{1,0:T(8,128)(2,1)}, bf16[2048,512]{1,0:T(8,128)(2,1)}, f32[2048,512]{1,0:T(8,128)}, f32[2048,512]{1,0:T(8,128)}, bf16[2048,512]{1,0:T...) custom-call(s32[1,2048]{1,0:T(1,128)S(1)} %bitcast.21, ...), custom_call_target="tpu_custom_call" | custom-call | tf_op jit(solution)/shard_map/trunk/pallas_call | solution.py:166
  17.8 1.6 %copy-done.3 = bf16[2048,512]{1,0:T(8,128)(2,1)S(1)} copy-done((bf16[2048,512]{1,0:T(8,128)(2,1)S(1)}, bf16[2048,512]{1,0:T(8,128)(2,1)}, u32[]{:S(2)}) %copy-start.3) | copy-done | bytes 2097176
  19.4 9.9 %own_risk.3.risk = f32[2048,512]{1,0:T(8,128)S(1)} custom-call(s32[4]{0:T(128)S(1)} %slice.16.starts, s32[4,512]{1,0:T(4,128)S(1)} %reshape.45.entry_ref, s32[1,2048]{1,0:T(1,128)S(1)} %bitcast.15, bf16[2048,512]{1,0:T(8,128)(2,1)S(1)} %get-tuple-element.145.weight_top, bf16[2048,512]{1,0:T(8,128)(2,1)S(1)} %copy-done.3), custom_call_target="tpu_custom_call" | custom-call | flops 8589934592 | bytes 33554432 | tf_op jit(solution)/shard_map/own_risk/pallas_call | solution.py:213
  29.4 4.1 %collective-permute-done.28.got = f32[264,512]{1,0:T(8,128)S(1)} collective-permute-done((f32[264,512]{1,0:T(8,128)S(1)}, f32[264,512]{1,0:T(8,128)S(1)}, u32[]{:S(2)}, u32[]{:S(2)}) %collective-permute-start.28) | collective-permute-done | bytes 540704 | tf_op jit(solution)/shard_map/ppermute | solution.py:583
  33.5 5.4 %hazards.3 = (bf16[2048,512]{1,0:T(8,128)(2,1)S(1)}, bf16[2048,512]{1,0:T(8,128)(2,1)S(1)}, f32[256,512]{1,0:T(8,128)S(1)}) custom-call(s32[1,2048]{1,0:T(1,128)S(1)} %bitcast.16, s32[1,2048]{1,0:T(1,128)S(1)} %bitcast.17, f32[2048,512]{1,0:T(8,128)S(1)} %own_risk.3.risk, bf16[2048,512]{1,0:T(8,128)(2,1)} %get-tuple-element.147.indicator_ref.indicator, ...), custom_call_target="tpu_custom_call" | custom-call | tf_op jit(solution)/shard_map/hazards/pallas_call | solution.py:320
  38.9 4.8 %collective-permute-start.29 = (f32[256,512]{1,0:T(8,128)S(1)}, f32[256,512]{1,0:T(8,128)S(1)}, u32[]{:S(2)}, u32[]{:S(2)}) collective-permute-start(f32[256,512]{1,0:T(8,128)S(1)} %get-tuple-element.152), channel_id=1, source_target_pairs={{0,1},{1,2},{2,3},{3,4},{4,5},{5,6},{6,7},{8,9},{9,10},{10,11},{11... | collective-permute-start | bytes 1572872 | tf_op jit(solution)/shard_map/ppermute | solution.py:583
  43.7 11.3 %own_exposure.3 = (f32[2048,512]{1,0:T(8,128)S(1)}, f32[8,512]{1,0:T(8,128)S(1)}) custom-call(s32[4]{0:T(128)S(1)} %slice.16.starts, s32[4,512]{1,0:T(4,128)S(1)} %reshape.43.first_ref, s32[1,2048]{1,0:T(1,128)S(1)} %bitcast.22, bf16[2048,512]{1,0:T(8,128)(2,1)S(1)} %get-tuple-element.149.hazard_top, bf16[2048,512]{1,0:T(8,128)(2,1)S(1)} %get-tuple-element.150.hazard_rest), custom_call_target="tpu_custom_call" | custom-call | flops 8589934592 | bytes 33554432 | tf_op jit(solution)/shard_map/own_exposure/pallas_call | solution.py:261
  55.1 14.2 %backward.3 = (bf16[2048,512]{1,0:T(8,128)(2,1)}, f32[776,512]{1,0:T(8,128)}, f32[776,512]{1,0:T(8,128)S(1)}) custom-call(s32[1]{0:T(128)} %bitcast.7.half, s32[1,2048]{1,0:T(1,128)S(1)} %get-tuple-element.144.rank_ref, f32[2048,512]{1,0:T(8,128)S(1)} %get-tuple-element.151.exposure_ref, f32[256,512]{1,0:T(8,128)S(1)} %collective-permute-done.29.got, ...), custom_call_target="tpu_custom_call" | custom-call | tf_op jit(solution)/shard_map/backward/pallas_call | solution.py:395
  69.5 3.3 %collective-permute-done.30.refs_1_ = f32[776,512]{1,0:T(8,128)S(1)} collective-permute-done((f32[776,512]{1,0:T(8,128)S(1)}, f32[776,512]{1,0:T(8,128)S(1)}, u32[]{:S(2)}, u32[]{:S(2)}) %collective-permute-start.30) | collective-permute-done | bytes 1589280 | tf_op jit(solution)/shard_map/ppermute | solution.py:502
  72.8 1.4 copy-done.1
  76.2 1.5 %collective-permute-start.32 = (f32[136,512]{1,0:T(8,128)S(1)}, f32[136,512]{1,0:T(8,128)S(1)}, u32[]{:S(2)}, u32[]{:S(2)}) collective-permute-start(f32[136,512]{1,0:T(8,128)S(1)} %get-tuple-element.164), channel_id=1, source_target_pairs={{0,16},{1,17},{2,18},{3,19},{4,20},{5,21},{6,22},{7,23},{8,24},{9,... | collective-permute-start | bytes 835592 | tf_op jit(solution)/shard_map/ppermute | solution.py:502
  78.6 1.5 %collective-permute-start.34 = (f32[64,512]{1,0:T(8,128)S(1)}, f32[64,512]{1,0:T(8,128)S(1)}, u32[]{:S(2)}, u32[]{:S(2)}) collective-permute-start(f32[64,512]{1,0:T(8,128)S(1)} %get-tuple-element.167), channel_id=1, source_target_pairs={{0,2},{1,3},{2,0},{3,1},{4,6},{5,7},{6,4},{7,5},{8,10},{9,11},{10,... | collective-permute-start | bytes 393224 | tf_op jit(solution)/shard_map/ppermute | solution.py:502
  80.1 2.7 %collective-permute-start.35 = (f32[64,512]{1,0:T(8,128)S(1)}, f32[64,512]{1,0:T(8,128)S(1)}, u32[]{:S(2)}, u32[]{:S(2)}) collective-permute-start(f32[64,512]{1,0:T(8,128)S(1)} %get-tuple-element.168), channel_id=1, source_target_pairs={{0,4},{1,5},{2,6},{3,7},{4,0},{5,1},{6,2},{7,3},{8,12},{9,13},{10,... | collective-permute-start | bytes 393224 | tf_op jit(solution)/shard_map/ppermute | solution.py:502
  82.8 2.5 %collective-permute-done.34.refs_5_ = f32[64,512]{1,0:T(8,128)S(1)} collective-permute-done((f32[64,512]{1,0:T(8,128)S(1)}, f32[64,512]{1,0:T(8,128)S(1)}, u32[]{:S(2)}, u32[]{:S(2)}) %collective-permute-start.34) | collective-permute-done | bytes 131104 | tf_op jit(solution)/shard_map/ppermute | solution.py:502
  85.3 3.0 %collective-permute-start.36 = (f32[64,512]{1,0:T(8,128)S(1)}, f32[64,512]{1,0:T(8,128)S(1)}, u32[]{:S(2)}, u32[]{:S(2)}) collective-permute-start(f32[64,512]{1,0:T(8,128)S(1)} %get-tuple-element.169), channel_id=1, source_target_pairs={{0,6},{1,7},{2,4},{3,5},{4,2},{5,3},{6,0},{7,1},{8,14},{9,15},{10,... | collective-permute-start | bytes 393224 | tf_op jit(solution)/shard_map/ppermute | solution.py:502
  88.4 2.4 %collective-permute-done.35.refs_6_ = f32[64,512]{1,0:T(8,128)S(1)} collective-permute-done((f32[64,512]{1,0:T(8,128)S(1)}, f32[64,512]{1,0:T(8,128)S(1)}, u32[]{:S(2)}, u32[]{:S(2)}) %collective-permute-start.35) | collective-permute-done | bytes 131104 | tf_op jit(solution)/shard_map/ppermute | solution.py:502
  93.0 2.7 %collective-permute-start.37 = (f32[40,512]{1,0:T(8,128)S(1)}, f32[40,512]{1,0:T(8,128)S(1)}, u32[]{:S(2)}, u32[]{:S(2)}) collective-permute-start(f32[40,512]{1,0:T(8,128)S(1)} %get-tuple-element.171), channel_id=1, source_target_pairs={{0,2},{1,3},{2,0},{3,1},{4,6},{5,7},{6,4},{7,5},{8,10},{9,11},{10,... | collective-permute-start | bytes 245768 | tf_op jit(solution)/shard_map/ppermute | solution.py:502
  99.2 1.5 %collective-permute-start.41 = (f32[16,512]{1,0:T(8,128)S(1)}, f32[16,512]{1,0:T(8,128)S(1)}, u32[]{:S(2)}, u32[]{:S(2)}) collective-permute-start(f32[16,512]{1,0:T(8,128)S(1)} %get-tuple-element.176), channel_id=1, source_target_pairs={{0,16},{1,17},{2,18},{3,19},{4,20},{5,21},{6,22},{7,23},{8,24},{9,... | collective-permute-start | bytes 98312 | tf_op jit(solution)/shard_map/ppermute | solution.py:502
  100.7 1.5 %collective-permute-done.40.refs_5_ = f32[16,512]{1,0:T(8,128)S(1)} collective-permute-done((f32[16,512]{1,0:T(8,128)S(1)}, f32[16,512]{1,0:T(8,128)S(1)}, u32[]{:S(2)}, u32[]{:S(2)}) %collective-permute-start.40) | collective-permute-done | bytes 32800 | tf_op jit(solution)/shard_map/ppermute | solution.py:502
  102.2 1.9 %collective-permute-start.42 = (f32[16,512]{1,0:T(8,128)S(1)}, f32[16,512]{1,0:T(8,128)S(1)}, u32[]{:S(2)}, u32[]{:S(2)}) collective-permute-start(f32[16,512]{1,0:T(8,128)S(1)} %get-tuple-element.177), channel_id=1, source_target_pairs={{0,17},{1,16},{2,19},{3,18},{4,21},{5,20},{6,23},{7,22},{8,25},{9,... | collective-permute-start | bytes 98312 | tf_op jit(solution)/shard_map/ppermute | solution.py:502
  104.1 2.9 %collective-permute-done.42.refs_7_ = f32[16,512]{1,0:T(8,128)S(1)} collective-permute-done((f32[16,512]{1,0:T(8,128)S(1)}, f32[16,512]{1,0:T(8,128)S(1)}, u32[]{:S(2)}, u32[]{:S(2)}) %collective-permute-start.42) | collective-permute-done | bytes 32800 | tf_op jit(solution)/shard_map/ppermute | solution.py:502
  109.6 1.7 %collective-permute-start.44 = (f32[32,512]{1,0:T(8,128)S(1)}, f32[32,512]{1,0:T(8,128)S(1)}, u32[]{:S(2)}, u32[]{:S(2)}) collective-permute-start(f32[32,512]{1,0:T(8,128)S(1)} %get-tuple-element.179.refs_0_), channel_id=1, source_target_pairs={{0,4},{1,5},{2,6},{3,7},{4,0},{5,1},{6,2},{7,3},{8,12},{9,13},{10,... | collective-permute-start | bytes 196616 | tf_op jit(solution)/shard_map/ppermute | solution.py:502
  111.3 1.6 %collective-permute-start.45 = (f32[32,512]{1,0:T(8,128)S(1)}, f32[32,512]{1,0:T(8,128)S(1)}, u32[]{:S(2)}, u32[]{:S(2)}) collective-permute-start(f32[32,512]{1,0:T(8,128)S(1)} %get-tuple-element.179.refs_0_), channel_id=1, source_target_pairs={{0,6},{1,7},{2,4},{3,5},{4,2},{5,3},{6,0},{7,1},{8,14},{9,15},{10,... | collective-permute-start | bytes 196616 | tf_op jit(solution)/shard_map/ppermute | solution.py:502
  112.9 1.9 %collective-permute-start.47 = (f32[16,512]{1,0:T(8,128)S(1)}, f32[16,512]{1,0:T(8,128)S(1)}, u32[]{:S(2)}, u32[]{:S(2)}) collective-permute-start(f32[16,512]{1,0:T(8,128)S(1)} %get-tuple-element.180.refs_4_), channel_id=1, source_target_pairs={{0,16},{1,17},{2,18},{3,19},{4,20},{5,21},{6,22},{7,23},{8,24},{9,... | collective-permute-start | bytes 98312 | tf_op jit(solution)/shard_map/ppermute | solution.py:502
  116.9 3.3 %collective-permute-done.48.refs_7_ = f32[16,512]{1,0:T(8,128)S(1)} collective-permute-done((f32[16,512]{1,0:T(8,128)S(1)}, f32[16,512]{1,0:T(8,128)S(1)}, u32[]{:S(2)}, u32[]{:S(2)}) %collective-permute-start.48) | collective-permute-done | bytes 32800 | tf_op jit(solution)/shard_map/ppermute | solution.py:502
  122.3 2.1 %collective-permute-start.51 = (f32[128,512]{1,0:T(8,128)S(1)}, f32[128,512]{1,0:T(8,128)S(1)}, u32[]{:S(2)}, u32[]{:S(2)}) collective-permute-start(f32[128,512]{1,0:T(8,128)S(1)} %get-tuple-element.181.refs_0_), channel_id=1, source_target_pairs={{0,17},{1,16},{2,19},{3,18},{4,21},{5,20},{6,23},{7,22},{8,25},{9,... | collective-permute-start | bytes 786440 | tf_op jit(solution)/shard_map/ppermute | solution.py:502
  124.4 3.0 %collective-permute-start.53 = (f32[64,512]{1,0:T(8,128)S(1)}, f32[64,512]{1,0:T(8,128)S(1)}, u32[]{:S(2)}, u32[]{:S(2)}) collective-permute-start(f32[64,512]{1,0:T(8,128)S(1)} %get-tuple-element.182.refs_4_), channel_id=1, source_target_pairs={{0,4},{1,5},{2,6},{3,7},{4,0},{5,1},{6,2},{7,3},{8,12},{9,13},{10,... | collective-permute-start | bytes 393224 | tf_op jit(solution)/shard_map/ppermute | solution.py:502
  128.7 3.1 %collective-permute-done.53.refs_6_ = f32[64,512]{1,0:T(8,128)S(1)} collective-permute-done((f32[64,512]{1,0:T(8,128)S(1)}, f32[64,512]{1,0:T(8,128)S(1)}, u32[]{:S(2)}, u32[]{:S(2)}) %collective-permute-start.53) | collective-permute-done | bytes 131104 | tf_op jit(solution)/shard_map/ppermute | solution.py:502
  131.8 2.5 %collective-permute-done.54.refs_7_ = f32[64,512]{1,0:T(8,128)S(1)} collective-permute-done((f32[64,512]{1,0:T(8,128)S(1)}, f32[64,512]{1,0:T(8,128)S(1)}, u32[]{:S(2)}, u32[]{:S(2)}) %collective-permute-start.54) | collective-permute-done | bytes 131104 | tf_op jit(solution)/shard_map/ppermute | solution.py:502
  136.3 2.2 %collective-permute-done.55 = f32[768,512]{1,0:T(8,128)S(1)} collective-permute-done((f32[768,512]{1,0:T(8,128)S(1)}, f32[768,512]{1,0:T(8,128)S(1)}, u32[]{:S(2)}, u32[]{:S(2)}) %collective-permute-start.55) | collective-permute-done | bytes 1572896 | tf_op jit(solution)/shard_map/ppermute | solution.py:502
  138.6 4.7 %conditional.1 = (bf16[2048,512]{1,0:T(8,128)(2,1)}, (f32[512,512]{1,0:T(8,128)}, f32[512,512]{1,0:T(8,128)}, f32[512,512]{1,0:T(8,128)}), (f32[512,512]{1,0:T(8...) conditional(s32[]{:T(128)} %bitcast.11, (f32[8,512]{1,0:T(8,128)S(1)}, s32[1]{0:T(128)}, ...), branch_computations={%region_0.1_spmd, %region_1.2_spmd} | conditional | flops 17179869184 | bytes 196970400 | solution.py:635
  138.6 1.9 %finish.2 = (f32[512,512]{1,0:T(8,128)}, f32[512,512]{1,0:T(8,128)}, f32[512,512]{1,0:T(8,128)}) custom-call(s32[1]{0:T(128)} %get-tuple-element.39.half, f32[768,512]{1,0:T(8,128)S(1)} %get-tuple-element.40.own, f32[768,512]{1,0:T(8,128)S(1)} %get-tuple-element.41.got), custom_call_target="tpu_custom_call" | custom-call | tf_op jit(solution)/shard_map/cond/branch_0_fun/finish/pallas_call | solution.py:569
  (87 shorter events, 25.7 us)
Async XLA Ops:
  16.4 17.1 %collective-permute-start.28 = (f32[264,512]{1,0:T(8,128)S(1)}, f32[264,512]{1,0:T(8,128)S(1)}, u32[]{:S(2)}, u32[]{:S(2)}) collective-permute-start(f32[264,512]{1,0:T(8,128)S(1)} %get-tuple-element.148), channel_id=1, source_target_pairs={{1,0},{2,1},{3,2},{4,3},{5,4},{6,5},{7,6},{9,8},{10,9},{11,10},{12... | collective-permute-start | bytes 1622024 | tf_op jit(solution)/shard_map/ppermute | solution.py:583
  38.9 16.1 %collective-permute-start.29 = (f32[256,512]{1,0:T(8,128)S(1)}, f32[256,512]{1,0:T(8,128)S(1)}, u32[]{:S(2)}, u32[]{:S(2)}) collective-permute-start(f32[256,512]{1,0:T(8,128)S(1)} %get-tuple-element.152), channel_id=1, source_target_pairs={{0,1},{1,2},{2,3},{3,4},{4,5},{5,6},{6,7},{8,9},{9,10},{10,11},{11... | collective-permute-start | bytes 1572872 | tf_op jit(solution)/shard_map/ppermute | solution.py:583
  69.3 3.4 %collective-permute-start.30 = (f32[776,512]{1,0:T(8,128)S(1)}, f32[776,512]{1,0:T(8,128)S(1)}, u32[]{:S(2)}, u32[]{:S(2)}) collective-permute-start(f32[776,512]{1,0:T(8,128)S(1)} %get-tuple-element.161), channel_id=1, source_target_pairs={{0,8},{1,9},{2,10},{3,11},{4,12},{5,13},{6,14},{7,15},{8,0},{9,1},... | collective-permute-start | bytes 4767752 | tf_op jit(solution)/shard_map/ppermute | solution.py:502
  75.0 17.2 %collective-permute-start.31 = (f32[136,512]{1,0:T(8,128)S(1)}, f32[136,512]{1,0:T(8,128)S(1)}, u32[]{:S(2)}, u32[]{:S(2)}) collective-permute-start(f32[136,512]{1,0:T(8,128)S(1)} %get-tuple-element.163), channel_id=1, source_target_pairs={{0,1},{1,0},{2,3},{3,2},{4,5},{5,4},{6,7},{7,6},{8,9},{9,8},{10,11... | collective-permute-start | bytes 835592 | tf_op jit(solution)/shard_map/ppermute | solution.py:502
  76.2 16.0 %collective-permute-start.32 = (f32[136,512]{1,0:T(8,128)S(1)}, f32[136,512]{1,0:T(8,128)S(1)}, u32[]{:S(2)}, u32[]{:S(2)}) collective-permute-start(f32[136,512]{1,0:T(8,128)S(1)} %get-tuple-element.164), channel_id=1, source_target_pairs={{0,16},{1,17},{2,18},{3,19},{4,20},{5,21},{6,22},{7,23},{8,24},{9,... | collective-permute-start | bytes 835592 | tf_op jit(solution)/shard_map/ppermute | solution.py:502
  77.8 14.4 %collective-permute-start.33 = (f32[136,512]{1,0:T(8,128)S(1)}, f32[136,512]{1,0:T(8,128)S(1)}, u32[]{:S(2)}, u32[]{:S(2)}) collective-permute-start(f32[136,512]{1,0:T(8,128)S(1)} %get-tuple-element.165), channel_id=1, source_target_pairs={{0,17},{1,16},{2,19},{3,18},{4,21},{5,20},{6,23},{7,22},{8,25},{9,... | collective-permute-start | bytes 835592 | tf_op jit(solution)/shard_map/ppermute | solution.py:502
  78.6 6.7 %collective-permute-start.34 = (f32[64,512]{1,0:T(8,128)S(1)}, f32[64,512]{1,0:T(8,128)S(1)}, u32[]{:S(2)}, u32[]{:S(2)}) collective-permute-start(f32[64,512]{1,0:T(8,128)S(1)} %get-tuple-element.167), channel_id=1, source_target_pairs={{0,2},{1,3},{2,0},{3,1},{4,6},{5,7},{6,4},{7,5},{8,10},{9,11},{10,... | collective-permute-start | bytes 393224 | tf_op jit(solution)/shard_map/ppermute | solution.py:502
  80.1 10.7 %collective-permute-start.35 = (f32[64,512]{1,0:T(8,128)S(1)}, f32[64,512]{1,0:T(8,128)S(1)}, u32[]{:S(2)}, u32[]{:S(2)}) collective-permute-start(f32[64,512]{1,0:T(8,128)S(1)} %get-tuple-element.168), channel_id=1, source_target_pairs={{0,4},{1,5},{2,6},{3,7},{4,0},{5,1},{6,2},{7,3},{8,12},{9,13},{10,... | collective-permute-start | bytes 393224 | tf_op jit(solution)/shard_map/ppermute | solution.py:502
  85.3 6.9 %collective-permute-start.36 = (f32[64,512]{1,0:T(8,128)S(1)}, f32[64,512]{1,0:T(8,128)S(1)}, u32[]{:S(2)}, u32[]{:S(2)}) collective-permute-start(f32[64,512]{1,0:T(8,128)S(1)} %get-tuple-element.169), channel_id=1, source_target_pairs={{0,6},{1,7},{2,4},{3,5},{4,2},{5,3},{6,0},{7,1},{8,14},{9,15},{10,... | collective-permute-start | bytes 393224 | tf_op jit(solution)/shard_map/ppermute | solution.py:502
  92.2 46.3 %copy-start.28 = (bf16[35,512]{1,0:T(8,128)(2,1)S(1)}, bf16[35,512]{1,0:T(8,128)(2,1)}, u32[]{:S(2)}) copy-start(bf16[35,512]{1,0:T(8,128)(2,1)} %constant.98.clone.low_ref) | copy-start | bytes 107524
  92.2 46.3 %copy-start.29 = (bf16[35,512]{1,0:T(8,128)(2,1)S(1)}, bf16[35,512]{1,0:T(8,128)(2,1)}, u32[]{:S(2)}) copy-start(bf16[35,512]{1,0:T(8,128)(2,1)} %constant.99.clone.high_ref) | copy-start | bytes 107524
  92.9 45.6 %copy-start.8 = (bf16[2048,512]{1,0:T(8,128)(2,1)S(1)}, bf16[2048,512]{1,0:T(8,128)(2,1)}, u32[]{:S(2)}) copy-start(bf16[2048,512]{1,0:T(8,128)(2,1)} %x_ref.3) | copy-start | bytes 6291460
  92.9 45.6 %copy-start.11 = (bf16[512,512]{1,0:T(8,128)(2,1)S(1)}, bf16[512,512]{1,0:T(8,128)(2,1)}, u32[]{:S(2)}) copy-start(bf16[512,512]{1,0:T(8,128)(2,1)} %w_in.3) | copy-start | bytes 1572868
  93.0 14.0 %collective-permute-start.37 = (f32[40,512]{1,0:T(8,128)S(1)}, f32[40,512]{1,0:T(8,128)S(1)}, u32[]{:S(2)}, u32[]{:S(2)}) collective-permute-start(f32[40,512]{1,0:T(8,128)S(1)} %get-tuple-element.171), channel_id=1, source_target_pairs={{0,2},{1,3},{2,0},{3,1},{4,6},{5,7},{6,4},{7,5},{8,10},{9,11},{10,... | collective-permute-start | bytes 245768 | tf_op jit(solution)/shard_map/ppermute | solution.py:502
  95.7 11.3 %collective-permute-start.38 = (f32[40,512]{1,0:T(8,128)S(1)}, f32[40,512]{1,0:T(8,128)S(1)}, u32[]{:S(2)}, u32[]{:S(2)}) collective-permute-start(f32[40,512]{1,0:T(8,128)S(1)} %get-tuple-element.172), channel_id=1, source_target_pairs={{0,4},{1,5},{2,6},{3,7},{4,0},{5,1},{6,2},{7,3},{8,12},{9,13},{10,... | collective-permute-start | bytes 245768 | tf_op jit(solution)/shard_map/ppermute | solution.py:502
  96.9 10.1 %collective-permute-start.39 = (f32[40,512]{1,0:T(8,128)S(1)}, f32[40,512]{1,0:T(8,128)S(1)}, u32[]{:S(2)}, u32[]{:S(2)}) collective-permute-start(f32[40,512]{1,0:T(8,128)S(1)} %get-tuple-element.173), channel_id=1, source_target_pairs={{0,6},{1,7},{2,4},{3,5},{4,2},{5,3},{6,0},{7,1},{8,14},{9,15},{10,... | collective-permute-start | bytes 245768 | tf_op jit(solution)/shard_map/ppermute | solution.py:502
  98.3 3.9 %collective-permute-start.40 = (f32[16,512]{1,0:T(8,128)S(1)}, f32[16,512]{1,0:T(8,128)S(1)}, u32[]{:S(2)}, u32[]{:S(2)}) collective-permute-start(f32[16,512]{1,0:T(8,128)S(1)} %get-tuple-element.175), channel_id=1, source_target_pairs={{0,1},{1,0},{2,3},{3,2},{4,5},{5,4},{6,7},{7,6},{8,9},{9,8},{10,11... | collective-permute-start | bytes 98312 | tf_op jit(solution)/shard_map/ppermute | solution.py:502
  99.2 5.0 %collective-permute-start.41 = (f32[16,512]{1,0:T(8,128)S(1)}, f32[16,512]{1,0:T(8,128)S(1)}, u32[]{:S(2)}, u32[]{:S(2)}) collective-permute-start(f32[16,512]{1,0:T(8,128)S(1)} %get-tuple-element.176), channel_id=1, source_target_pairs={{0,16},{1,17},{2,18},{3,19},{4,20},{5,21},{6,22},{7,23},{8,24},{9,... | collective-permute-start | bytes 98312 | tf_op jit(solution)/shard_map/ppermute | solution.py:502
  102.2 4.8 %collective-permute-start.42 = (f32[16,512]{1,0:T(8,128)S(1)}, f32[16,512]{1,0:T(8,128)S(1)}, u32[]{:S(2)}, u32[]{:S(2)}) collective-permute-start(f32[16,512]{1,0:T(8,128)S(1)} %get-tuple-element.177), channel_id=1, source_target_pairs={{0,17},{1,16},{2,19},{3,18},{4,21},{5,20},{6,23},{7,22},{8,25},{9,... | collective-permute-start | bytes 98312 | tf_op jit(solution)/shard_map/ppermute | solution.py:502
  107.6 7.2 %collective-permute-start.46 = (f32[16,512]{1,0:T(8,128)S(1)}, f32[16,512]{1,0:T(8,128)S(1)}, u32[]{:S(2)}, u32[]{:S(2)}) collective-permute-start(f32[16,512]{1,0:T(8,128)S(1)} %get-tuple-element.180.refs_4_), channel_id=1, source_target_pairs={{0,1},{1,0},{2,3},{3,2},{4,5},{5,4},{6,7},{7,6},{8,9},{9,8},{10,11... | collective-permute-start | bytes 98312 | tf_op jit(solution)/shard_map/ppermute | solution.py:502
  108.6 11.6 %collective-permute-start.43 = (f32[32,512]{1,0:T(8,128)S(1)}, f32[32,512]{1,0:T(8,128)S(1)}, u32[]{:S(2)}, u32[]{:S(2)}) collective-permute-start(f32[32,512]{1,0:T(8,128)S(1)} %get-tuple-element.179.refs_0_), channel_id=1, source_target_pairs={{0,2},{1,3},{2,0},{3,1},{4,6},{5,7},{6,4},{7,5},{8,10},{9,11},{10,... | collective-permute-start | bytes 196616 | tf_op jit(solution)/shard_map/ppermute | solution.py:502
  109.6 10.6 %collective-permute-start.44 = (f32[32,512]{1,0:T(8,128)S(1)}, f32[32,512]{1,0:T(8,128)S(1)}, u32[]{:S(2)}, u32[]{:S(2)}) collective-permute-start(f32[32,512]{1,0:T(8,128)S(1)} %get-tuple-element.179.refs_0_), channel_id=1, source_target_pairs={{0,4},{1,5},{2,6},{3,7},{4,0},{5,1},{6,2},{7,3},{8,12},{9,13},{10,... | collective-permute-start | bytes 196616 | tf_op jit(solution)/shard_map/ppermute | solution.py:502
  111.3 8.8 %collective-permute-start.45 = (f32[32,512]{1,0:T(8,128)S(1)}, f32[32,512]{1,0:T(8,128)S(1)}, u32[]{:S(2)}, u32[]{:S(2)}) collective-permute-start(f32[32,512]{1,0:T(8,128)S(1)} %get-tuple-element.179.refs_0_), channel_id=1, source_target_pairs={{0,6},{1,7},{2,4},{3,5},{4,2},{5,3},{6,0},{7,1},{8,14},{9,15},{10,... | collective-permute-start | bytes 196616 | tf_op jit(solution)/shard_map/ppermute | solution.py:502
  112.9 3.9 %collective-permute-start.47 = (f32[16,512]{1,0:T(8,128)S(1)}, f32[16,512]{1,0:T(8,128)S(1)}, u32[]{:S(2)}, u32[]{:S(2)}) collective-permute-start(f32[16,512]{1,0:T(8,128)S(1)} %get-tuple-element.180.refs_4_), channel_id=1, source_target_pairs={{0,16},{1,17},{2,18},{3,19},{4,20},{5,21},{6,22},{7,23},{8,24},{9,... | collective-permute-start | bytes 98312 | tf_op jit(solution)/shard_map/ppermute | solution.py:502
  114.9 5.3 %collective-permute-start.48 = (f32[16,512]{1,0:T(8,128)S(1)}, f32[16,512]{1,0:T(8,128)S(1)}, u32[]{:S(2)}, u32[]{:S(2)}) collective-permute-start(f32[16,512]{1,0:T(8,128)S(1)} %get-tuple-element.180.refs_4_), channel_id=1, source_target_pairs={{0,17},{1,16},{2,19},{3,18},{4,21},{5,20},{6,23},{7,22},{8,25},{9,... | collective-permute-start | bytes 98312 | tf_op jit(solution)/shard_map/ppermute | solution.py:502
  120.8 6.7 %collective-permute-start.52 = (f32[64,512]{1,0:T(8,128)S(1)}, f32[64,512]{1,0:T(8,128)S(1)}, u32[]{:S(2)}, u32[]{:S(2)}) collective-permute-start(f32[64,512]{1,0:T(8,128)S(1)} %get-tuple-element.182.refs_4_), channel_id=1, source_target_pairs={{0,2},{1,3},{2,0},{3,1},{4,6},{5,7},{6,4},{7,5},{8,10},{9,11},{10,... | collective-permute-start | bytes 393224 | tf_op jit(solution)/shard_map/ppermute | solution.py:502
  120.9 13.5 %collective-permute-start.49 = (f32[128,512]{1,0:T(8,128)S(1)}, f32[128,512]{1,0:T(8,128)S(1)}, u32[]{:S(2)}, u32[]{:S(2)}) collective-permute-start(f32[128,512]{1,0:T(8,128)S(1)} %get-tuple-element.181.refs_0_), channel_id=1, source_target_pairs={{0,1},{1,0},{2,3},{3,2},{4,5},{5,4},{6,7},{7,6},{8,9},{9,8},{10,11... | collective-permute-start | bytes 786440 | tf_op jit(solution)/shard_map/ppermute | solution.py:502
  122.3 12.1 %collective-permute-start.50 = (f32[128,512]{1,0:T(8,128)S(1)}, f32[128,512]{1,0:T(8,128)S(1)}, u32[]{:S(2)}, u32[]{:S(2)}) collective-permute-start(f32[128,512]{1,0:T(8,128)S(1)} %get-tuple-element.181.refs_0_), channel_id=1, source_target_pairs={{0,16},{1,17},{2,18},{3,19},{4,20},{5,21},{6,22},{7,23},{8,24},{9,... | collective-permute-start | bytes 786440 | tf_op jit(solution)/shard_map/ppermute | solution.py:502
  122.3 12.1 %collective-permute-start.51 = (f32[128,512]{1,0:T(8,128)S(1)}, f32[128,512]{1,0:T(8,128)S(1)}, u32[]{:S(2)}, u32[]{:S(2)}) collective-permute-start(f32[128,512]{1,0:T(8,128)S(1)} %get-tuple-element.181.refs_0_), channel_id=1, source_target_pairs={{0,17},{1,16},{2,19},{3,18},{4,21},{5,20},{6,23},{7,22},{8,25},{9,... | collective-permute-start | bytes 786440 | tf_op jit(solution)/shard_map/ppermute | solution.py:502
  124.4 7.4 %collective-permute-start.53 = (f32[64,512]{1,0:T(8,128)S(1)}, f32[64,512]{1,0:T(8,128)S(1)}, u32[]{:S(2)}, u32[]{:S(2)}) collective-permute-start(f32[64,512]{1,0:T(8,128)S(1)} %get-tuple-element.182.refs_4_), channel_id=1, source_target_pairs={{0,4},{1,5},{2,6},{3,7},{4,0},{5,1},{6,2},{7,3},{8,12},{9,13},{10,... | collective-permute-start | bytes 393224 | tf_op jit(solution)/shard_map/ppermute | solution.py:502
  127.5 6.9 %collective-permute-start.54 = (f32[64,512]{1,0:T(8,128)S(1)}, f32[64,512]{1,0:T(8,128)S(1)}, u32[]{:S(2)}, u32[]{:S(2)}) collective-permute-start(f32[64,512]{1,0:T(8,128)S(1)} %get-tuple-element.182.refs_4_), channel_id=1, source_target_pairs={{0,6},{1,7},{2,4},{3,5},{4,2},{5,3},{6,0},{7,1},{8,14},{9,15},{10,... | collective-permute-start | bytes 393224 | tf_op jit(solution)/shard_map/ppermute | solution.py:502
  135.0 3.5 %collective-permute-start.55 = (f32[768,512]{1,0:T(8,128)S(1)}, f32[768,512]{1,0:T(8,128)S(1)}, u32[]{:S(2)}, u32[]{:S(2)}) collective-permute-start(f32[768,512]{1,0:T(8,128)S(1)} %collect_second.3), channel_id=1, source_target_pairs={{0,8},{1,9},{2,10},{3,11},{4,12},{5,13},{6,14},{7,15},{8,0},{9,1},... | collective-permute-start | bytes 4718600 | tf_op jit(solution)/shard_map/ppermute | solution.py:502
  (15 other events, 243.4 us)

commit v3 on v2

v3 whole, which is shorter than its diff:
```python
from functools import partial

import jax
import jax.numpy as jnp
import numpy as np
from jax import lax
from jax.experimental import pallas as pl
from jax.experimental.pallas import tpu as pltpu
from jax.sharding import PartitionSpec as P

BITS = 15
LANES = 128
TILE = 512
DEPTH = 512
GROUP = 256
MIB = 1024 * 1024
F32 = jnp.float32
BF16 = jnp.bfloat16
I32 = jnp.int32


def two_parts(value):
    top = value.astype(BF16)
    return top, (value - top.astype(F32)).astype(BF16)


def iota(shape, dim):
    return lax.broadcasted_iota(I32, shape, dim)


def ones_where(mask):
    return jnp.where(mask, 1.0, 0.0).astype(BF16)


def dot(a, b, ca=1, cb=0):
    return lax.dot_general(a, b, (((ca,), (cb,)), ((), ())), preferred_element_type=F32)


def widen(column, width):
    return jnp.concatenate([column] * (width // column.shape[1]), axis=1)


def as_column(row):
    parts = [
        jnp.broadcast_to(row[:, k : k + LANES], (LANES, LANES)).T
        for k in range(0, row.shape[1], LANES)
    ]
    return jnp.concatenate(parts, axis=0)


def whole():
    return pl.BlockSpec(memory_space=pltpu.VMEM)


def rows_of(tile, width):
    return pl.BlockSpec((tile, width), lambda i: (i, 0))


def fixed(shape):
    return pl.BlockSpec(shape, lambda i: (0, 0), pipeline_mode=pl.Buffered(1))


def lanes_of(height, tile):
    return pl.BlockSpec((height, tile), lambda i: (0, i))


def in_hbm(array):
    return pltpu.with_memory_space_constraint(array, pltpu.HBM)


def in_vmem(array):
    return pltpu.with_memory_space_constraint(array, pltpu.VMEM)


def sent_rows(cap):
    return cap * 3 // 4 if cap == GROUP else cap


def group_rows(t, sent):
    return pl.ds(0, sent) if sent < GROUP else pl.ds(pl.multiple_of(t * GROUP, GROUP), GROUP)


def put_parts(out, chunk, value):
    rows = value.shape[0]
    at = 0 if chunk is None else pl.multiple_of(chunk * 2 * rows, 2 * rows)
    out[pl.ds(at, rows), :], out[pl.ds(at + rows, rows), :] = two_parts(value)


def twice(mask, chunk):
    parts = []
    for k in range(0, mask.shape[1], chunk):
        parts += [mask[:, k : k + chunk]] * 2
    return jnp.concatenate(parts, axis=1)


def params(mib):
    return pltpu.CompilerParams(vmem_limit_bytes=mib * MIB)


def rank_entries(entry_ref, rank_ref, note, cap):
    rows = entry_ref.shape[1]
    high = rows // LANES
    place = entry_ref[...] + rows
    crosses = place < rows
    high_hit = ones_where((iota((high, rows), 0) == (place >> 7)) & crosses)
    low_hit = jnp.where((iota((LANES, rows), 0) == (place & (LANES - 1))) & crosses, 1.0, 0.0)
    present = ones_where(dot(high_hit, low_hit.astype(BF16), 1, 1) > 0.5)
    square = (LANES, LANES)
    within = dot(present, ones_where(iota(square, 0) < iota(square, 1)))
    small = (high, high)
    ahead = dot(ones_where(iota(small, 1) < iota(small, 0)), present)
    table = within + jnp.sum(ahead, axis=1, keepdims=True)
    table_high = jnp.floor(table * (1.0 / 256.0))
    table_low = table - 256.0 * table_high
    found = 256.0 * dot(table_high.astype(BF16), high_hit, 0, 0)
    found = found + dot(table_low.astype(BF16), high_hit, 0, 0)
    rank = jnp.sum(found * low_hit, axis=0, keepdims=True)
    rank_ref[...] = jnp.where(crosses, rank.astype(I32), -1)
    count = jnp.sum(present.astype(F32))
    note[...] = jnp.where(iota(note.shape, 0) == 1, jnp.where(count > sent_rows(cap), 1.0, 0.0), 0.0)


def trunk_kernel(
    cap, entry_ref, x_ref, events_ref, byte_ref, shift_ref, w_in, w_mid, w_out,
    first_hidden, hidden, slope_in, slope_mid, indicator_out, weight, send, note,
    rank_ref,
):
    step = pl.program_id(0)
    tile = x_ref.shape[0]

    @pl.when(step == 0)
    def _():
        rank_entries(entry_ref, rank_ref, note, cap)
        send[...] = jnp.zeros_like(send)

    events = events_ref[...]
    split = jnp.concatenate([events & 255, events >> 8], axis=0).astype(F32).astype(BF16)
    spread = dot(split, byte_ref[...], 0, 0)
    bits = jnp.bitwise_and(jnp.right_shift(spread.astype(I32), shift_ref[...]), 1)
    indicator = bits.astype(F32)
    indicator_out[...] = indicator.astype(BF16)

    preact = dot(x_ref[...], w_in[...])
    sigma = jax.nn.sigmoid(preact)
    first = (preact * sigma).astype(BF16)
    first_hidden[...] = first
    slope_in[...] = sigma * (1.0 + preact * (1.0 - sigma))
    mid_pre = dot(first, w_mid[...])
    sigma = jax.nn.sigmoid(mid_pre)
    second = (mid_pre * sigma).astype(BF16)
    hidden[...] = second
    slope_mid[...] = sigma * (1.0 + mid_pre * (1.0 - sigma))
    log_hazard = dot(second, w_out[...])
    put_parts(weight, None, jnp.exp(log_hazard))
    note[0:1, :] -= jnp.sum(indicator * log_hazard, axis=0, keepdims=True)

    sent = sent_rows(cap)
    own = pl.ds(pl.multiple_of(step * tile, tile), tile)
    rank = rank_ref[:, own]
    entry = (entry_ref[:, own] + rank_ref.shape[1]).astype(F32)

    def total(t, _):
        hit = iota((GROUP, tile), 0) + t * GROUP == rank
        place = jnp.max(jnp.where(hit, entry, 0.0), axis=1, keepdims=True)
        place = jnp.broadcast_to(place, (GROUP, LANES))
        parts = [place[k : k + LANES, :].T[0:1] for k in range(0, GROUP, LANES)]
        spot = (send.shape[0] - sent, GROUP)
        place = jnp.broadcast_to(jnp.concatenate(parts, axis=1), spot)
        place = jnp.where(iota(spot, 0) == t, place, 0.0)
        send[sent:, 0:GROUP] = jnp.maximum(send[sent:, 0:GROUP], place)
        at = group_rows(t, sent)
        hit = ones_where(hit)[: min(GROUP, sent)]
        send[at, :] += dot(twice(hit, tile), weight[...])
        return 0

    lax.fori_loop(0, cap // GROUP, total, 0)


def trunk(cap, entry, features, events, w_in, w_mid, w_out):
    rows, width = features.shape
    mid = w_in.shape[1]
    wide = w_mid.shape[1]
    out_width = w_out.shape[1]
    words = events.shape[1]
    column = np.arange(out_width)
    owner = (np.arange(words)[:, None] == column // BITS).astype(np.float32)
    bit = column % BITS
    byte = jnp.asarray(np.concatenate([owner * (bit < 8), owner * (bit >= 8)]), BF16)
    shift = jnp.asarray((bit % 8)[None, :], I32)
    sent = sent_rows(cap) + -(-(cap // GROUP) // 8) * 8
    like = jax.ShapeDtypeStruct
    return pl.pallas_call(
        partial(trunk_kernel, cap),
        grid=(rows // TILE,),
        in_specs=[whole(), rows_of(TILE, width), lanes_of(words, TILE)]
        + [whole()] * 2
        + [fixed(w.shape) for w in (w_in, w_mid, w_out)],
        out_specs=[
            rows_of(TILE, mid), rows_of(TILE, wide), rows_of(TILE, mid), rows_of(TILE, wide),
            rows_of(TILE, out_width), rows_of(2 * TILE, out_width),
        ]
        + [whole()] * 3,
        out_shape=[
            pltpu.HBM((rows, mid), BF16), pltpu.HBM((rows, wide), BF16),
            pltpu.HBM((rows, mid), F32), pltpu.HBM((rows, wide), F32),
            pltpu.HBM((rows, out_width), BF16), pltpu.HBM((2 * rows, out_width), BF16),
            like((sent, out_width), F32),
            like((8, out_width), F32), like((1, rows), I32),
        ],
        compiler_params=params(28),
        name="trunk",
    )(entry, in_hbm(features), in_hbm(events.T), byte, shift, *map(in_hbm, (w_in, w_mid, w_out)))


def own_risk_kernel(starts, entry_ref, first_ref, weight, out):
    step = pl.program_id(0)
    tile = first_ref.shape[1]
    rows = weight.shape[0] // 2
    first = widen(as_column(first_ref[...]), DEPTH)
    own = pl.ds(pl.multiple_of(step * tile, tile), tile)
    out[own, :] = jnp.zeros((tile, out.shape[1]), F32)

    def part(k, _):
        at = pl.multiple_of(k * DEPTH, DEPTH)
        row = iota((tile, DEPTH), 1) + at
        entry = entry_ref[pl.ds(k, 1), :]
        mask = ones_where((row >= first) & (entry <= first))
        both = pl.ds(pl.multiple_of(k * 2 * DEPTH, 2 * DEPTH), 2 * DEPTH)
        out[own, :] += dot(twice(mask, DEPTH), weight[both, :])
        return 0

    lax.fori_loop(starts[step] // DEPTH, rows // DEPTH, part, 0)


def block_sum(flops):
    return pl.CostEstimate(flops=flops, bytes_accessed=flops // 256, transcendentals=0)


def own_risk(starts, entry, first, weight):
    rows, width = weight.shape[0] // 2, weight.shape[1]
    return pl.pallas_call(
        own_risk_kernel,
        grid=(rows // TILE,),
        in_specs=[
            pl.BlockSpec(memory_space=pltpu.SMEM), whole(), lanes_of(1, TILE),
            fixed(weight.shape),
        ],
        out_specs=whole(),
        out_shape=pltpu.VMEM((rows, width), F32),
        compiler_params=params(16),
        cost_estimate=block_sum(rows * rows * width * 4),
        name="own_risk",
    )(starts, entry.reshape(rows // DEPTH, DEPTH), first, in_hbm(weight))


def own_exposure_kernel(starts, first_ref, entry_ref, hazard, out, note):
    step = pl.program_id(0)
    tile = entry_ref.shape[1]

    @pl.when(step == 0)
    def _():
        note[...] = jnp.zeros_like(note)

    entry = widen(as_column(entry_ref[...]), DEPTH)
    row = iota((tile, DEPTH), 0) + step * tile
    own = pl.ds(pl.multiple_of(step * tile, tile), tile)
    out[own, :] = jnp.zeros((tile, out.shape[1]), F32)
    last = step * tile + tile - 1
    parts = jnp.int32(0)
    for k in range(first_ref.shape[0]):
        parts += jnp.where(starts[k * (DEPTH // TILE)] <= last, 1, 0).astype(I32)

    def part(k, _):
        first = first_ref[pl.ds(k, 1), :]
        mask = ones_where((first >= entry) & (first <= row))
        both = pl.ds(pl.multiple_of(k * 2 * DEPTH, 2 * DEPTH), 2 * DEPTH)
        out[own, :] += dot(twice(mask, DEPTH), hazard[both, :])
        return 0

    lax.fori_loop(0, parts, part, 0)
    top = hazard[pl.ds(pl.multiple_of(step * 2 * tile, tile), tile), :].astype(F32)
    rest = hazard[pl.ds(pl.multiple_of(step * 2 * tile + tile, tile), tile), :].astype(F32)
    logs = jnp.where(top > 0.0, jnp.log(top + rest), 0.0)
    note[0:1, :] -= jnp.sum(logs, axis=0, keepdims=True)


def own_exposure(starts, first, entry, hazard):
    rows, width = hazard.shape[0] // 2, hazard.shape[1]
    like = jax.ShapeDtypeStruct
    return pl.pallas_call(
        own_exposure_kernel,
        grid=(rows // TILE,),
        in_specs=[
            pl.BlockSpec(memory_space=pltpu.SMEM), whole(), lanes_of(1, TILE), whole()
        ],
        out_specs=[whole(), whole()],
        out_shape=[pltpu.VMEM((rows, width), F32), like((8, width), F32)],
        compiler_params=params(12),
        cost_estimate=block_sum(rows * rows * width * 4),
        name="own_exposure",
    )(starts, first.reshape(rows // DEPTH, DEPTH), entry, in_vmem(hazard))


def split_sum(source, parts, cap):
    sent = sent_rows(cap)
    for t in range(cap // GROUP):
        rows = min(GROUP, sent - t * GROUP)
        value = source[t * GROUP : t * GROUP + rows, :]
        if rows < GROUP:
            value = jnp.concatenate([value, jnp.zeros((GROUP - rows, value.shape[1]), F32)], axis=0)
        put_parts(parts, t, value)


def group_sum(mask, parts, t):
    at = pl.ds(pl.multiple_of(t * 2 * GROUP, 2 * GROUP), 2 * GROUP)
    return dot(twice(mask, GROUP), parts[at, :])


def hazard_kernel(
    cap, first_all, first_ref, risk, indicator_ref, got, hazard, sums, parts
):
    step = pl.program_id(0)
    tile = first_ref.shape[1]
    rows = hazard.shape[0] // 2
    own = pl.ds(pl.multiple_of(step * tile, tile), tile)

    @pl.when(step == 0)
    def _():
        split_sum(got, parts, cap)

    first = widen(as_column(first_ref[...]).astype(F32), GROUP)
    divisor = risk[own, :]
    sent = sent_rows(cap)

    def beyond(t, total):
        entry = got[pl.ds(sent + t, 1), 0:GROUP]
        return total + group_sum(ones_where(entry <= first), parts, t)

    divisor = lax.fori_loop(0, cap // GROUP, beyond, divisor)
    put_parts(hazard, step, indicator_ref[...].astype(F32) / divisor)

    @pl.when(step == pl.num_programs(0) - 1)
    def _():
        def total(t, _):
            entry = as_column(got[pl.ds(sent + t, 1), 0:GROUP])[: min(GROUP, sent)]
            entry = widen(entry, rows)
            mask = ones_where(first_all[...].astype(F32) >= entry)
            sums[group_rows(t, sent), :] = dot(twice(mask, DEPTH), hazard[...])
            return 0

        lax.fori_loop(0, cap // GROUP, total, 0)


def hazards(cap, first, risk, indicator, got):
    rows, width = risk.shape
    like = jax.ShapeDtypeStruct
    return pl.pallas_call(
        partial(hazard_kernel, cap),
        grid=(rows // TILE,),
        in_specs=[
            whole(), lanes_of(1, TILE), whole(), rows_of(TILE, width), whole()
        ],
        out_specs=[whole(), whole()],
        out_shape=[pltpu.VMEM((2 * rows, width), BF16), like((sent_rows(cap), width), F32)],
        scratch_shapes=[pltpu.VMEM((2 * cap, width), BF16)],
        compiler_params=params(20),
        name="hazards",
    )(first, first, in_vmem(risk), in_hbm(indicator), got)


def backward_kernel(
    cap, factor, half, rank_ref, exposure_ref, got, note, log_part, weight, indicator, hidden,
    slope_mid, first_hidden, slope_in, x_ref, w_in, w_mid, w_out, grad_x, keep, send,
    parts, grad_in, grad_mid, grad_out,
):
    step = pl.program_id(0)
    tile = rank_ref.shape[1]
    own = pl.ds(pl.multiple_of(step * tile, tile), tile)

    @pl.when(step == 0)
    def _():
        split_sum(got, parts, cap)
        grad_in[...] = jnp.zeros_like(grad_in)
        grad_mid[...] = jnp.zeros_like(grad_mid)
        grad_out[...] = jnp.zeros_like(grad_out)

    rank = widen(as_column(rank_ref[...]), GROUP)

    def behind(t, total):
        return total + group_sum(ones_where(rank == iota((tile, GROUP), 1) + t * GROUP), parts, t)

    exposure = lax.fori_loop(0, cap // GROUP, behind, exposure_ref[own, :])
    top = weight[pl.ds(pl.multiple_of(step * 2 * tile, tile), tile), :].astype(F32)
    rest = weight[pl.ds(pl.multiple_of(step * 2 * tile + tile, tile), tile), :].astype(F32)
    eta = ((top + rest) * exposure - indicator[own, :].astype(F32)).astype(BF16)
    grad_out[...] += dot(hidden[own, :], eta, 0, 0)
    mid = (dot(eta, w_out[...], 1, 1) * slope_mid[own, :]).astype(BF16)
    grad_mid[...] += dot(first_hidden[own, :], mid, 0, 0)
    pre = (dot(mid, w_mid[...], 1, 1) * slope_in[own, :]).astype(BF16)
    grad_in[...] += dot(x_ref[own, :], pre, 0, 0)
    grad_x[...] = dot(pre, w_in[...], 1, 1).astype(BF16)

    @pl.when(step == pl.num_programs(0) - 1)
    def _():
        body, rest = grad_mid.shape[0], grad_out.shape[0] // 2
        end = body + rest

        def write(out, block, at):
            out[0:body, :] = block[...] * factor
            out[body:end, :] = grad_out[at : at + rest, :] * factor
            out[end:, :] = note[...] + log_part[...]

        @pl.when(half[0] == 0)
        def _():
            write(keep, grad_mid, 0)
            write(send, grad_in, rest)

        @pl.when(half[0] != 0)
        def _():
            write(keep, grad_in, rest)
            write(send, grad_mid, 0)


def backward(cap, factor, half, rank, exposure, got, notes, kept, features, w_in, w_mid, w_out):
    rows, width = features.shape
    out_width = exposure.shape[1]
    halves = (w_mid.shape[0] + w_out.shape[0] // 2 + 8, out_width)
    tiles = [in_vmem(a) for a in (*kept, features)]
    weights = (w_in, w_mid, w_out)
    return pl.pallas_call(
        partial(backward_kernel, cap, factor),
        grid=(rows // TILE,),
        in_specs=[pl.BlockSpec(memory_space=pltpu.SMEM), lanes_of(1, TILE)]
        + [whole()] * (2 + len(notes))
        + [whole()] * (len(tiles) + 3),
        out_specs=[rows_of(TILE, width), whole(), whole()],
        out_shape=[
            pltpu.HBM((rows, width), BF16), pltpu.HBM(halves, F32),
            jax.ShapeDtypeStruct(halves, F32),
        ],
        scratch_shapes=[pltpu.VMEM((2 * cap, out_width), BF16)]
        + [pltpu.VMEM(w.shape, F32) for w in weights],
        compiler_params=params(20),
        name="backward",
    )(half, rank, in_vmem(exposure), got, *notes, *tiles, *weights)


def in_steps(rows, work):
    step = 16 if rows % 16 == 0 else 8
    if rows <= step:
        work(0, rows)
        return

    def body(k, _):
        work(pl.multiple_of(k * step, 8), step)
        return 0

    lax.fori_loop(0, rows // step, body, 0, unroll=2)


def spread_kernel(sizes, streams, me, *refs):
    count = sum(sizes)
    outs = iter(refs[count:])
    groups_of = []
    for size in sizes:
        groups_of.append(refs[:size])
        refs = refs[size:]

    def total(which, rows):
        value = groups_of[which][0][rows, :]
        for ref in groups_of[which][1:]:
            value = value + ref[rows, :]
        return value

    for i, (which, at, rows, tail_at, tail, groups) in enumerate(streams):
        if not groups:
            flag = jnp.max(total(which, pl.ds(at, rows)))
            next(outs)[0] = jnp.where(flag > 0.0, 1, 0).astype(I32)
            continue
        piece = rows // groups
        for m in range(groups):
            out = next(outs)
            begin = at
            if groups > 1:
                begin = pl.multiple_of(at + jnp.bitwise_xor(me[i], m) * piece, 8)

            def work(row, step, out=out, begin=begin):
                source = pl.ds(pl.multiple_of(begin + row, 8), step)
                out[pl.ds(row, step), :] = total(which, source)

            in_steps(piece, work)
            if tail:
                out[piece : piece + tail, :] = total(which, pl.ds(tail_at, tail))


def spread(terms, streams, me, name):
    width = terms[0][0].shape[1]
    shapes, places = [], []
    for _, _, rows, _, tail, groups in streams:
        if groups:
            shapes += [pltpu.VMEM((rows // groups + tail, width), F32)] * groups
            places += [pl.BlockSpec(memory_space=pltpu.VMEM)] * groups
        else:
            shapes.append(jax.ShapeDtypeStruct((1,), I32))
            places.append(pl.BlockSpec(memory_space=pltpu.SMEM))
    flat = [a for term in terms for a in term]
    out = pl.pallas_call(
        partial(spread_kernel, [len(term) for term in terms], streams),
        in_specs=[pl.BlockSpec(memory_space=pltpu.SMEM)]
        + [pl.BlockSpec(memory_space=pltpu.VMEM)] * len(flat),
        out_specs=places,
        out_shape=shapes,
        compiler_params=params(16),
        name=name,
    )(me, *flat)
    parts = []
    for stream in streams:
        parts.append(out[: max(stream[-1], 1)])
        out = out[max(stream[-1], 1) :]
    return parts


def collect_kernel(places, me, *refs):
    count = sum(groups for groups, _, _ in places)
    outs = refs[count:]
    start = 0
    for i, (groups, which, at) in enumerate(places):
        piece = refs[start].shape[0]
        for m in range(groups):
            begin = pl.multiple_of(at + jnp.bitwise_xor(me[i], m) * piece, 8)

            def work(row, step, out=outs[which], ref=refs[start + m], begin=begin):
                target = pl.ds(pl.multiple_of(begin + row, 8), step)
                out[target, :] = ref[pl.ds(row, step), :]

            in_steps(piece, work)
        start += groups


def collect(streams, out_rows, me, name):
    flat = [a for pieces, _, _ in streams for a in pieces]
    width = flat[0].shape[1]
    return pl.pallas_call(
        partial(collect_kernel, [(len(pieces), which, at) for pieces, which, at in streams]),
        in_specs=[pl.BlockSpec(memory_space=pltpu.SMEM)]
        + [pl.BlockSpec(memory_space=pltpu.VMEM)] * len(flat),
        out_specs=[pl.BlockSpec(memory_space=pltpu.VMEM)] * len(out_rows),
        out_shape=[pltpu.VMEM((rows, width), F32) for rows in out_rows],
        compiler_params=params(16),
        name=name,
    )(me, *flat)


def plan(body, rest):
    strata, chain = lax.axis_size("strata"), lax.axis_size("chain")
    if strata % 2 or chain % 4 or strata & (strata - 1) or chain & (chain - 1):
        return None
    across = chain // 4
    plane, line = strata // 2 * across, 4
    if body % (8 * plane * line) or rest % (8 * line):
        return None
    return across, plane, line


def hop(block, strata_flip, chain_flip):
    strata, chain = lax.axis_size("strata"), lax.axis_size("chain")
    route = [
        (s * chain + c, (s ^ strata_flip) * chain + (c ^ chain_flip))
        for s in range(strata)
        for c in range(chain)
    ]
    return lax.ppermute(block, ("strata", "chain"), route)


def hops(groups):
    across, plane, line = groups
    strata, chain = lax.axis_index("strata"), lax.axis_index("chain")

    def plane_hops(pieces):
        return [pieces[0]] + [
            hop(pieces[m], m // across * 2, m % across) for m in range(1, plane)
        ]

    def line_hops(pieces):
        return [pieces[0]] + [hop(pieces[m], 0, m * across) for m in range(1, line)]

    return plane_hops, line_hops, strata // 2 * across + chain % across, chain // across


def reduced(keep, send, body, rest, groups):
    plane_hops, line_hops, in_plane, in_line = hops(groups)
    _, plane, line = groups
    end = body + rest
    tail = keep.shape[0] - end
    a, b = spread(
        [[keep, hop(send, 1, 0)]],
        [(0, 0, body, end, tail, plane), (0, body, rest, 0, 0, line)],
        jnp.stack([in_plane, in_line]), "spread_first",
    )
    a, b = plane_hops(a), line_hops(b)
    size_a, size_b = body // plane, rest // line
    none = jnp.zeros((3,), I32)
    ((b,),) = spread([b], [(0, 0, size_b, 0, 0, 1)], none, "lines_summed")
    (a,) = spread(
        [a], [(0, 0, size_a, size_a, tail, line)], in_line.reshape(1), "spread_second"
    )
    a, b = line_hops(a), plane_hops([b] * plane)
    ((b,),) = spread([b], [(0, 0, size_b, 0, 0, 1)], none, "rest_summed")
    size_a = size_a // line
    (a,), (note,), (flag,) = spread(
        [a],
        [(0, 0, size_a, 0, 0, 1), (0, size_a, tail, 0, 0, 1), (0, size_a + 1, 1, 0, 0, 0)],
        none, "body_summed",
    )
    (a,) = collect(
        [(line_hops([a] * line), 0, 0)], [body // plane], in_line.reshape(1), "collect_first"
    )
    return flag, note, a, b


def gathered(a, b, body, rest, groups):
    plane_hops, line_hops, in_plane, in_line = hops(groups)
    _, plane, line = groups
    a, b = plane_hops([a] * plane), line_hops([b] * line)
    (own,) = collect(
        [(a, 0, 0), (b, 0, body)], [body + rest], jnp.stack([in_plane, in_line]), "collect_second"
    )
    return own, hop(own, 1, 0)


def place_kernel(of_core, half, block, *refs):
    grad_in, grad_mid, grad_out, sems = refs[-4:]
    body, rest = grad_mid.shape[0], grad_out.shape[0] // 2

    def write(target, at):
        copies = [
            pltpu.make_async_copy(block.at[pl.ds(0, body)], target, sems.at[0]),
            pltpu.make_async_copy(
                block.at[pl.ds(body, rest)], grad_out.at[pl.ds(at, rest)], sems.at[1]
            ),
        ]
        for copy in copies:
            copy.start()
        for copy in copies:
            copy.wait()

    @pl.when(half[0] == of_core)
    def _():
        write(grad_mid, 0)

    @pl.when(half[0] != of_core)
    def _():
        write(grad_in, rest)


def place(of_core, half, block, shapes, results):
    somewhere = pl.BlockSpec(memory_space=pl.ANY)
    return pl.pallas_call(
        partial(place_kernel, of_core),
        in_specs=[
            pl.BlockSpec(memory_space=pltpu.SMEM), pl.BlockSpec(memory_space=pltpu.VMEM)
        ]
        + [somewhere] * len(results),
        out_specs=[somewhere] * 3,
        out_shape=[pltpu.HBM(shape, F32) for shape in shapes],
        scratch_shapes=[pltpu.SemaphoreType.DMA((2,))],
        input_output_aliases={2 + i: i for i in range(len(results))},
        compiler_params=params(16),
        name="place",
    )(half, block, *results)


def finish(half, own, got, shapes):
    results = place(0, half, own, shapes, ())
    return place(1, half, got, shapes, results)


def from_behind(block, axis, distance):
    devices = range(lax.axis_size(axis))
    route = [(i - distance, i) for i in devices if i - distance in devices]
    return lax.ppermute(block, axis, route)


def pipeline(cap, total_rows, half, features, events, first, entry, w_in, w_mid, w_out):
    rows = features.shape[0]
    first_row = first.reshape(1, rows)
    entry_row = entry.reshape(1, rows)
    starts = first[::TILE]
    (
        first_hidden, hidden, slope_in, slope_mid, indicator, weight, send, note, rank,
    ) = trunk(cap, entry_row, features, events, w_in, w_mid, w_out)
    got = from_behind(send, "chain", -1)
    risk = own_risk(starts, entry, first_row, weight)
    hazard, sums = hazards(cap, first_row, risk, indicator, got)
    got_sums = from_behind(sums, "chain", 1)
    exposure, log_part = own_exposure(starts, first, entry_row, hazard)
    kept = (weight, indicator, hidden, slope_mid, first_hidden, slope_in)
    return backward(
        cap, total_rows ** (-0.5), half, rank, exposure, got_sums, (note, log_part), kept,
        features, w_in, w_mid, w_out,
    )


def on_device(features, events, tie_first, entry_row, w_in, w_mid, w_out):
    rows = features.shape[0]
    total_rows = rows * lax.axis_size("chain") * lax.axis_size("strata")
    block_start = lax.axis_index("chain") * rows
    first = tie_first - block_start
    entry = entry_row - block_start
    args = (features, events, first, entry, w_in, w_mid, w_out)
    shapes = (w_in.shape, w_mid.shape, w_out.shape)
    body, rest = w_mid.shape[0], w_out.shape[0] // 2
    end = body + rest
    groups = plan(body, rest)
    half = jnp.zeros((1,), I32)
    if groups:
        half = half + lax.axis_index("strata") % 2

    def run(cap):
        grad_x, keep, send = pipeline(cap, total_rows, half, *args)
        if groups:
            flag, note, a, b = reduced(keep, send, body, rest, groups)
        else:
            a, b = lax.psum((keep, send[:end]), ("strata", "chain"))
            a, note = a[:end], a[end:]
            flag = (note[1, 0:1] > 0).astype(I32)
        return flag, note, grad_x, a, b

    _, note, grad_x, a, b = lax.while_loop(
        lambda state: state[0][0] > 0, lambda _: run(rows), run(min(GROUP, rows))
    )
    own, other = gathered(a, b, body, rest, groups) if groups else (a, b)
    return (note[0] / total_rows, grad_x, *finish(half, own, other, shapes))


def solution(mesh):
    placed = (
        P(("strata", "chain"), None),
        P(("strata", "chain"), None),
        P(("strata", "chain")),
        P(("strata", "chain")),
        P(),
        P(),
        P(),
    )
    return jax.shard_map(
        on_device,
        mesh=mesh,
        in_specs=placed,
        out_specs=(P(), P(("strata", "chain"), None), P(), P(), P()),
        check_vma=False,
    )
```

time: 145 us -> 131 us (0.903)
  local copies, waits for them, and re-layouts: 8.9 us -> 3.18 us
  waiting for transfers between devices: 30.6 us -> 25.5 us
  starting transfers between devices: 42.5 us -> 38.5 us
    ppermute x26 -> x23, starting transfers between devices: 36.4 us -> 32.4 us  [hop(): return lax.ppermute(block, ('strata', 'chain'), route)]
    cond x5 -> x0, local copies, waits for them, and re-layouts: 2.84 us -> none
    ppermute x2, waiting for transfers between devices: 4.14 us -> 1.38 us  [from_behind(): return lax.ppermute(block, axis, route)]
    unnamed x36, local copies, waits for them, and re-layouts: 5.44 us -> 3.06 us
    pallas_call x1, Pallas kernels: 14.2 us -> 12 us  [backward(): pl.pallas_call(partial(backward_kernel, cap, factor), grid=(rows // TILE,...]
    ppermute x26 -> x23, waiting for transfers between devices: 26.4 us -> 24.2 us  [hop(): return lax.ppermute(block, ('strata', 'chain'), route)]
    pallas_call x3 -> x5, Pallas kernels: 2.09 us -> 4.15 us  [spread(): pl.pallas_call(partial(spread_kernel, [len(term) for term in terms], stre...]
    pallas_call x1, Pallas kernels: 9.94 us -> 11.5 us  [own_risk(): pl.pallas_call(own_risk_kernel, grid=(rows // TILE,), in_specs=[pl.BlockS...]
  transfers between devices with their start and end apart: 28 -> 25, of which waited for: 12 -> 11; matrix products, arithmetic and copies ran while one was open for 1% -> 1% of each run, Pallas kernels for 15% -> 20%
where the time goes in v3:
time: 131 us
  Pallas kernels  60 us (46%)
  starting transfers between devices  38.5 us (29%)
  waiting for transfers between devices  25.5 us (19%)
  local copies, waits for them, and re-layouts  3.18 us (2%)
  other arithmetic  1.36 us (1%)
    ppermute x23, starting transfers between devices, hop(): return lax.ppermute(block, ('strata', 'chain'), route)  32.4 us
    ppermute x23, waiting for transfers between devices, hop(): return lax.ppermute(block, ('strata', 'chain'), route)  24.2 us
    pallas_call x1, Pallas kernels, trunk(): pl.pallas_call(partial(trunk_kernel, cap), grid=(rows // TILE,), in_specs...  12.6 us
    pallas_call x1, Pallas kernels, backward(): pl.pallas_call(partial(backward_kernel, cap, factor), grid=(rows // TILE,...  12 us
    pallas_call x1, Pallas kernels, own_exposure(): pl.pallas_call(own_exposure_kernel, grid=(rows // TILE,), in_specs=[pl.Bl...  11.6 us
    pallas_call x1, Pallas kernels, own_risk(): pl.pallas_call(own_risk_kernel, grid=(rows // TILE,), in_specs=[pl.BlockS...  11.5 us
    ppermute x2, starting transfers between devices, from_behind(): return lax.ppermute(block, axis, route)  6.17 us
    pallas_call x1, Pallas kernels, hazards(): pl.pallas_call(partial(hazard_kernel, cap), grid=(rows // TILE,), in_spec...  5.2 us
  transfers between devices with their start and end apart: 25, of which 11 were waited for; matrix products, arithmetic and copies ran while one was open for 1% of the time, Pallas kernels for 20%

profile of v3, /device:TPU:0, one launch (start us, length us, event | category | flops | bytes accessed | tf_op | source)
XLA Modules:
  0.0 130.8 jit_solution(9897415920644666530)
XLA Ops:
  2.9 12.6 %trunk.6 = (bf16[2048,512]{1,0:T(8,128)(2,1)}, bf16[2048,512]{1,0:T(8,128)(2,1)}, f32[2048,512]{1,0:T(8,128)}, f32[2048,512]{1,0:T(8,128)}, bf16[2048,512]{1,0:T...) custom-call(s32[1,2048]{1,0:T(1,128)S(1)} %bitcast.38, ...), custom_call_target="tpu_custom_call" | custom-call | tf_op jit(solution)/shard_map/trunk/pallas_call | solution.py:192
  15.5 1.3 collective-permute-start.18
  16.9 11.5 %own_risk.2.risk = f32[2048,512]{1,0:T(8,128)S(1)} custom-call(s32[4]{0:T(128)S(1)} %slice.9.starts, s32[4,512]{1,0:T(4,128)S(1)} %reshape.50.entry_ref, s32[1,2048]{1,0:T(1,128)S(1)} %bitcast.32, bf16[4096,512]{1,0:T(8,128)(2,1)} %get-tuple-element.284.weight), custom_call_target="tpu_custom_call" | custom-call | flops 8589934592 | bytes 33554432 | tf_op jit(solution)/shard_map/own_risk/pallas_call | solution.py:241
  28.4 1.4 %collective-permute-done.18.got = f32[200,512]{1,0:T(8,128)S(1)} collective-permute-done((f32[200,512]{1,0:T(8,128)S(1)}, f32[200,512]{1,0:T(8,128)S(1)}, u32[]{:S(2)}, u32[]{:S(2)}) %collective-permute-start.18) | collective-permute-done | bytes 409632 | tf_op jit(solution)/shard_map/ppermute | solution.py:681
  29.8 5.2 %hazards.6 = (bf16[4096,512]{1,0:T(8,128)(2,1)S(1)}, f32[192,512]{1,0:T(8,128)S(1)}) custom-call(s32[1,2048]{1,0:T(1,128)S(1)} %bitcast.33, s32[1,2048]{1,0:T(1,128)S(1)} %bitcast.34, f32[2048,512]{1,0:T(8,128)S(1)} %own_risk.2.risk, bf16[2048,512]{1,0:T(8,128)(2,1)} %get-tuple-element.285.indicator_ref.indicator, f32[200,512]{1,0:T(8,128)S(1)} %collective-permute-done.18.got), custom_call_target="tpu_custom_call" | custom-call | tf_op jit(solution)/shard_map/hazards/pallas_call | solution.py:357
  35.0 4.9 %collective-permute-start.19 = (f32[192,512]{1,0:T(8,128)S(1)}, f32[192,512]{1,0:T(8,128)S(1)}, u32[]{:S(2)}, u32[]{:S(2)}) collective-permute-start(f32[192,512]{1,0:T(8,128)S(1)} %get-tuple-element.289), channel_id=1, source_target_pairs={{0,1},{1,2},{2,3},{3,4},{4,5},{5,6},{6,7},{8,9},{9,10},{10,11},{11... | collective-permute-start | bytes 1179656 | tf_op jit(solution)/shard_map/ppermute | solution.py:681
  40.0 11.6 %own_exposure.6 = (f32[2048,512]{1,0:T(8,128)S(1)}, f32[8,512]{1,0:T(8,128)S(1)}) custom-call(s32[4]{0:T(128)S(1)} %slice.9.starts, s32[4,512]{1,0:T(4,128)S(1)} %reshape.48.first_ref, s32[1,2048]{1,0:T(1,128)S(1)} %bitcast.39, bf16[4096,512]{1,0:T(8,128)(2,1)S(1)} %get-tuple-element.287.hazard), custom_call_target="tpu_custom_call" | custom-call | flops 8589934592 | bytes 33554432 | tf_op jit(solution)/shard_map/own_exposure/pallas_call | solution.py:290
  51.7 12.0 %backward.6 = (bf16[2048,512]{1,0:T(8,128)(2,1)}, f32[776,512]{1,0:T(8,128)}, f32[776,512]{1,0:T(8,128)}) custom-call(s32[1]{0:T(128)} %bitcast.2.half, s32[1,2048]{1,0:T(1,128)S(1)} %get-tuple-element.283.rank_ref, f32[2048,512]{1,0:T(8,128)S(1)} %get-tuple-element.288.exposure_ref, f32[192,512]{1,0:T(8,128)S(1)} %collective-permute-done.19.got, ...), custom_call_target="tpu_custom_call" | custom-call | tf_op jit(solution)/shard_map/backward/pallas_call | solution.py:430
  63.7 3.7 %collective-permute-done.20.refs_1_ = f32[776,512]{1,0:T(8,128)} collective-permute-done((f32[776,512]{1,0:T(8,128)}, f32[776,512]{1,0:T(8,128)}, u32[]{:S(2)}, u32[]{:S(2)}) %collective-permute-start.20) | collective-permute-done | bytes 1589280 | tf_op jit(solution)/shard_map/ppermute | solution.py:572
  67.4 1.4 %copy-done.15 = f32[776,512]{1,0:T(8,128)S(1)} copy-done((f32[776,512]{1,0:T(8,128)S(1)}, f32[776,512]{1,0:T(8,128)}, u32[]{:S(2)}) %copy-start.15) | copy-done | bytes 1589272
  68.8 1.7 %spread_first.6 = (f32[136,512]{1,0:T(8,128)S(1)}, f32[136,512]{1,0:T(8,128)S(1)}, f32[136,512]{1,0:T(8,128)S(1)}, f32[136,512]{1,0:T(8,128)S(1)}, f32[64,512]{1...) custom-call(s32[2]{0:T(128)S(1)} %pad_add_fusion.1.me, ...), custom_call_target="tpu_custom_call" | custom-call | tf_op jit(solution)/shard_map/spread_first/pallas_call | solution.py:507
  70.6 3.7 %collective-permute-start.21 = (f32[136,512]{1,0:T(8,128)S(1)}, f32[136,512]{1,0:T(8,128)S(1)}, u32[]{:S(2)}, u32[]{:S(2)}) collective-permute-start(f32[136,512]{1,0:T(8,128)S(1)} %get-tuple-element.299), channel_id=1, source_target_pairs={{0,1},{1,0},{2,3},{3,2},{4,5},{5,4},{6,7},{7,6},{8,9},{9,8},{10,11... | collective-permute-start | bytes 835592 | tf_op jit(solution)/shard_map/ppermute | solution.py:572
  74.2 1.5 %collective-permute-start.23 = (f32[136,512]{1,0:T(8,128)S(1)}, f32[136,512]{1,0:T(8,128)S(1)}, u32[]{:S(2)}, u32[]{:S(2)}) collective-permute-start(f32[136,512]{1,0:T(8,128)S(1)} %get-tuple-element.301), channel_id=1, source_target_pairs={{0,17},{1,16},{2,19},{3,18},{4,21},{5,20},{6,23},{7,22},{8,25},{9,... | collective-permute-start | bytes 835592 | tf_op jit(solution)/shard_map/ppermute | solution.py:572
  76.3 2.6 %collective-permute-start.31 = (f32[64,512]{1,0:T(8,128)S(1)}, f32[64,512]{1,0:T(8,128)S(1)}, u32[]{:S(2)}, u32[]{:S(2)}) collective-permute-start(f32[64,512]{1,0:T(8,128)S(1)} %get-tuple-element.312), channel_id=1, source_target_pairs={{0,4},{1,5},{2,6},{3,7},{4,0},{5,1},{6,2},{7,3},{8,12},{9,13},{10,... | collective-permute-start | bytes 393224 | tf_op jit(solution)/shard_map/ppermute | solution.py:572
  78.9 2.8 %collective-permute-done.21.refs_1_ = f32[136,512]{1,0:T(8,128)S(1)} collective-permute-done((f32[136,512]{1,0:T(8,128)S(1)}, f32[136,512]{1,0:T(8,128)S(1)}, u32[]{:S(2)}, u32[]{:S(2)}) %collective-permute-start.21) | collective-permute-done | bytes 278560 | tf_op jit(solution)/shard_map/ppermute | solution.py:572
  81.7 2.6 %collective-permute-start.32 = (f32[64,512]{1,0:T(8,128)S(1)}, f32[64,512]{1,0:T(8,128)S(1)}, u32[]{:S(2)}, u32[]{:S(2)}) collective-permute-start(f32[64,512]{1,0:T(8,128)S(1)} %get-tuple-element.313), channel_id=1, source_target_pairs={{0,6},{1,7},{2,4},{3,5},{4,2},{5,3},{6,0},{7,1},{8,14},{9,15},{10,... | collective-permute-start | bytes 393224 | tf_op jit(solution)/shard_map/ppermute | solution.py:572
  84.3 4.3 %collective-permute-done.22.refs_2_ = f32[136,512]{1,0:T(8,128)S(1)} collective-permute-done((f32[136,512]{1,0:T(8,128)S(1)}, f32[136,512]{1,0:T(8,128)S(1)}, u32[]{:S(2)}, u32[]{:S(2)}) %collective-permute-start.22) | collective-permute-done | bytes 278560 | tf_op jit(solution)/shard_map/ppermute | solution.py:572
  89.5 1.7 %collective-permute-start.33 = (f32[64,512]{1,0:T(8,128)S(1)}, f32[64,512]{1,0:T(8,128)S(1)}, u32[]{:S(2)}, u32[]{:S(2)}) collective-permute-start(f32[64,512]{1,0:T(8,128)S(1)} %lines_summed.2.refs_0_), channel_id=1, source_target_pairs={{0,1},{1,0},{2,3},{3,2},{4,5},{5,4},{6,7},{7,6},{8,9},{9,8},{10,11... | collective-permute-start | bytes 393224 | tf_op jit(solution)/shard_map/ppermute | solution.py:572
  91.2 3.9 %collective-permute-start.25 = (f32[40,512]{1,0:T(8,128)S(1)}, f32[40,512]{1,0:T(8,128)S(1)}, u32[]{:S(2)}, u32[]{:S(2)}) collective-permute-start(f32[40,512]{1,0:T(8,128)S(1)} %get-tuple-element.304), channel_id=1, source_target_pairs={{0,4},{1,5},{2,6},{3,7},{4,0},{5,1},{6,2},{7,3},{8,12},{9,13},{10,... | collective-permute-start | bytes 245768 | tf_op jit(solution)/shard_map/ppermute | solution.py:572
  95.1 1.2 collective-permute-start.26
  98.3 2.1 %collective-permute-done.25.refs_2_ = f32[40,512]{1,0:T(8,128)S(1)} collective-permute-done((f32[40,512]{1,0:T(8,128)S(1)}, f32[40,512]{1,0:T(8,128)S(1)}, u32[]{:S(2)}, u32[]{:S(2)}) %collective-permute-start.25) | collective-permute-done | bytes 81952 | tf_op jit(solution)/shard_map/ppermute | solution.py:572
  101.5 1.2 body_summed.6
  102.7 1.3 %collective-permute-start.27 = (f32[32,512]{1,0:T(8,128)S(1)}, f32[32,512]{1,0:T(8,128)S(1)}, u32[]{:S(2)}, u32[]{:S(2)}) collective-permute-start(f32[32,512]{1,0:T(8,128)S(1)} %get-tuple-element.309.refs_0_), channel_id=1, source_target_pairs={{0,2},{1,3},{2,0},{3,1},{4,6},{5,7},{6,4},{7,5},{8,10},{9,11},{10,... | collective-permute-start | bytes 196616 | tf_op jit(solution)/shard_map/ppermute | solution.py:572
  104.9 2.2 %collective-permute-start.29 = (f32[32,512]{1,0:T(8,128)S(1)}, f32[32,512]{1,0:T(8,128)S(1)}, u32[]{:S(2)}, u32[]{:S(2)}) collective-permute-start(f32[32,512]{1,0:T(8,128)S(1)} %get-tuple-element.309.refs_0_), channel_id=1, source_target_pairs={{0,6},{1,7},{2,4},{3,5},{4,2},{5,3},{6,0},{7,1},{8,14},{9,15},{10,... | collective-permute-start | bytes 196616 | tf_op jit(solution)/shard_map/ppermute | solution.py:572
  107.8 2.1 %collective-permute-done.28.refs_2_ = f32[32,512]{1,0:T(8,128)S(1)} collective-permute-done((f32[32,512]{1,0:T(8,128)S(1)}, f32[32,512]{1,0:T(8,128)S(1)}, u32[]{:S(2)}, u32[]{:S(2)}) %collective-permute-start.28) | collective-permute-done | bytes 65568 | tf_op jit(solution)/shard_map/ppermute | solution.py:572
  109.9 1.2 collective-permute-done.29.refs_3_
  114.1 2.3 %collective-permute-start.38 = (f32[128,512]{1,0:T(8,128)S(1)}, f32[128,512]{1,0:T(8,128)S(1)}, u32[]{:S(2)}, u32[]{:S(2)}) collective-permute-start(f32[128,512]{1,0:T(8,128)S(1)} %get-tuple-element.842), channel_id=1, source_target_pairs={{0,17},{1,16},{2,19},{3,18},{4,21},{5,20},{6,23},{7,22},{8,25},{9,... | collective-permute-start | bytes 786440 | tf_op jit(solution)/shard_map/ppermute | solution.py:572
  116.4 1.9 %collective-permute-start.40 = (f32[64,512]{1,0:T(8,128)S(1)}, f32[64,512]{1,0:T(8,128)S(1)}, u32[]{:S(2)}, u32[]{:S(2)}) collective-permute-start(f32[64,512]{1,0:T(8,128)S(1)} %get-tuple-element.843), channel_id=1, source_target_pairs={{0,4},{1,5},{2,6},{3,7},{4,0},{5,1},{6,2},{7,3},{8,12},{9,13},{10,... | collective-permute-start | bytes 393224 | tf_op jit(solution)/shard_map/ppermute | solution.py:572
  118.3 1.7 %collective-permute-start.41 = (f32[64,512]{1,0:T(8,128)S(1)}, f32[64,512]{1,0:T(8,128)S(1)}, u32[]{:S(2)}, u32[]{:S(2)}) collective-permute-start(f32[64,512]{1,0:T(8,128)S(1)} %get-tuple-element.843), channel_id=1, source_target_pairs={{0,6},{1,7},{2,4},{3,5},{4,2},{5,3},{6,0},{7,1},{8,14},{9,15},{10,... | collective-permute-start | bytes 393224 | tf_op jit(solution)/shard_map/ppermute | solution.py:572
  120.0 3.7 %collective-permute-done.40.refs_6_ = f32[64,512]{1,0:T(8,128)S(1)} collective-permute-done((f32[64,512]{1,0:T(8,128)S(1)}, f32[64,512]{1,0:T(8,128)S(1)}, u32[]{:S(2)}, u32[]{:S(2)}) %collective-permute-start.40) | collective-permute-done | bytes 131104 | tf_op jit(solution)/shard_map/ppermute | solution.py:572
  123.7 1.4 %collective-permute-done.41.refs_7_ = f32[64,512]{1,0:T(8,128)S(1)} collective-permute-done((f32[64,512]{1,0:T(8,128)S(1)}, f32[64,512]{1,0:T(8,128)S(1)}, u32[]{:S(2)}, u32[]{:S(2)}) %collective-permute-start.41) | collective-permute-done | bytes 131104 | tf_op jit(solution)/shard_map/ppermute | solution.py:572
  127.8 1.7 %collective-permute-done.42.block = f32[768,512]{1,0:T(8,128)S(1)} collective-permute-done((f32[768,512]{1,0:T(8,128)S(1)}, f32[768,512]{1,0:T(8,128)S(1)}, u32[]{:S(2)}, u32[]{:S(2)}) %collective-permute-start.42) | collective-permute-done | bytes 1572896 | tf_op jit(solution)/shard_map/ppermute | solution.py:572
  (79 shorter events, 15.1 us)
Async XLA Ops:
  0.6 16.2 %copy-start.28 = (s32[2048]{0:T(1024)S(1)}, s32[2048]{0:T(1024)}, u32[]{:S(2)}) copy-start(s32[2048]{0:T(1024)} %param.15) | copy-start | bytes 24580
  15.5 14.3 %collective-permute-start.18 = (f32[200,512]{1,0:T(8,128)S(1)}, f32[200,512]{1,0:T(8,128)S(1)}, u32[]{:S(2)}, u32[]{:S(2)}) collective-permute-start(f32[200,512]{1,0:T(8,128)S(1)} %get-tuple-element.286), channel_id=1, source_target_pairs={{1,0},{2,1},{3,2},{4,3},{5,4},{6,5},{7,6},{9,8},{10,9},{11,10},{12... | collective-permute-start | bytes 1228808 | tf_op jit(solution)/shard_map/ppermute | solution.py:681
  35.0 16.6 %collective-permute-start.19 = (f32[192,512]{1,0:T(8,128)S(1)}, f32[192,512]{1,0:T(8,128)S(1)}, u32[]{:S(2)}, u32[]{:S(2)}) collective-permute-start(f32[192,512]{1,0:T(8,128)S(1)} %get-tuple-element.289), channel_id=1, source_target_pairs={{0,1},{1,2},{2,3},{3,4},{4,5},{5,6},{6,7},{8,9},{9,10},{10,11},{11... | collective-permute-start | bytes 1179656 | tf_op jit(solution)/shard_map/ppermute | solution.py:681
  39.9 11.7 %copy-start = (bf16[2048,512]{1,0:T(8,128)(2,1)S(1)}, bf16[2048,512]{1,0:T(8,128)(2,1)}, u32[]{:S(2)}) copy-start(bf16[2048,512]{1,0:T(8,128)(2,1)} %x_ref.3) | copy-start | bytes 6291460
  39.9 11.7 %copy-start.9 = (bf16[2048,512]{1,0:T(8,128)(2,1)S(1)}, bf16[2048,512]{1,0:T(8,128)(2,1)}, u32[]{:S(2)}) copy-start(bf16[2048,512]{1,0:T(8,128)(2,1)} %get-tuple-element.285.indicator_ref.indicator) | copy-start | bytes 6291460
  63.6 3.8 %collective-permute-start.20 = (f32[776,512]{1,0:T(8,128)}, f32[776,512]{1,0:T(8,128)}, u32[]{:S(2)}, u32[]{:S(2)}) collective-permute-start(f32[776,512]{1,0:T(8,128)} %get-tuple-element.297), channel_id=1, source_target_pairs={{0,8},{1,9},{2,10},{3,11},{4,12},{5,13},{6,14},{7,15},{8,0},{9,1},... | collective-permute-start | bytes 4767752 | tf_op jit(solution)/shard_map/ppermute | solution.py:572
  63.7 25.0 %copy-start.18 = (s32[2]{0:T(128)}, s32[2]{0:T(128)S(1)}, u32[]{:S(2)}) copy-start(s32[2]{0:T(128)S(1)} %pad_add_fusion.1.me) | copy-start | bytes 28
  70.6 40.6 %copy-start.26 = (bf16[70,512]{1,0:T(8,128)(2,1)S(1)}, bf16[70,512]{1,0:T(8,128)(2,1)}, u32[]{:S(2)}) copy-start(bf16[70,512]{1,0:T(8,128)(2,1)} %constant.140.clone..sunk.3) | copy-start | bytes 215044
  70.6 40.6 %copy-start.27 = (s32[1,512]{1,0:T(1,128)S(1)}, s32[1,512]{1,0:T(1,128)}, u32[]{:S(2)}) copy-start(s32[1,512]{1,0:T(1,128)} %constant.141.clone..sunk.3) | copy-start | bytes 6148
  70.6 11.1 %collective-permute-start.21 = (f32[136,512]{1,0:T(8,128)S(1)}, f32[136,512]{1,0:T(8,128)S(1)}, u32[]{:S(2)}, u32[]{:S(2)}) collective-permute-start(f32[136,512]{1,0:T(8,128)S(1)} %get-tuple-element.299), channel_id=1, source_target_pairs={{0,1},{1,0},{2,3},{3,2},{4,5},{5,4},{6,7},{7,6},{8,9},{9,8},{10,11... | collective-permute-start | bytes 835592 | tf_op jit(solution)/shard_map/ppermute | solution.py:572
  74.2 14.4 %collective-permute-start.22 = (f32[136,512]{1,0:T(8,128)S(1)}, f32[136,512]{1,0:T(8,128)S(1)}, u32[]{:S(2)}, u32[]{:S(2)}) collective-permute-start(f32[136,512]{1,0:T(8,128)S(1)} %get-tuple-element.300), channel_id=1, source_target_pairs={{0,16},{1,17},{2,18},{3,19},{4,20},{5,21},{6,22},{7,23},{8,24},{9,... | collective-permute-start | bytes 835592 | tf_op jit(solution)/shard_map/ppermute | solution.py:572
  74.2 14.4 %collective-permute-start.23 = (f32[136,512]{1,0:T(8,128)S(1)}, f32[136,512]{1,0:T(8,128)S(1)}, u32[]{:S(2)}, u32[]{:S(2)}) collective-permute-start(f32[136,512]{1,0:T(8,128)S(1)} %get-tuple-element.301), channel_id=1, source_target_pairs={{0,17},{1,16},{2,19},{3,18},{4,21},{5,20},{6,23},{7,22},{8,25},{9,... | collective-permute-start | bytes 835592 | tf_op jit(solution)/shard_map/ppermute | solution.py:572
  75.8 13.1 %collective-permute-start.30 = (f32[64,512]{1,0:T(8,128)S(1)}, f32[64,512]{1,0:T(8,128)S(1)}, u32[]{:S(2)}, u32[]{:S(2)}) collective-permute-start(f32[64,512]{1,0:T(8,128)S(1)} %get-tuple-element.311), channel_id=1, source_target_pairs={{0,2},{1,3},{2,0},{3,1},{4,6},{5,7},{6,4},{7,5},{8,10},{9,11},{10,... | collective-permute-start | bytes 393224 | tf_op jit(solution)/shard_map/ppermute | solution.py:572
  76.3 12.6 %collective-permute-start.31 = (f32[64,512]{1,0:T(8,128)S(1)}, f32[64,512]{1,0:T(8,128)S(1)}, u32[]{:S(2)}, u32[]{:S(2)}) collective-permute-start(f32[64,512]{1,0:T(8,128)S(1)} %get-tuple-element.312), channel_id=1, source_target_pairs={{0,4},{1,5},{2,6},{3,7},{4,0},{5,1},{6,2},{7,3},{8,12},{9,13},{10,... | collective-permute-start | bytes 393224 | tf_op jit(solution)/shard_map/ppermute | solution.py:572
  81.7 7.2 %collective-permute-start.32 = (f32[64,512]{1,0:T(8,128)S(1)}, f32[64,512]{1,0:T(8,128)S(1)}, u32[]{:S(2)}, u32[]{:S(2)}) collective-permute-start(f32[64,512]{1,0:T(8,128)S(1)} %get-tuple-element.313), channel_id=1, source_target_pairs={{0,6},{1,7},{2,4},{3,5},{4,2},{5,3},{6,0},{7,1},{8,14},{9,15},{10,... | collective-permute-start | bytes 393224 | tf_op jit(solution)/shard_map/ppermute | solution.py:572
  88.7 8.5 %collective-permute-start.24 = (f32[40,512]{1,0:T(8,128)S(1)}, f32[40,512]{1,0:T(8,128)S(1)}, u32[]{:S(2)}, u32[]{:S(2)}) collective-permute-start(f32[40,512]{1,0:T(8,128)S(1)} %get-tuple-element.303), channel_id=1, source_target_pairs={{0,2},{1,3},{2,0},{3,1},{4,6},{5,7},{6,4},{7,5},{8,10},{9,11},{10,... | collective-permute-start | bytes 245768 | tf_op jit(solution)/shard_map/ppermute | solution.py:572
  89.5 15.4 %collective-permute-start.33 = (f32[64,512]{1,0:T(8,128)S(1)}, f32[64,512]{1,0:T(8,128)S(1)}, u32[]{:S(2)}, u32[]{:S(2)}) collective-permute-start(f32[64,512]{1,0:T(8,128)S(1)} %lines_summed.2.refs_0_), channel_id=1, source_target_pairs={{0,1},{1,0},{2,3},{3,2},{4,5},{5,4},{6,7},{7,6},{8,9},{9,8},{10,11... | collective-permute-start | bytes 393224 | tf_op jit(solution)/shard_map/ppermute | solution.py:572
  91.2 9.2 %collective-permute-start.25 = (f32[40,512]{1,0:T(8,128)S(1)}, f32[40,512]{1,0:T(8,128)S(1)}, u32[]{:S(2)}, u32[]{:S(2)}) collective-permute-start(f32[40,512]{1,0:T(8,128)S(1)} %get-tuple-element.304), channel_id=1, source_target_pairs={{0,4},{1,5},{2,6},{3,7},{4,0},{5,1},{6,2},{7,3},{8,12},{9,13},{10,... | collective-permute-start | bytes 245768 | tf_op jit(solution)/shard_map/ppermute | solution.py:572
  95.1 6.3 %collective-permute-start.26 = (f32[40,512]{1,0:T(8,128)S(1)}, f32[40,512]{1,0:T(8,128)S(1)}, u32[]{:S(2)}, u32[]{:S(2)}) collective-permute-start(f32[40,512]{1,0:T(8,128)S(1)} %get-tuple-element.305), channel_id=1, source_target_pairs={{0,6},{1,7},{2,4},{3,5},{4,2},{5,3},{6,0},{7,1},{8,14},{9,15},{10,... | collective-permute-start | bytes 245768 | tf_op jit(solution)/shard_map/ppermute | solution.py:572
  96.3 10.9 %collective-permute-start.34 = (f32[64,512]{1,0:T(8,128)S(1)}, f32[64,512]{1,0:T(8,128)S(1)}, u32[]{:S(2)}, u32[]{:S(2)}) collective-permute-start(f32[64,512]{1,0:T(8,128)S(1)} %lines_summed.2.refs_0_), channel_id=1, source_target_pairs={{0,16},{1,17},{2,18},{3,19},{4,20},{5,21},{6,22},{7,23},{8,24},{9,... | collective-permute-start | bytes 393224 | tf_op jit(solution)/shard_map/ppermute | solution.py:572
  97.2 9.9 %collective-permute-start.35 = (f32[64,512]{1,0:T(8,128)S(1)}, f32[64,512]{1,0:T(8,128)S(1)}, u32[]{:S(2)}, u32[]{:S(2)}) collective-permute-start(f32[64,512]{1,0:T(8,128)S(1)} %lines_summed.2.refs_0_), channel_id=1, source_target_pairs={{0,17},{1,16},{2,19},{3,18},{4,21},{5,20},{6,23},{7,22},{8,25},{9,... | collective-permute-start | bytes 393224 | tf_op jit(solution)/shard_map/ppermute | solution.py:572
  102.7 5.1 %collective-permute-start.27 = (f32[32,512]{1,0:T(8,128)S(1)}, f32[32,512]{1,0:T(8,128)S(1)}, u32[]{:S(2)}, u32[]{:S(2)}) collective-permute-start(f32[32,512]{1,0:T(8,128)S(1)} %get-tuple-element.309.refs_0_), channel_id=1, source_target_pairs={{0,2},{1,3},{2,0},{3,1},{4,6},{5,7},{6,4},{7,5},{8,10},{9,11},{10,... | collective-permute-start | bytes 196616 | tf_op jit(solution)/shard_map/ppermute | solution.py:572
  104.0 5.9 %collective-permute-start.28 = (f32[32,512]{1,0:T(8,128)S(1)}, f32[32,512]{1,0:T(8,128)S(1)}, u32[]{:S(2)}, u32[]{:S(2)}) collective-permute-start(f32[32,512]{1,0:T(8,128)S(1)} %get-tuple-element.309.refs_0_), channel_id=1, source_target_pairs={{0,4},{1,5},{2,6},{3,7},{4,0},{5,1},{6,2},{7,3},{8,12},{9,13},{10,... | collective-permute-start | bytes 196616 | tf_op jit(solution)/shard_map/ppermute | solution.py:572
  104.9 6.2 %collective-permute-start.29 = (f32[32,512]{1,0:T(8,128)S(1)}, f32[32,512]{1,0:T(8,128)S(1)}, u32[]{:S(2)}, u32[]{:S(2)}) collective-permute-start(f32[32,512]{1,0:T(8,128)S(1)} %get-tuple-element.309.refs_0_), channel_id=1, source_target_pairs={{0,6},{1,7},{2,4},{3,5},{4,2},{5,3},{6,0},{7,1},{8,14},{9,15},{10,... | collective-permute-start | bytes 196616 | tf_op jit(solution)/shard_map/ppermute | solution.py:572
  111.1 14.0 %copy-start.19 = (s32[2]{0:T(128)S(1)}, s32[2]{0:T(128)}, u32[]{:S(2)}) copy-start(s32[2]{0:T(128)} %copy-done.18) | copy-start | bytes 28
  112.0 6.2 %collective-permute-start.39 = (f32[64,512]{1,0:T(8,128)S(1)}, f32[64,512]{1,0:T(8,128)S(1)}, u32[]{:S(2)}, u32[]{:S(2)}) collective-permute-start(f32[64,512]{1,0:T(8,128)S(1)} %get-tuple-element.843), channel_id=1, source_target_pairs={{0,2},{1,3},{2,0},{3,1},{4,6},{5,7},{6,4},{7,5},{8,10},{9,11},{10,... | collective-permute-start | bytes 393224 | tf_op jit(solution)/shard_map/ppermute | solution.py:572
  112.9 12.3 %collective-permute-start.36 = (f32[128,512]{1,0:T(8,128)S(1)}, f32[128,512]{1,0:T(8,128)S(1)}, u32[]{:S(2)}, u32[]{:S(2)}) collective-permute-start(f32[128,512]{1,0:T(8,128)S(1)} %get-tuple-element.842), channel_id=1, source_target_pairs={{0,1},{1,0},{2,3},{3,2},{4,5},{5,4},{6,7},{7,6},{8,9},{9,8},{10,11... | collective-permute-start | bytes 786440 | tf_op jit(solution)/shard_map/ppermute | solution.py:572
  113.5 11.7 %collective-permute-start.37 = (f32[128,512]{1,0:T(8,128)S(1)}, f32[128,512]{1,0:T(8,128)S(1)}, u32[]{:S(2)}, u32[]{:S(2)}) collective-permute-start(f32[128,512]{1,0:T(8,128)S(1)} %get-tuple-element.842), channel_id=1, source_target_pairs={{0,16},{1,17},{2,18},{3,19},{4,20},{5,21},{6,22},{7,23},{8,24},{9,... | collective-permute-start | bytes 786440 | tf_op jit(solution)/shard_map/ppermute | solution.py:572
  114.1 11.1 %collective-permute-start.38 = (f32[128,512]{1,0:T(8,128)S(1)}, f32[128,512]{1,0:T(8,128)S(1)}, u32[]{:S(2)}, u32[]{:S(2)}) collective-permute-start(f32[128,512]{1,0:T(8,128)S(1)} %get-tuple-element.842), channel_id=1, source_target_pairs={{0,17},{1,16},{2,19},{3,18},{4,21},{5,20},{6,23},{7,22},{8,25},{9,... | collective-permute-start | bytes 786440 | tf_op jit(solution)/shard_map/ppermute | solution.py:572
  116.4 7.4 %collective-permute-start.40 = (f32[64,512]{1,0:T(8,128)S(1)}, f32[64,512]{1,0:T(8,128)S(1)}, u32[]{:S(2)}, u32[]{:S(2)}) collective-permute-start(f32[64,512]{1,0:T(8,128)S(1)} %get-tuple-element.843), channel_id=1, source_target_pairs={{0,4},{1,5},{2,6},{3,7},{4,0},{5,1},{6,2},{7,3},{8,12},{9,13},{10,... | collective-permute-start | bytes 393224 | tf_op jit(solution)/shard_map/ppermute | solution.py:572
  118.3 6.9 %collective-permute-start.41 = (f32[64,512]{1,0:T(8,128)S(1)}, f32[64,512]{1,0:T(8,128)S(1)}, u32[]{:S(2)}, u32[]{:S(2)}) collective-permute-start(f32[64,512]{1,0:T(8,128)S(1)} %get-tuple-element.843), channel_id=1, source_target_pairs={{0,6},{1,7},{2,4},{3,5},{4,2},{5,3},{6,0},{7,1},{8,14},{9,15},{10,... | collective-permute-start | bytes 393224 | tf_op jit(solution)/shard_map/ppermute | solution.py:572
  125.9 3.5 %collective-permute-start.42 = (f32[768,512]{1,0:T(8,128)S(1)}, f32[768,512]{1,0:T(8,128)S(1)}, u32[]{:S(2)}, u32[]{:S(2)}) collective-permute-start(f32[768,512]{1,0:T(8,128)S(1)} %collect_second.1.block), channel_id=1, source_target_pairs={{0,8},{1,9},{2,10},{3,11},{4,12},{5,13},{6,14},{7,15},{8,0},{9,1},... | collective-permute-start | bytes 4718600 | tf_op jit(solution)/shard_map/ppermute | solution.py:572
  (11 other events, 96.4 us)

commit v4 on v3

--- a/solution.py
+++ b/solution.py
@@ -97,10 +97,10 @@
     return pltpu.CompilerParams(vmem_limit_bytes=mib * MIB)
 
 
-def rank_entries(entry_ref, rank_ref, note, cap):
-    rows = entry_ref.shape[1]
+def rank_entries(entry, rank_ref, note, cap):
+    rows = entry.shape[1]
     high = rows // LANES
-    place = entry_ref[...] + rows
+    place = entry + rows
     crosses = place < rows
     high_hit = ones_where((iota((high, rows), 0) == (place >> 7)) & crosses)
     low_hit = jnp.where((iota((LANES, rows), 0) == (place & (LANES - 1))) & crosses, 1.0, 0.0)
@@ -121,7 +121,7 @@
 
 
 def trunk_kernel(
-    cap, entry_ref, x_ref, events_ref, byte_ref, shift_ref, w_in, w_mid, w_out,
+    cap, block_start, entry_ref, x_ref, events_ref, byte_ref, shift_ref, w_in, w_mid, w_out,
     first_hidden, hidden, slope_in, slope_mid, indicator_out, weight, send, note,
     rank_ref,
 ):
@@ -130,7 +130,7 @@
 
     @pl.when(step == 0)
     def _():
-        rank_entries(entry_ref, rank_ref, note, cap)
+        rank_entries(entry_ref[...] - block_start[0], rank_ref, note, cap)
         send[...] = jnp.zeros_like(send)
 
     events = events_ref[...]
@@ -157,7 +157,7 @@
     sent = sent_rows(cap)
     own = pl.ds(pl.multiple_of(step * tile, tile), tile)
     rank = rank_ref[:, own]
-    entry = (entry_ref[:, own] + rank_ref.shape[1]).astype(F32)
+    entry = (entry_ref[:, own] - block_start[0] + rank_ref.shape[1]).astype(F32)
 
     def total(t, _):
         hit = iota((GROUP, tile), 0) + t * GROUP == rank
@@ -176,7 +176,7 @@
     lax.fori_loop(0, cap // GROUP, total, 0)
 
 
-def trunk(cap, entry, features, events, w_in, w_mid, w_out):
+def trunk(cap, block_start, entry, features, events, w_in, w_mid, w_out):
     rows, width = features.shape
     mid = w_in.shape[1]
     wide = w_mid.shape[1]
@@ -188,13 +188,16 @@
     byte = jnp.asarray(np.concatenate([owner * (bit < 8), owner * (bit >= 8)]), BF16)
     shift = jnp.asarray((bit % 8)[None, :], I32)
     sent = sent_rows(cap) + -(-(cap // GROUP) // 8) * 8
+    constant = (byte, shift, w_in, w_mid, w_out)
     like = jax.ShapeDtypeStruct
     return pl.pallas_call(
         partial(trunk_kernel, cap),
         grid=(rows // TILE,),
-        in_specs=[whole(), rows_of(TILE, width), lanes_of(words, TILE)]
-        + [whole()] * 2
-        + [fixed(w.shape) for w in (w_in, w_mid, w_out)],
+        in_specs=[
+            pl.BlockSpec(memory_space=pltpu.SMEM), fixed((1, rows)), rows_of(TILE, width),
+            lanes_of(words, TILE),
+        ]
+        + [fixed(a.shape) for a in constant],
         out_specs=[
             rows_of(TILE, mid), rows_of(TILE, wide), rows_of(TILE, mid), rows_of(TILE, wide),
             rows_of(TILE, out_width), rows_of(2 * TILE, out_width),
@@ -209,7 +212,7 @@
         ],
         compiler_params=params(28),
         name="trunk",
-    )(entry, in_hbm(features), in_hbm(events.T), byte, shift, *map(in_hbm, (w_in, w_mid, w_out)))
+    )(block_start, *map(in_hbm, (entry, features, events.T, *constant)))
 
 
 def own_risk_kernel(starts, entry_ref, first_ref, weight, out):
@@ -264,24 +267,27 @@
     entry = widen(as_column(entry_ref[...]), DEPTH)
     row = iota((tile, DEPTH), 0) + step * tile
     own = pl.ds(pl.multiple_of(step * tile, tile), tile)
-    out[own, :] = jnp.zeros((tile, out.shape[1]), F32)
     last = step * tile + tile - 1
     parts = jnp.int32(0)
     for k in range(first_ref.shape[0]):
         parts += jnp.where(starts[k * (DEPTH // TILE)] <= last, 1, 0).astype(I32)
 
-    def part(k, _):
+    def part(k):
         first = first_ref[pl.ds(k, 1), :]
         mask = ones_where((first >= entry) & (first <= row))
         both = pl.ds(pl.multiple_of(k * 2 * DEPTH, 2 * DEPTH), 2 * DEPTH)
-        out[own, :] += dot(twice(mask, DEPTH), hazard[both, :])
+        return dot(twice(mask, DEPTH), hazard[both, :])
+
+    def others(i, _):
+        out[own, :] += part(i + jnp.where(i >= step, 1, 0).astype(I32))
         return 0
 
-    lax.fori_loop(0, parts, part, 0)
+    out[own, :] = part(step)
     top = hazard[pl.ds(pl.multiple_of(step * 2 * tile, tile), tile), :].astype(F32)
     rest = hazard[pl.ds(pl.multiple_of(step * 2 * tile + tile, tile), tile), :].astype(F32)
     logs = jnp.where(top > 0.0, jnp.log(top + rest), 0.0)
     note[0:1, :] -= jnp.sum(logs, axis=0, keepdims=True)
+    lax.fori_loop(0, parts - 1, others, 0)
 
 
 def own_exposure(starts, first, entry, hazard):
@@ -458,9 +464,19 @@
     lax.fori_loop(0, rows // step, body, 0, unroll=2)
 
 
-def spread_kernel(sizes, streams, me, *refs):
+def spread_kernel(sizes, streams, fetch, me, *refs):
     count = sum(sizes)
     outs = iter(refs[count:])
+    if fetch:
+        held, sems = refs[-1 - count : -1], refs[-1]
+        copies = [
+            pltpu.make_async_copy(refs[i], held[i], sems.at[i]) for i in range(count)
+        ]
+        for copy in copies:
+            copy.start()
+        for copy in copies:
+            copy.wait()
+        refs = held
     groups_of = []
     for size in sizes:
         groups_of.append(refs[:size])
@@ -493,7 +509,7 @@
                 out[piece : piece + tail, :] = total(which, pl.ds(tail_at, tail))
 
 
-def spread(terms, streams, me, name):
+def spread(terms, streams, me, name, fetch=False):
     width = terms[0][0].shape[1]
     shapes, places = [], []
     for _, _, rows, _, tail, groups in streams:
@@ -504,12 +520,14 @@
             shapes.append(jax.ShapeDtypeStruct((1,), I32))
             places.append(pl.BlockSpec(memory_space=pltpu.SMEM))
     flat = [a for term in terms for a in term]
+    scratch = [pltpu.VMEM(a.shape, F32) for a in flat] + [pltpu.SemaphoreType.DMA((len(flat),))]
     out = pl.pallas_call(
-        partial(spread_kernel, [len(term) for term in terms], streams),
+        partial(spread_kernel, [len(term) for term in terms], streams, fetch),
         in_specs=[pl.BlockSpec(memory_space=pltpu.SMEM)]
-        + [pl.BlockSpec(memory_space=pltpu.VMEM)] * len(flat),
+        + [pl.BlockSpec(memory_space=pl.ANY if fetch else pltpu.VMEM)] * len(flat),
         out_specs=places,
         out_shape=shapes,
+        scratch_shapes=scratch if fetch else [],
         compiler_params=params(16),
         name=name,
     )(me, *flat)
@@ -593,9 +611,9 @@
     end = body + rest
     tail = keep.shape[0] - end
     a, b = spread(
-        [[keep, hop(send, 1, 0)]],
+        [[in_hbm(keep), hop(send, 1, 0)]],
         [(0, 0, body, end, tail, plane), (0, body, rest, 0, 0, line)],
-        jnp.stack([in_plane, in_line]), "spread_first",
+        jnp.stack([in_plane, in_line]), "spread_first", fetch=True,
     )
     a, b = plane_hops(a), line_hops(b)
     size_a, size_b = body // plane, rest // line
@@ -681,19 +699,24 @@
     return lax.ppermute(block, axis, route)
 
 
-def pipeline(cap, total_rows, half, features, events, first, entry, w_in, w_mid, w_out):
+def pipeline(cap, total_rows, half, features, events, tie_first, entry_row, w_in, w_mid, w_out):
     rows = features.shape[0]
-    first_row = first.reshape(1, rows)
-    entry_row = entry.reshape(1, rows)
+    block_start = (lax.axis_index("chain") * rows).reshape(1)
+    first = tie_first - block_start
+    entry = entry_row - block_start
+    first_line = first.reshape(1, rows)
+    entry_line = entry.reshape(1, rows)
     starts = first[::TILE]
     (
         first_hidden, hidden, slope_in, slope_mid, indicator, weight, send, note, rank,
-    ) = trunk(cap, entry_row, features, events, w_in, w_mid, w_out)
+    ) = trunk(
+        cap, block_start, entry_row.reshape(1, rows), features, events, w_in, w_mid, w_out
+    )
     got = from_behind(send, "chain", -1)
-    risk = own_risk(starts, entry, first_row, weight)
-    hazard, sums = hazards(cap, first_row, risk, indicator, got)
+    risk = own_risk(starts, entry, first_line, weight)
+    hazard, sums = hazards(cap, first_line, risk, indicator, got)
     got_sums = from_behind(sums, "chain", 1)
-    exposure, log_part = own_exposure(starts, first, entry_row, hazard)
+    exposure, log_part = own_exposure(starts, first, entry_line, hazard)
     kept = (weight, indicator, hidden, slope_mid, first_hidden, slope_in)
     return backward(
         cap, total_rows ** (-0.5), half, rank, exposure, got_sums, (note, log_part), kept,
@@ -704,10 +727,7 @@
 def on_device(features, events, tie_first, entry_row, w_in, w_mid, w_out):
     rows = features.shape[0]
     total_rows = rows * lax.axis_size("chain") * lax.axis_size("strata")
-    block_start = lax.axis_index("chain") * rows
-    first = tie_first - block_start
-    entry = entry_row - block_start
-    args = (features, events, first, entry, w_in, w_mid, w_out)
+    args = (features, events, tie_first, entry_row, w_in, w_mid, w_out)
     shapes = (w_in.shape, w_mid.shape, w_out.shape)
     body, rest = w_mid.shape[0], w_out.shape[0] // 2
     end = body + rest

time: 131 us -> 128 us (0.977)
  local copies, waits for them, and re-layouts: 3.18 us -> 0.18 us
  Pallas kernels: 60 us -> 57.7 us
  waiting for transfers between devices: 25.5 us -> 27.6 us
    unnamed x36 -> x28, local copies, waits for them, and re-layouts: 3.06 us -> 0.07 us
    pallas_call x1, Pallas kernels: 11.6 us -> 9.57 us  [own_exposure(): pl.pallas_call(own_exposure_kernel, grid=(rows // TILE,), in_specs=[pl.Bl...]
    pallas_call x1, Pallas kernels: 11.5 us -> 10.1 us  [own_risk(): pl.pallas_call(own_risk_kernel, grid=(rows // TILE,), in_specs=[pl.BlockS...]
    ppermute x2, waiting for transfers between devices: 1.38 us -> 2.77 us  [from_behind(): return lax.ppermute(block, axis, route)]
  transfers between devices with their start and end apart: 25 -> 25, of which waited for: 11 -> 11; matrix products, arithmetic and copies ran while one was open for 1% -> 1% of each run, Pallas kernels for 20% -> 18%
where the time goes in v4:
time: 128 us
  Pallas kernels  57.7 us (45%)
  starting transfers between devices  39.4 us (31%)
  waiting for transfers between devices  27.6 us (22%)
    ppermute x23, starting transfers between devices, hop(): return lax.ppermute(block, ('strata', 'chain'), route)  33.2 us
    ppermute x23, waiting for transfers between devices, hop(): return lax.ppermute(block, ('strata', 'chain'), route)  24.9 us
    pallas_call x1, Pallas kernels, trunk(): pl.pallas_call(partial(trunk_kernel, cap), grid=(rows // TILE,), in_specs...  12.7 us
    pallas_call x1, Pallas kernels, backward(): pl.pallas_call(partial(backward_kernel, cap, factor), grid=(rows // TILE,...  12 us
    pallas_call x1, Pallas kernels, own_risk(): pl.pallas_call(own_risk_kernel, grid=(rows // TILE,), in_specs=[pl.BlockS...  10.1 us
    pallas_call x1, Pallas kernels, own_exposure(): pl.pallas_call(own_exposure_kernel, grid=(rows // TILE,), in_specs=[pl.Bl...  9.57 us
    ppermute x2, starting transfers between devices, from_behind(): return lax.ppermute(block, axis, route)  6.17 us
    pallas_call x1, Pallas kernels, hazards(): pl.pallas_call(partial(hazard_kernel, cap), grid=(rows // TILE,), in_spec...  5.2 us
  transfers between devices with their start and end apart: 25, of which 11 were waited for; matrix products, arithmetic and copies ran while one was open for 1% of the time, Pallas kernels for 18%

profile of v4, /device:TPU:0, one launch (start us, length us, event | category | flops | bytes accessed | tf_op | source)
XLA Modules:
  0.0 127.7 jit_solution(5331039486209876910)
XLA Ops:
  0.7 12.7 %trunk.6 = (bf16[2048,512]{1,0:T(8,128)(2,1)}, bf16[2048,512]{1,0:T(8,128)(2,1)}, f32[2048,512]{1,0:T(8,128)}, f32[2048,512]{1,0:T(8,128)}, bf16[2048,512]{1,0:T...) custom-call(s32[1]{0:T(128)} %bitcast.3.block_start, ...), custom_call_target="tpu_custom_call" | custom-call | tf_op jit(solution)/shard_map/trunk/pallas_call | solution.py:193
  13.3 1.3 %collective-permute-start.18 = (f32[200,512]{1,0:T(8,128)S(1)}, f32[200,512]{1,0:T(8,128)S(1)}, u32[]{:S(2)}, u32[]{:S(2)}) collective-permute-start(f32[200,512]{1,0:T(8,128)S(1)} %get-tuple-element.286), channel_id=1, source_target_pairs={{1,0},{2,1},{3,2},{4,3},{5,4},{6,5},{7,6},{9,8},{10,9},{11,10},{12... | collective-permute-start | bytes 1228808 | tf_op jit(solution)/shard_map/ppermute | solution.py:699
  14.8 10.1 %own_risk.2.risk = f32[2048,512]{1,0:T(8,128)S(1)} custom-call(s32[4]{0:T(128)S(1)} %slice.9.starts, s32[4,512]{1,0:T(4,128)S(1)} %reshape.96.entry_ref, s32[1,2048]{1,0:T(1,128)S(1)} %bitcast.32, bf16[4096,512]{1,0:T(8,128)(2,1)} %get-tuple-element.284.weight), custom_call_target="tpu_custom_call" | custom-call | flops 8589934592 | bytes 33554432 | tf_op jit(solution)/shard_map/own_risk/pallas_call | solution.py:244
  24.8 2.8 %collective-permute-done.18.got = f32[200,512]{1,0:T(8,128)S(1)} collective-permute-done((f32[200,512]{1,0:T(8,128)S(1)}, f32[200,512]{1,0:T(8,128)S(1)}, u32[]{:S(2)}, u32[]{:S(2)}) %collective-permute-start.18) | collective-permute-done | bytes 409632 | tf_op jit(solution)/shard_map/ppermute | solution.py:699
  27.6 5.2 %hazards.6 = (bf16[4096,512]{1,0:T(8,128)(2,1)S(1)}, f32[192,512]{1,0:T(8,128)S(1)}) custom-call(s32[1,2048]{1,0:T(1,128)S(1)} %bitcast.33, s32[1,2048]{1,0:T(1,128)S(1)} %bitcast.34, f32[2048,512]{1,0:T(8,128)S(1)} %own_risk.2.risk, bf16[2048,512]{1,0:T(8,128)(2,1)} %get-tuple-element.285.indicator_ref.indicator, f32[200,512]{1,0:T(8,128)S(1)} %collective-permute-done.18.got), custom_call_target="tpu_custom_call" | custom-call | tf_op jit(solution)/shard_map/hazards/pallas_call | solution.py:363
  32.8 4.9 %collective-permute-start.19 = (f32[192,512]{1,0:T(8,128)S(1)}, f32[192,512]{1,0:T(8,128)S(1)}, u32[]{:S(2)}, u32[]{:S(2)}) collective-permute-start(f32[192,512]{1,0:T(8,128)S(1)} %get-tuple-element.289), channel_id=1, source_target_pairs={{0,1},{1,2},{2,3},{3,4},{4,5},{5,6},{6,7},{8,9},{9,10},{10,11},{11... | collective-permute-start | bytes 1179656 | tf_op jit(solution)/shard_map/ppermute | solution.py:699
  37.8 9.6 %own_exposure.6 = (f32[2048,512]{1,0:T(8,128)S(1)}, f32[8,512]{1,0:T(8,128)S(1)}) custom-call(s32[4]{0:T(128)S(1)} %slice.9.starts, s32[4,512]{1,0:T(4,128)S(1)} %reshape.93.first_ref, s32[1,2048]{1,0:T(1,128)S(1)} %bitcast.35, bf16[4096,512]{1,0:T(8,128)(2,1)S(1)} %get-tuple-element.287.hazard), custom_call_target="tpu_custom_call" | custom-call | flops 8589934592 | bytes 33554432 | tf_op jit(solution)/shard_map/own_exposure/pallas_call | solution.py:296
  47.5 12.0 %backward.6 = (bf16[2048,512]{1,0:T(8,128)(2,1)}, f32[776,512]{1,0:T(8,128)}, f32[776,512]{1,0:T(8,128)}) custom-call(s32[1]{0:T(128)} %bitcast.2.half, s32[1,2048]{1,0:T(1,128)S(1)} %get-tuple-element.283.rank_ref, f32[2048,512]{1,0:T(8,128)S(1)} %get-tuple-element.288.exposure_ref, f32[192,512]{1,0:T(8,128)S(1)} %collective-permute-done.19.got, ...), custom_call_target="tpu_custom_call" | custom-call | tf_op jit(solution)/shard_map/backward/pallas_call | solution.py:436
  60.6 3.3 %collective-permute-done.20.refs_1_ = f32[776,512]{1,0:T(8,128)} collective-permute-done((f32[776,512]{1,0:T(8,128)}, f32[776,512]{1,0:T(8,128)}, u32[]{:S(2)}, u32[]{:S(2)}) %collective-permute-start.20) | collective-permute-done | bytes 1589280 | tf_op jit(solution)/shard_map/ppermute | solution.py:590
  63.9 2.7 %spread_first.6 = (f32[136,512]{1,0:T(8,128)S(1)}, f32[136,512]{1,0:T(8,128)S(1)}, f32[136,512]{1,0:T(8,128)S(1)}, f32[136,512]{1,0:T(8,128)S(1)}, f32[64,512]{1...) custom-call(s32[2]{0:T(128)S(1)} %pad_add_fusion.1.me, ...), custom_call_target="tpu_custom_call" | custom-call | tf_op jit(solution)/shard_map/spread_first/pallas_call | solution.py:524
  66.7 4.5 %collective-permute-start.21 = (f32[136,512]{1,0:T(8,128)S(1)}, f32[136,512]{1,0:T(8,128)S(1)}, u32[]{:S(2)}, u32[]{:S(2)}) collective-permute-start(f32[136,512]{1,0:T(8,128)S(1)} %get-tuple-element.299), channel_id=1, source_target_pairs={{0,1},{1,0},{2,3},{3,2},{4,5},{5,4},{6,7},{7,6},{8,9},{9,8},{10,11... | collective-permute-start | bytes 835592 | tf_op jit(solution)/shard_map/ppermute | solution.py:590
  71.1 1.5 %collective-permute-start.23 = (f32[136,512]{1,0:T(8,128)S(1)}, f32[136,512]{1,0:T(8,128)S(1)}, u32[]{:S(2)}, u32[]{:S(2)}) collective-permute-start(f32[136,512]{1,0:T(8,128)S(1)} %get-tuple-element.301), channel_id=1, source_target_pairs={{0,17},{1,16},{2,19},{3,18},{4,21},{5,20},{6,23},{7,22},{8,25},{9,... | collective-permute-start | bytes 835592 | tf_op jit(solution)/shard_map/ppermute | solution.py:590
  73.8 1.5 %collective-permute-start.31 = (f32[64,512]{1,0:T(8,128)S(1)}, f32[64,512]{1,0:T(8,128)S(1)}, u32[]{:S(2)}, u32[]{:S(2)}) collective-permute-start(f32[64,512]{1,0:T(8,128)S(1)} %get-tuple-element.312), channel_id=1, source_target_pairs={{0,4},{1,5},{2,6},{3,7},{4,0},{5,1},{6,2},{7,3},{8,12},{9,13},{10,... | collective-permute-start | bytes 393224 | tf_op jit(solution)/shard_map/ppermute | solution.py:590
  75.3 3.3 %collective-permute-done.21.refs_1_ = f32[136,512]{1,0:T(8,128)S(1)} collective-permute-done((f32[136,512]{1,0:T(8,128)S(1)}, f32[136,512]{1,0:T(8,128)S(1)}, u32[]{:S(2)}, u32[]{:S(2)}) %collective-permute-start.21) | collective-permute-done | bytes 278560 | tf_op jit(solution)/shard_map/ppermute | solution.py:590
  78.6 2.2 %collective-permute-start.32 = (f32[64,512]{1,0:T(8,128)S(1)}, f32[64,512]{1,0:T(8,128)S(1)}, u32[]{:S(2)}, u32[]{:S(2)}) collective-permute-start(f32[64,512]{1,0:T(8,128)S(1)} %get-tuple-element.313), channel_id=1, source_target_pairs={{0,6},{1,7},{2,4},{3,5},{4,2},{5,3},{6,0},{7,1},{8,14},{9,15},{10,... | collective-permute-start | bytes 393224 | tf_op jit(solution)/shard_map/ppermute | solution.py:590
  80.8 4.8 %collective-permute-done.22.refs_2_ = f32[136,512]{1,0:T(8,128)S(1)} collective-permute-done((f32[136,512]{1,0:T(8,128)S(1)}, f32[136,512]{1,0:T(8,128)S(1)}, u32[]{:S(2)}, u32[]{:S(2)}) %collective-permute-start.22) | collective-permute-done | bytes 278560 | tf_op jit(solution)/shard_map/ppermute | solution.py:590
  87.2 1.3 %collective-permute-start.33 = (f32[64,512]{1,0:T(8,128)S(1)}, f32[64,512]{1,0:T(8,128)S(1)}, u32[]{:S(2)}, u32[]{:S(2)}) collective-permute-start(f32[64,512]{1,0:T(8,128)S(1)} %lines_summed.2.refs_0_), channel_id=1, source_target_pairs={{0,1},{1,0},{2,3},{3,2},{4,5},{5,4},{6,7},{7,6},{8,9},{9,8},{10,11... | collective-permute-start | bytes 393224 | tf_op jit(solution)/shard_map/ppermute | solution.py:590
  88.4 2.9 %collective-permute-start.25 = (f32[40,512]{1,0:T(8,128)S(1)}, f32[40,512]{1,0:T(8,128)S(1)}, u32[]{:S(2)}, u32[]{:S(2)}) collective-permute-start(f32[40,512]{1,0:T(8,128)S(1)} %get-tuple-element.304), channel_id=1, source_target_pairs={{0,4},{1,5},{2,6},{3,7},{4,0},{5,1},{6,2},{7,3},{8,12},{9,13},{10,... | collective-permute-start | bytes 245768 | tf_op jit(solution)/shard_map/ppermute | solution.py:590
  91.3 1.6 %collective-permute-start.26 = (f32[40,512]{1,0:T(8,128)S(1)}, f32[40,512]{1,0:T(8,128)S(1)}, u32[]{:S(2)}, u32[]{:S(2)}) collective-permute-start(f32[40,512]{1,0:T(8,128)S(1)} %get-tuple-element.305), channel_id=1, source_target_pairs={{0,6},{1,7},{2,4},{3,5},{4,2},{5,3},{6,0},{7,1},{8,14},{9,15},{10,... | collective-permute-start | bytes 245768 | tf_op jit(solution)/shard_map/ppermute | solution.py:590
  92.9 1.3 %collective-permute-start.34 = (f32[64,512]{1,0:T(8,128)S(1)}, f32[64,512]{1,0:T(8,128)S(1)}, u32[]{:S(2)}, u32[]{:S(2)}) collective-permute-start(f32[64,512]{1,0:T(8,128)S(1)} %lines_summed.2.refs_0_), channel_id=1, source_target_pairs={{0,16},{1,17},{2,18},{3,19},{4,20},{5,21},{6,22},{7,23},{8,24},{9,... | collective-permute-start | bytes 393224 | tf_op jit(solution)/shard_map/ppermute | solution.py:590
  94.9 1.6 %collective-permute-done.25.refs_2_ = f32[40,512]{1,0:T(8,128)S(1)} collective-permute-done((f32[40,512]{1,0:T(8,128)S(1)}, f32[40,512]{1,0:T(8,128)S(1)}, u32[]{:S(2)}, u32[]{:S(2)}) %collective-permute-start.25) | collective-permute-done | bytes 81952 | tf_op jit(solution)/shard_map/ppermute | solution.py:590
  96.5 1.2 collective-permute-done.26.refs_3_
  97.7 1.2 body_summed.6
  100.1 1.2 collective-permute-start.28
  101.2 2.1 %collective-permute-start.29 = (f32[32,512]{1,0:T(8,128)S(1)}, f32[32,512]{1,0:T(8,128)S(1)}, u32[]{:S(2)}, u32[]{:S(2)}) collective-permute-start(f32[32,512]{1,0:T(8,128)S(1)} %get-tuple-element.309.refs_0_), channel_id=1, source_target_pairs={{0,6},{1,7},{2,4},{3,5},{4,2},{5,3},{6,0},{7,1},{8,14},{9,15},{10,... | collective-permute-start | bytes 196616 | tf_op jit(solution)/shard_map/ppermute | solution.py:590
  103.9 2.3 %collective-permute-done.28.refs_2_ = f32[32,512]{1,0:T(8,128)S(1)} collective-permute-done((f32[32,512]{1,0:T(8,128)S(1)}, f32[32,512]{1,0:T(8,128)S(1)}, u32[]{:S(2)}, u32[]{:S(2)}) %collective-permute-start.28) | collective-permute-done | bytes 65568 | tf_op jit(solution)/shard_map/ppermute | solution.py:590
  106.2 1.2 collective-permute-done.29.refs_3_
  110.1 2.6 %collective-permute-start.38 = (f32[128,512]{1,0:T(8,128)S(1)}, f32[128,512]{1,0:T(8,128)S(1)}, u32[]{:S(2)}, u32[]{:S(2)}) collective-permute-start(f32[128,512]{1,0:T(8,128)S(1)} %get-tuple-element.804), channel_id=1, source_target_pairs={{0,17},{1,16},{2,19},{3,18},{4,21},{5,20},{6,23},{7,22},{8,25},{9,... | collective-permute-start | bytes 786440 | tf_op jit(solution)/shard_map/ppermute | solution.py:590
  112.7 1.9 %collective-permute-start.40 = (f32[64,512]{1,0:T(8,128)S(1)}, f32[64,512]{1,0:T(8,128)S(1)}, u32[]{:S(2)}, u32[]{:S(2)}) collective-permute-start(f32[64,512]{1,0:T(8,128)S(1)} %get-tuple-element.805), channel_id=1, source_target_pairs={{0,4},{1,5},{2,6},{3,7},{4,0},{5,1},{6,2},{7,3},{8,12},{9,13},{10,... | collective-permute-start | bytes 393224 | tf_op jit(solution)/shard_map/ppermute | solution.py:590
  114.6 2.0 %collective-permute-start.41 = (f32[64,512]{1,0:T(8,128)S(1)}, f32[64,512]{1,0:T(8,128)S(1)}, u32[]{:S(2)}, u32[]{:S(2)}) collective-permute-start(f32[64,512]{1,0:T(8,128)S(1)} %get-tuple-element.805), channel_id=1, source_target_pairs={{0,6},{1,7},{2,4},{3,5},{4,2},{5,3},{6,0},{7,1},{8,14},{9,15},{10,... | collective-permute-start | bytes 393224 | tf_op jit(solution)/shard_map/ppermute | solution.py:590
  116.6 5.5 %collective-permute-done.40.refs_6_ = f32[64,512]{1,0:T(8,128)S(1)} collective-permute-done((f32[64,512]{1,0:T(8,128)S(1)}, f32[64,512]{1,0:T(8,128)S(1)}, u32[]{:S(2)}, u32[]{:S(2)}) %collective-permute-start.40) | collective-permute-done | bytes 131104 | tf_op jit(solution)/shard_map/ppermute | solution.py:590
  124.7 1.7 %collective-permute-done.42.block = f32[768,512]{1,0:T(8,128)S(1)} collective-permute-done((f32[768,512]{1,0:T(8,128)S(1)}, f32[768,512]{1,0:T(8,128)S(1)}, u32[]{:S(2)}, u32[]{:S(2)}) %collective-permute-start.42) | collective-permute-done | bytes 1572896 | tf_op jit(solution)/shard_map/ppermute | solution.py:590
  (68 shorter events, 13.0 us)
Async XLA Ops:
  0.6 14.0 %copy-start.24 = (s32[2048]{0:T(1024)S(1)}, s32[2048]{0:T(1024)}, u32[]{:S(2)}) copy-start(s32[2048]{0:T(1024)} %param.16) | copy-start | bytes 24580
  0.6 14.0 %copy-start.26 = (s32[2048]{0:T(1024)S(1)}, s32[2048]{0:T(1024)}, u32[]{:S(2)}) copy-start(s32[2048]{0:T(1024)} %param.15) | copy-start | bytes 24580
  13.3 14.3 %collective-permute-start.18 = (f32[200,512]{1,0:T(8,128)S(1)}, f32[200,512]{1,0:T(8,128)S(1)}, u32[]{:S(2)}, u32[]{:S(2)}) collective-permute-start(f32[200,512]{1,0:T(8,128)S(1)} %get-tuple-element.286), channel_id=1, source_target_pairs={{1,0},{2,1},{3,2},{4,3},{5,4},{6,5},{7,6},{9,8},{10,9},{11,10},{12... | collective-permute-start | bytes 1228808 | tf_op jit(solution)/shard_map/ppermute | solution.py:699
  32.8 14.6 %collective-permute-start.19 = (f32[192,512]{1,0:T(8,128)S(1)}, f32[192,512]{1,0:T(8,128)S(1)}, u32[]{:S(2)}, u32[]{:S(2)}) collective-permute-start(f32[192,512]{1,0:T(8,128)S(1)} %get-tuple-element.289), channel_id=1, source_target_pairs={{0,1},{1,2},{2,3},{3,4},{4,5},{5,6},{6,7},{8,9},{9,10},{10,11},{11... | collective-permute-start | bytes 1179656 | tf_op jit(solution)/shard_map/ppermute | solution.py:699
  37.7 9.7 %copy-start = (bf16[2048,512]{1,0:T(8,128)(2,1)S(1)}, bf16[2048,512]{1,0:T(8,128)(2,1)}, u32[]{:S(2)}) copy-start(bf16[2048,512]{1,0:T(8,128)(2,1)} %x_ref.3) | copy-start | bytes 6291460
  37.7 9.7 %copy-start.8 = (bf16[2048,512]{1,0:T(8,128)(2,1)S(1)}, bf16[2048,512]{1,0:T(8,128)(2,1)}, u32[]{:S(2)}) copy-start(bf16[2048,512]{1,0:T(8,128)(2,1)} %get-tuple-element.285.indicator_ref.indicator) | copy-start | bytes 6291460
  37.7 9.7 %copy-start.9 = (f32[2048,512]{1,0:T(8,128)S(1)}, f32[2048,512]{1,0:T(8,128)}, u32[]{:S(2)}) copy-start(f32[2048,512]{1,0:T(8,128)} %get-tuple-element.295.slope_in) | copy-start | bytes 12582916
  37.7 9.7 %copy-start.10 = (f32[2048,512]{1,0:T(8,128)S(1)}, f32[2048,512]{1,0:T(8,128)}, u32[]{:S(2)}) copy-start(f32[2048,512]{1,0:T(8,128)} %get-tuple-element.293.slope_mid) | copy-start | bytes 12582916
  59.5 4.4 %collective-permute-start.20 = (f32[776,512]{1,0:T(8,128)}, f32[776,512]{1,0:T(8,128)}, u32[]{:S(2)}, u32[]{:S(2)}) collective-permute-start(f32[776,512]{1,0:T(8,128)} %get-tuple-element.297), channel_id=1, source_target_pairs={{0,8},{1,9},{2,10},{3,11},{4,12},{5,13},{6,14},{7,15},{8,0},{9,1},... | collective-permute-start | bytes 4767752 | tf_op jit(solution)/shard_map/ppermute | solution.py:590
  66.7 11.9 %collective-permute-start.21 = (f32[136,512]{1,0:T(8,128)S(1)}, f32[136,512]{1,0:T(8,128)S(1)}, u32[]{:S(2)}, u32[]{:S(2)}) collective-permute-start(f32[136,512]{1,0:T(8,128)S(1)} %get-tuple-element.299), channel_id=1, source_target_pairs={{0,1},{1,0},{2,3},{3,2},{4,5},{5,4},{6,7},{7,6},{8,9},{9,8},{10,11... | collective-permute-start | bytes 835592 | tf_op jit(solution)/shard_map/ppermute | solution.py:590
  71.1 14.4 %collective-permute-start.22 = (f32[136,512]{1,0:T(8,128)S(1)}, f32[136,512]{1,0:T(8,128)S(1)}, u32[]{:S(2)}, u32[]{:S(2)}) collective-permute-start(f32[136,512]{1,0:T(8,128)S(1)} %get-tuple-element.300), channel_id=1, source_target_pairs={{0,16},{1,17},{2,18},{3,19},{4,20},{5,21},{6,22},{7,23},{8,24},{9,... | collective-permute-start | bytes 835592 | tf_op jit(solution)/shard_map/ppermute | solution.py:590
  71.1 14.4 %collective-permute-start.23 = (f32[136,512]{1,0:T(8,128)S(1)}, f32[136,512]{1,0:T(8,128)S(1)}, u32[]{:S(2)}, u32[]{:S(2)}) collective-permute-start(f32[136,512]{1,0:T(8,128)S(1)} %get-tuple-element.301), channel_id=1, source_target_pairs={{0,17},{1,16},{2,19},{3,18},{4,21},{5,20},{6,23},{7,22},{8,25},{9,... | collective-permute-start | bytes 835592 | tf_op jit(solution)/shard_map/ppermute | solution.py:590
  72.7 13.9 %collective-permute-start.30 = (f32[64,512]{1,0:T(8,128)S(1)}, f32[64,512]{1,0:T(8,128)S(1)}, u32[]{:S(2)}, u32[]{:S(2)}) collective-permute-start(f32[64,512]{1,0:T(8,128)S(1)} %get-tuple-element.311), channel_id=1, source_target_pairs={{0,2},{1,3},{2,0},{3,1},{4,6},{5,7},{6,4},{7,5},{8,10},{9,11},{10,... | collective-permute-start | bytes 393224 | tf_op jit(solution)/shard_map/ppermute | solution.py:590
  73.8 12.7 %collective-permute-start.31 = (f32[64,512]{1,0:T(8,128)S(1)}, f32[64,512]{1,0:T(8,128)S(1)}, u32[]{:S(2)}, u32[]{:S(2)}) collective-permute-start(f32[64,512]{1,0:T(8,128)S(1)} %get-tuple-element.312), channel_id=1, source_target_pairs={{0,4},{1,5},{2,6},{3,7},{4,0},{5,1},{6,2},{7,3},{8,12},{9,13},{10,... | collective-permute-start | bytes 393224 | tf_op jit(solution)/shard_map/ppermute | solution.py:590
  78.6 8.0 %collective-permute-start.32 = (f32[64,512]{1,0:T(8,128)S(1)}, f32[64,512]{1,0:T(8,128)S(1)}, u32[]{:S(2)}, u32[]{:S(2)}) collective-permute-start(f32[64,512]{1,0:T(8,128)S(1)} %get-tuple-element.313), channel_id=1, source_target_pairs={{0,6},{1,7},{2,4},{3,5},{4,2},{5,3},{6,0},{7,1},{8,14},{9,15},{10,... | collective-permute-start | bytes 393224 | tf_op jit(solution)/shard_map/ppermute | solution.py:590
  85.6 8.6 %collective-permute-start.24 = (f32[40,512]{1,0:T(8,128)S(1)}, f32[40,512]{1,0:T(8,128)S(1)}, u32[]{:S(2)}, u32[]{:S(2)}) collective-permute-start(f32[40,512]{1,0:T(8,128)S(1)} %get-tuple-element.303), channel_id=1, source_target_pairs={{0,2},{1,3},{2,0},{3,1},{4,6},{5,7},{6,4},{7,5},{8,10},{9,11},{10,... | collective-permute-start | bytes 245768 | tf_op jit(solution)/shard_map/ppermute | solution.py:590
  87.2 14.1 %collective-permute-start.33 = (f32[64,512]{1,0:T(8,128)S(1)}, f32[64,512]{1,0:T(8,128)S(1)}, u32[]{:S(2)}, u32[]{:S(2)}) collective-permute-start(f32[64,512]{1,0:T(8,128)S(1)} %lines_summed.2.refs_0_), channel_id=1, source_target_pairs={{0,1},{1,0},{2,3},{3,2},{4,5},{5,4},{6,7},{7,6},{8,9},{9,8},{10,11... | collective-permute-start | bytes 393224 | tf_op jit(solution)/shard_map/ppermute | solution.py:590
  88.4 8.0 %collective-permute-start.25 = (f32[40,512]{1,0:T(8,128)S(1)}, f32[40,512]{1,0:T(8,128)S(1)}, u32[]{:S(2)}, u32[]{:S(2)}) collective-permute-start(f32[40,512]{1,0:T(8,128)S(1)} %get-tuple-element.304), channel_id=1, source_target_pairs={{0,4},{1,5},{2,6},{3,7},{4,0},{5,1},{6,2},{7,3},{8,12},{9,13},{10,... | collective-permute-start | bytes 245768 | tf_op jit(solution)/shard_map/ppermute | solution.py:590
  91.3 6.3 %collective-permute-start.26 = (f32[40,512]{1,0:T(8,128)S(1)}, f32[40,512]{1,0:T(8,128)S(1)}, u32[]{:S(2)}, u32[]{:S(2)}) collective-permute-start(f32[40,512]{1,0:T(8,128)S(1)} %get-tuple-element.305), channel_id=1, source_target_pairs={{0,6},{1,7},{2,4},{3,5},{4,2},{5,3},{6,0},{7,1},{8,14},{9,15},{10,... | collective-permute-start | bytes 245768 | tf_op jit(solution)/shard_map/ppermute | solution.py:590
  92.9 10.4 %collective-permute-start.34 = (f32[64,512]{1,0:T(8,128)S(1)}, f32[64,512]{1,0:T(8,128)S(1)}, u32[]{:S(2)}, u32[]{:S(2)}) collective-permute-start(f32[64,512]{1,0:T(8,128)S(1)} %lines_summed.2.refs_0_), channel_id=1, source_target_pairs={{0,16},{1,17},{2,18},{3,19},{4,20},{5,21},{6,22},{7,23},{8,24},{9,... | collective-permute-start | bytes 393224 | tf_op jit(solution)/shard_map/ppermute | solution.py:590
  94.2 9.1 %collective-permute-start.35 = (f32[64,512]{1,0:T(8,128)S(1)}, f32[64,512]{1,0:T(8,128)S(1)}, u32[]{:S(2)}, u32[]{:S(2)}) collective-permute-start(f32[64,512]{1,0:T(8,128)S(1)} %lines_summed.2.refs_0_), channel_id=1, source_target_pairs={{0,17},{1,16},{2,19},{3,18},{4,21},{5,20},{6,23},{7,22},{8,25},{9,... | collective-permute-start | bytes 393224 | tf_op jit(solution)/shard_map/ppermute | solution.py:590
  98.9 5.1 %collective-permute-start.27 = (f32[32,512]{1,0:T(8,128)S(1)}, f32[32,512]{1,0:T(8,128)S(1)}, u32[]{:S(2)}, u32[]{:S(2)}) collective-permute-start(f32[32,512]{1,0:T(8,128)S(1)} %get-tuple-element.309.refs_0_), channel_id=1, source_target_pairs={{0,2},{1,3},{2,0},{3,1},{4,6},{5,7},{6,4},{7,5},{8,10},{9,11},{10,... | collective-permute-start | bytes 196616 | tf_op jit(solution)/shard_map/ppermute | solution.py:590
  100.1 6.2 %collective-permute-start.28 = (f32[32,512]{1,0:T(8,128)S(1)}, f32[32,512]{1,0:T(8,128)S(1)}, u32[]{:S(2)}, u32[]{:S(2)}) collective-permute-start(f32[32,512]{1,0:T(8,128)S(1)} %get-tuple-element.309.refs_0_), channel_id=1, source_target_pairs={{0,4},{1,5},{2,6},{3,7},{4,0},{5,1},{6,2},{7,3},{8,12},{9,13},{10,... | collective-permute-start | bytes 196616 | tf_op jit(solution)/shard_map/ppermute | solution.py:590
  101.2 6.2 %collective-permute-start.29 = (f32[32,512]{1,0:T(8,128)S(1)}, f32[32,512]{1,0:T(8,128)S(1)}, u32[]{:S(2)}, u32[]{:S(2)}) collective-permute-start(f32[32,512]{1,0:T(8,128)S(1)} %get-tuple-element.309.refs_0_), channel_id=1, source_target_pairs={{0,6},{1,7},{2,4},{3,5},{4,2},{5,3},{6,0},{7,1},{8,14},{9,15},{10,... | collective-permute-start | bytes 196616 | tf_op jit(solution)/shard_map/ppermute | solution.py:590
  107.4 14.7 %copy-start.15 = (s32[2]{0:T(128)S(1)}, s32[2]{0:T(128)}, u32[]{:S(2)}) copy-start(s32[2]{0:T(128)} %copy-done.14) | copy-start | bytes 28
  108.3 6.3 %collective-permute-start.39 = (f32[64,512]{1,0:T(8,128)S(1)}, f32[64,512]{1,0:T(8,128)S(1)}, u32[]{:S(2)}, u32[]{:S(2)}) collective-permute-start(f32[64,512]{1,0:T(8,128)S(1)} %get-tuple-element.805), channel_id=1, source_target_pairs={{0,2},{1,3},{2,0},{3,1},{4,6},{5,7},{6,4},{7,5},{8,10},{9,11},{10,... | collective-permute-start | bytes 393224 | tf_op jit(solution)/shard_map/ppermute | solution.py:590
  109.2 12.9 %collective-permute-start.36 = (f32[128,512]{1,0:T(8,128)S(1)}, f32[128,512]{1,0:T(8,128)S(1)}, u32[]{:S(2)}, u32[]{:S(2)}) collective-permute-start(f32[128,512]{1,0:T(8,128)S(1)} %get-tuple-element.804), channel_id=1, source_target_pairs={{0,1},{1,0},{2,3},{3,2},{4,5},{5,4},{6,7},{7,6},{8,9},{9,8},{10,11... | collective-permute-start | bytes 786440 | tf_op jit(solution)/shard_map/ppermute | solution.py:590
  109.7 12.4 %collective-permute-start.37 = (f32[128,512]{1,0:T(8,128)S(1)}, f32[128,512]{1,0:T(8,128)S(1)}, u32[]{:S(2)}, u32[]{:S(2)}) collective-permute-start(f32[128,512]{1,0:T(8,128)S(1)} %get-tuple-element.804), channel_id=1, source_target_pairs={{0,16},{1,17},{2,18},{3,19},{4,20},{5,21},{6,22},{7,23},{8,24},{9,... | collective-permute-start | bytes 786440 | tf_op jit(solution)/shard_map/ppermute | solution.py:590
  110.1 12.0 %collective-permute-start.38 = (f32[128,512]{1,0:T(8,128)S(1)}, f32[128,512]{1,0:T(8,128)S(1)}, u32[]{:S(2)}, u32[]{:S(2)}) collective-permute-start(f32[128,512]{1,0:T(8,128)S(1)} %get-tuple-element.804), channel_id=1, source_target_pairs={{0,17},{1,16},{2,19},{3,18},{4,21},{5,20},{6,23},{7,22},{8,25},{9,... | collective-permute-start | bytes 786440 | tf_op jit(solution)/shard_map/ppermute | solution.py:590
  112.7 9.4 %collective-permute-start.40 = (f32[64,512]{1,0:T(8,128)S(1)}, f32[64,512]{1,0:T(8,128)S(1)}, u32[]{:S(2)}, u32[]{:S(2)}) collective-permute-start(f32[64,512]{1,0:T(8,128)S(1)} %get-tuple-element.805), channel_id=1, source_target_pairs={{0,4},{1,5},{2,6},{3,7},{4,0},{5,1},{6,2},{7,3},{8,12},{9,13},{10,... | collective-permute-start | bytes 393224 | tf_op jit(solution)/shard_map/ppermute | solution.py:590
  114.6 7.5 %collective-permute-start.41 = (f32[64,512]{1,0:T(8,128)S(1)}, f32[64,512]{1,0:T(8,128)S(1)}, u32[]{:S(2)}, u32[]{:S(2)}) collective-permute-start(f32[64,512]{1,0:T(8,128)S(1)} %get-tuple-element.805), channel_id=1, source_target_pairs={{0,6},{1,7},{2,4},{3,5},{4,2},{5,3},{6,0},{7,1},{8,14},{9,15},{10,... | collective-permute-start | bytes 393224 | tf_op jit(solution)/shard_map/ppermute | solution.py:590
  122.9 3.5 %collective-permute-start.42 = (f32[768,512]{1,0:T(8,128)S(1)}, f32[768,512]{1,0:T(8,128)S(1)}, u32[]{:S(2)}, u32[]{:S(2)}) collective-permute-start(f32[768,512]{1,0:T(8,128)S(1)} %collect_second.1.block), channel_id=1, source_target_pairs={{0,8},{1,9},{2,10},{3,11},{4,12},{5,13},{6,14},{7,15},{8,0},{9,1},... | collective-permute-start | bytes 4718600 | tf_op jit(solution)/shard_map/ppermute | solution.py:590
  (7 other events, 64.2 us)

commit v5 on v4

--- a/solution.py
+++ b/solution.py
@@ -215,24 +215,40 @@
     )(block_start, *map(in_hbm, (entry, features, events.T, *constant)))
 
 
+def parts_at(array, row, count):
+    if count == DEPTH:
+        return array[pl.ds(pl.multiple_of(row * 2, 2 * DEPTH), 2 * DEPTH), :]
+    at = row + row // DEPTH * DEPTH
+    top = array[pl.ds(pl.multiple_of(at, count), count), :]
+    rest = array[pl.ds(pl.multiple_of(at + DEPTH, count), count), :]
+    return jnp.concatenate([top, rest], axis=0)
+
+
 def own_risk_kernel(starts, entry_ref, first_ref, weight, out):
     step = pl.program_id(0)
     tile = first_ref.shape[1]
     rows = weight.shape[0] // 2
-    first = widen(as_column(first_ref[...]), DEPTH)
+    first = as_column(first_ref[...])
     own = pl.ds(pl.multiple_of(step * tile, tile), tile)
-    out[own, :] = jnp.zeros((tile, out.shape[1]), F32)
-
-    def part(k, _):
-        at = pl.multiple_of(k * DEPTH, DEPTH)
-        row = iota((tile, DEPTH), 1) + at
-        entry = entry_ref[pl.ds(k, 1), :]
-        mask = ones_where((row >= first) & (entry <= first))
-        both = pl.ds(pl.multiple_of(k * 2 * DEPTH, 2 * DEPTH), 2 * DEPTH)
-        out[own, :] += dot(twice(mask, DEPTH), weight[both, :])
+
+    def part(at, count):
+        at = pl.multiple_of(at, count)
+        row = iota((tile, count), 1) + at
+        wide = widen(first, count)
+        mask = ones_where((row >= wide) & (entry_ref[:, pl.ds(at, count)] <= wide))
+        return dot(twice(mask, count), parts_at(weight, at, count))
+
+    def ahead(k, _):
+        out[own, :] += part(k * LANES, LANES)
         return 0
 
-    lax.fori_loop(starts[step] // DEPTH, rows // DEPTH, part, 0)
+    def behind(k, _):
+        out[own, :] += part(k * DEPTH, DEPTH)
+        return 0
+
+    out[own, :] = part(step * tile, tile)
+    lax.fori_loop(starts[step * (tile // LANES)] // LANES, step * (tile // LANES), ahead, 0)
+    lax.fori_loop(step + 1, rows // DEPTH, behind, 0)
 
 
 def block_sum(flops):
@@ -253,7 +269,7 @@
         compiler_params=params(16),
         cost_estimate=block_sum(rows * rows * width * 4),
         name="own_risk",
-    )(starts, entry.reshape(rows // DEPTH, DEPTH), first, in_hbm(weight))
+    )(starts, entry, first, in_hbm(weight))
 
 
 def own_exposure_kernel(starts, first_ref, entry_ref, hazard, out, note):
@@ -264,30 +280,36 @@
     def _():
         note[...] = jnp.zeros_like(note)
 
-    entry = widen(as_column(entry_ref[...]), DEPTH)
-    row = iota((tile, DEPTH), 0) + step * tile
+    entry = as_column(entry_ref[...])
     own = pl.ds(pl.multiple_of(step * tile, tile), tile)
-    last = step * tile + tile - 1
-    parts = jnp.int32(0)
-    for k in range(first_ref.shape[0]):
-        parts += jnp.where(starts[k * (DEPTH // TILE)] <= last, 1, 0).astype(I32)
-
-    def part(k):
-        first = first_ref[pl.ds(k, 1), :]
-        mask = ones_where((first >= entry) & (first <= row))
-        both = pl.ds(pl.multiple_of(k * 2 * DEPTH, 2 * DEPTH), 2 * DEPTH)
-        return dot(twice(mask, DEPTH), hazard[both, :])
-
-    def others(i, _):
-        out[own, :] += part(i + jnp.where(i >= step, 1, 0).astype(I32))
+    end = (step + 1) * tile
+    reach = jnp.int32(0)
+    for k in range(first_ref.shape[1] // LANES):
+        inside = (k * LANES >= end) & (starts[k] < end)
+        reach += jnp.where(inside, 1, 0).astype(I32)
+
+    def part(at, count):
+        at = pl.multiple_of(at, count)
+        first = first_ref[:, pl.ds(at, count)]
+        row = iota((tile, count), 0) + step * tile
+        mask = ones_where((first >= widen(entry, count)) & (first <= row))
+        return dot(twice(mask, count), parts_at(hazard, at, count))
+
+    def before(k, _):
+        out[own, :] += part(k * DEPTH, DEPTH)
         return 0
 
-    out[own, :] = part(step)
+    def after(k, _):
+        out[own, :] += part(end + k * LANES, LANES)
+        return 0
+
+    out[own, :] = part(step * tile, tile)
     top = hazard[pl.ds(pl.multiple_of(step * 2 * tile, tile), tile), :].astype(F32)
     rest = hazard[pl.ds(pl.multiple_of(step * 2 * tile + tile, tile), tile), :].astype(F32)
     logs = jnp.where(top > 0.0, jnp.log(top + rest), 0.0)
     note[0:1, :] -= jnp.sum(logs, axis=0, keepdims=True)
-    lax.fori_loop(0, parts - 1, others, 0)
+    lax.fori_loop(0, step, before, 0)
+    lax.fori_loop(0, reach, after, 0)
 
 
 def own_exposure(starts, first, entry, hazard):
@@ -304,7 +326,7 @@
         compiler_params=params(12),
         cost_estimate=block_sum(rows * rows * width * 4),
         name="own_exposure",
-    )(starts, first.reshape(rows // DEPTH, DEPTH), entry, in_vmem(hazard))
+    )(starts, first, entry, in_vmem(hazard))
 
 
 def split_sum(source, parts, cap):
@@ -396,15 +418,25 @@
         return total + group_sum(ones_where(rank == iota((tile, GROUP), 1) + t * GROUP), parts, t)
 
     exposure = lax.fori_loop(0, cap // GROUP, behind, exposure_ref[own, :])
-    top = weight[pl.ds(pl.multiple_of(step * 2 * tile, tile), tile), :].astype(F32)
-    rest = weight[pl.ds(pl.multiple_of(step * 2 * tile + tile, tile), tile), :].astype(F32)
-    eta = ((top + rest) * exposure - indicator[own, :].astype(F32)).astype(BF16)
-    grad_out[...] += dot(hidden[own, :], eta, 0, 0)
-    mid = (dot(eta, w_out[...], 1, 1) * slope_mid[own, :]).astype(BF16)
-    grad_mid[...] += dot(first_hidden[own, :], mid, 0, 0)
-    pre = (dot(mid, w_mid[...], 1, 1) * slope_in[own, :]).astype(BF16)
-    grad_in[...] += dot(x_ref[own, :], pre, 0, 0)
-    grad_x[...] = dot(pre, w_in[...], 1, 1).astype(BF16)
+    part = tile // 2
+    cuts = [slice(0, part), slice(part, tile)]
+    at = [pl.ds(pl.multiple_of(step * tile + k * part, part), part) for k in range(2)]
+    etas = []
+    for k in range(2):
+        start = step * 2 * tile + k * part
+        top = weight[pl.ds(pl.multiple_of(start, part), part), :].astype(F32)
+        rest = weight[pl.ds(pl.multiple_of(start + tile, part), part), :].astype(F32)
+        value = (top + rest) * exposure[cuts[k]] - indicator[at[k], :].astype(F32)
+        etas.append(value.astype(BF16))
+    mids = [dot(eta, w_out[...], 1, 1) for eta in etas]
+    grad_out[...] += dot(hidden[own, :], jnp.concatenate(etas, axis=0), 0, 0)
+    mids = [(mids[k] * slope_mid[at[k], :]).astype(BF16) for k in range(2)]
+    pres = [dot(mid, w_mid[...], 1, 1) for mid in mids]
+    grad_mid[...] += dot(first_hidden[own, :], jnp.concatenate(mids, axis=0), 0, 0)
+    pres = [(pres[k] * slope_in[at[k], :]).astype(BF16) for k in range(2)]
+    grad_in[...] += dot(x_ref[own, :], jnp.concatenate(pres, axis=0), 0, 0)
+    for k in range(2):
+        grad_x[cuts[k], :] = dot(pres[k], w_in[...], 1, 1).astype(BF16)
 
     @pl.when(step == pl.num_programs(0) - 1)
     def _():
@@ -706,17 +738,17 @@
     entry = entry_row - block_start
     first_line = first.reshape(1, rows)
     entry_line = entry.reshape(1, rows)
-    starts = first[::TILE]
+    starts = first[::LANES]
     (
         first_hidden, hidden, slope_in, slope_mid, indicator, weight, send, note, rank,
     ) = trunk(
         cap, block_start, entry_row.reshape(1, rows), features, events, w_in, w_mid, w_out
     )
     got = from_behind(send, "chain", -1)
-    risk = own_risk(starts, entry, first_line, weight)
+    risk = own_risk(starts, entry_line, first_line, weight)
     hazard, sums = hazards(cap, first_line, risk, indicator, got)
     got_sums = from_behind(sums, "chain", 1)
-    exposure, log_part = own_exposure(starts, first, entry_line, hazard)
+    exposure, log_part = own_exposure(starts, first_line, entry_line, hazard)
     kept = (weight, indicator, hidden, slope_mid, first_hidden, slope_in)
     return backward(
         cap, total_rows ** (-0.5), half, rank, exposure, got_sums, (note, log_part), kept,

time: 128 us -> 125 us (0.977)
  waiting for transfers between devices: 27.6 us -> 25.7 us
    ppermute x23, waiting for transfers between devices: 24.9 us -> 22.7 us  [hop(): return lax.ppermute(block, ('strata', 'chain'), route)]
  transfers between devices with their start and end apart: 25 -> 25, of which waited for: 11 -> 12; matrix products, arithmetic and copies ran while one was open for 1% -> 1% of each run, Pallas kernels for 18% -> 19%
where the time goes in v5:
time: 125 us; the launch traced here: 124 us
  Pallas kernels  57.2 us (46%)
  starting transfers between devices  38.4 us (31%)
  waiting for transfers between devices  25.7 us (21%)
    ppermute x23, starting transfers between devices, hop(): return lax.ppermute(block, ('strata', 'chain'), route)  32.6 us
    ppermute x23, waiting for transfers between devices, hop(): return lax.ppermute(block, ('strata', 'chain'), route)  22.7 us
    pallas_call x1, Pallas kernels, trunk(): pl.pallas_call(partial(trunk_kernel, cap), grid=(rows // TILE,), in_specs...  12.6 us
    pallas_call x1, Pallas kernels, backward(): pl.pallas_call(partial(backward_kernel, cap, factor), grid=(rows // TILE,...  11.2 us
    pallas_call x1, Pallas kernels, own_exposure(): pl.pallas_call(own_exposure_kernel, grid=(rows // TILE,), in_specs=[pl.Bl...  9.97 us
    pallas_call x1, Pallas kernels, own_risk(): pl.pallas_call(own_risk_kernel, grid=(rows // TILE,), in_specs=[pl.BlockS...  9.92 us
    ppermute x2, starting transfers between devices, from_behind(): return lax.ppermute(block, axis, route)  5.85 us
    pallas_call x1, Pallas kernels, hazards(): pl.pallas_call(partial(hazard_kernel, cap), grid=(rows // TILE,), in_spec...  5.2 us
  transfers between devices with their start and end apart: 25, of which 12 were waited for; matrix products, arithmetic and copies ran while one was open for 1% of the time, Pallas kernels for 19%

profile of v5, /device:TPU:0, one launch (start us, length us, event | category | flops | bytes accessed | tf_op | source)
XLA Modules:
  0.0 124.2 jit_solution(7846351216239349187)
XLA Ops:
  0.7 12.6 %trunk.6 = (bf16[2048,512]{1,0:T(8,128)(2,1)}, bf16[2048,512]{1,0:T(8,128)(2,1)}, f32[2048,512]{1,0:T(8,128)}, f32[2048,512]{1,0:T(8,128)}, bf16[2048,512]{1,0:T...) custom-call(s32[1]{0:T(128)} %bitcast.3.block_start, ...), custom_call_target="tpu_custom_call" | custom-call | tf_op jit(solution)/shard_map/trunk/pallas_call | solution.py:193
  13.3 1.3 %collective-permute-start.18 = (f32[200,512]{1,0:T(8,128)S(1)}, f32[200,512]{1,0:T(8,128)S(1)}, u32[]{:S(2)}, u32[]{:S(2)}) collective-permute-start(f32[200,512]{1,0:T(8,128)S(1)} %get-tuple-element.286), channel_id=1, source_target_pairs={{1,0},{2,1},{3,2},{4,3},{5,4},{6,5},{7,6},{9,8},{10,9},{11,10},{12... | collective-permute-start | bytes 1228808 | tf_op jit(solution)/shard_map/ppermute | solution.py:731
  14.7 9.9 %own_risk.2.risk = f32[2048,512]{1,0:T(8,128)S(1)} custom-call(s32[16]{0:T(128)S(1)} %slice.9.starts, s32[1,2048]{1,0:T(1,128)S(1)} %bitcast.37, s32[1,2048]{1,0:T(1,128)S(1)} %bitcast.33, bf16[4096,512]{1,0:T(8,128)(2,1)} %get-tuple-element.284.weight), custom_call_target="tpu_custom_call" | custom-call | flops 8589934592 | bytes 33554432 | tf_op jit(solution)/shard_map/own_risk/pallas_call | solution.py:260
  24.7 2.9 %collective-permute-done.18.got = f32[200,512]{1,0:T(8,128)S(1)} collective-permute-done((f32[200,512]{1,0:T(8,128)S(1)}, f32[200,512]{1,0:T(8,128)S(1)}, u32[]{:S(2)}, u32[]{:S(2)}) %collective-permute-start.18) | collective-permute-done | bytes 409632 | tf_op jit(solution)/shard_map/ppermute | solution.py:731
  27.6 5.2 %hazards.6 = (bf16[4096,512]{1,0:T(8,128)(2,1)S(1)}, f32[192,512]{1,0:T(8,128)S(1)}) custom-call(s32[1,2048]{1,0:T(1,128)S(1)} %bitcast.34, s32[1,2048]{1,0:T(1,128)S(1)} %bitcast.35, f32[2048,512]{1,0:T(8,128)S(1)} %own_risk.2.risk, bf16[2048,512]{1,0:T(8,128)(2,1)} %get-tuple-element.285.indicator_ref.indicator, f32[200,512]{1,0:T(8,128)S(1)} %collective-permute-done.18.got), custom_call_target="tpu_custom_call" | custom-call | tf_op jit(solution)/shard_map/hazards/pallas_call | solution.py:385
  32.8 4.6 %collective-permute-start.19 = (f32[192,512]{1,0:T(8,128)S(1)}, f32[192,512]{1,0:T(8,128)S(1)}, u32[]{:S(2)}, u32[]{:S(2)}) collective-permute-start(f32[192,512]{1,0:T(8,128)S(1)} %get-tuple-element.289), channel_id=1, source_target_pairs={{0,1},{1,2},{2,3},{3,4},{4,5},{5,6},{6,7},{8,9},{9,10},{10,11},{11... | collective-permute-start | bytes 1179656 | tf_op jit(solution)/shard_map/ppermute | solution.py:731
  37.5 10.0 %own_exposure.6 = (f32[2048,512]{1,0:T(8,128)S(1)}, f32[8,512]{1,0:T(8,128)S(1)}) custom-call(s32[16]{0:T(128)S(1)} %slice.9.starts, s32[1,2048]{1,0:T(1,128)S(1)} %bitcast.36, s32[1,2048]{1,0:T(1,128)S(1)} %bitcast.38, bf16[4096,512]{1,0:T(8,128)(2,1)S(1)} %get-tuple-element.287.hazard), custom_call_target="tpu_custom_call" | custom-call | flops 8589934592 | bytes 33554432 | tf_op jit(solution)/shard_map/own_exposure/pallas_call | solution.py:318
  47.6 11.2 %backward.6 = (bf16[2048,512]{1,0:T(8,128)(2,1)}, f32[776,512]{1,0:T(8,128)}, f32[776,512]{1,0:T(8,128)}) custom-call(s32[1]{0:T(128)} %bitcast.2.half, s32[1,2048]{1,0:T(1,128)S(1)} %get-tuple-element.283.rank_ref, f32[2048,512]{1,0:T(8,128)S(1)} %get-tuple-element.288.exposure_ref, f32[192,512]{1,0:T(8,128)S(1)} %collective-permute-done.19.got, ...), custom_call_target="tpu_custom_call" | custom-call | tf_op jit(solution)/shard_map/backward/pallas_call | solution.py:468
  58.8 3.7 %collective-permute-done.20.refs_1_ = f32[776,512]{1,0:T(8,128)} collective-permute-done((f32[776,512]{1,0:T(8,128)}, f32[776,512]{1,0:T(8,128)}, u32[]{:S(2)}, u32[]{:S(2)}) %collective-permute-start.20) | collective-permute-done | bytes 1589280 | tf_op jit(solution)/shard_map/ppermute | solution.py:622
  62.5 2.7 %spread_first.6 = (f32[136,512]{1,0:T(8,128)S(1)}, f32[136,512]{1,0:T(8,128)S(1)}, f32[136,512]{1,0:T(8,128)S(1)}, f32[136,512]{1,0:T(8,128)S(1)}, f32[64,512]{1...) custom-call(s32[2]{0:T(128)S(1)} %pad_add_fusion.1.me, ...), custom_call_target="tpu_custom_call" | custom-call | tf_op jit(solution)/shard_map/spread_first/pallas_call | solution.py:556
  65.3 1.6 %collective-permute-start.21 = (f32[136,512]{1,0:T(8,128)S(1)}, f32[136,512]{1,0:T(8,128)S(1)}, u32[]{:S(2)}, u32[]{:S(2)}) collective-permute-start(f32[136,512]{1,0:T(8,128)S(1)} %get-tuple-element.299), channel_id=1, source_target_pairs={{0,1},{1,0},{2,3},{3,2},{4,5},{5,4},{6,7},{7,6},{8,9},{9,8},{10,11... | collective-permute-start | bytes 835592 | tf_op jit(solution)/shard_map/ppermute | solution.py:622
  66.9 1.5 %collective-permute-start.22 = (f32[136,512]{1,0:T(8,128)S(1)}, f32[136,512]{1,0:T(8,128)S(1)}, u32[]{:S(2)}, u32[]{:S(2)}) collective-permute-start(f32[136,512]{1,0:T(8,128)S(1)} %get-tuple-element.300), channel_id=1, source_target_pairs={{0,16},{1,17},{2,18},{3,19},{4,20},{5,21},{6,22},{7,23},{8,24},{9,... | collective-permute-start | bytes 835592 | tf_op jit(solution)/shard_map/ppermute | solution.py:622
  69.0 1.8 %collective-permute-start.30 = (f32[64,512]{1,0:T(8,128)S(1)}, f32[64,512]{1,0:T(8,128)S(1)}, u32[]{:S(2)}, u32[]{:S(2)}) collective-permute-start(f32[64,512]{1,0:T(8,128)S(1)} %get-tuple-element.311), channel_id=1, source_target_pairs={{0,2},{1,3},{2,0},{3,1},{4,6},{5,7},{6,4},{7,5},{8,10},{9,11},{10,... | collective-permute-start | bytes 393224 | tf_op jit(solution)/shard_map/ppermute | solution.py:622
  70.7 1.8 %collective-permute-start.31 = (f32[64,512]{1,0:T(8,128)S(1)}, f32[64,512]{1,0:T(8,128)S(1)}, u32[]{:S(2)}, u32[]{:S(2)}) collective-permute-start(f32[64,512]{1,0:T(8,128)S(1)} %get-tuple-element.312), channel_id=1, source_target_pairs={{0,4},{1,5},{2,6},{3,7},{4,0},{5,1},{6,2},{7,3},{8,12},{9,13},{10,... | collective-permute-start | bytes 393224 | tf_op jit(solution)/shard_map/ppermute | solution.py:622
  72.5 2.4 %collective-permute-done.21.refs_1_ = f32[136,512]{1,0:T(8,128)S(1)} collective-permute-done((f32[136,512]{1,0:T(8,128)S(1)}, f32[136,512]{1,0:T(8,128)S(1)}, u32[]{:S(2)}, u32[]{:S(2)}) %collective-permute-start.21) | collective-permute-done | bytes 278560 | tf_op jit(solution)/shard_map/ppermute | solution.py:622
  74.9 3.1 %collective-permute-start.32 = (f32[64,512]{1,0:T(8,128)S(1)}, f32[64,512]{1,0:T(8,128)S(1)}, u32[]{:S(2)}, u32[]{:S(2)}) collective-permute-start(f32[64,512]{1,0:T(8,128)S(1)} %get-tuple-element.313), channel_id=1, source_target_pairs={{0,6},{1,7},{2,4},{3,5},{4,2},{5,3},{6,0},{7,1},{8,14},{9,15},{10,... | collective-permute-start | bytes 393224 | tf_op jit(solution)/shard_map/ppermute | solution.py:622
  78.0 2.4 %collective-permute-done.22.refs_2_ = f32[136,512]{1,0:T(8,128)S(1)} collective-permute-done((f32[136,512]{1,0:T(8,128)S(1)}, f32[136,512]{1,0:T(8,128)S(1)}, u32[]{:S(2)}, u32[]{:S(2)}) %collective-permute-start.22) | collective-permute-done | bytes 278560 | tf_op jit(solution)/shard_map/ppermute | solution.py:622
  80.3 1.3 %collective-permute-done.23.refs_3_ = f32[136,512]{1,0:T(8,128)S(1)} collective-permute-done((f32[136,512]{1,0:T(8,128)S(1)}, f32[136,512]{1,0:T(8,128)S(1)}, u32[]{:S(2)}, u32[]{:S(2)}) %collective-permute-start.23) | collective-permute-done | bytes 278560 | tf_op jit(solution)/shard_map/ppermute | solution.py:622
  81.7 1.4 %collective-permute-start.24 = (f32[40,512]{1,0:T(8,128)S(1)}, f32[40,512]{1,0:T(8,128)S(1)}, u32[]{:S(2)}, u32[]{:S(2)}) collective-permute-start(f32[40,512]{1,0:T(8,128)S(1)} %get-tuple-element.303), channel_id=1, source_target_pairs={{0,2},{1,3},{2,0},{3,1},{4,6},{5,7},{6,4},{7,5},{8,10},{9,11},{10,... | collective-permute-start | bytes 245768 | tf_op jit(solution)/shard_map/ppermute | solution.py:622
  83.7 1.5 %collective-permute-start.33 = (f32[64,512]{1,0:T(8,128)S(1)}, f32[64,512]{1,0:T(8,128)S(1)}, u32[]{:S(2)}, u32[]{:S(2)}) collective-permute-start(f32[64,512]{1,0:T(8,128)S(1)} %lines_summed.2.refs_0_), channel_id=1, source_target_pairs={{0,1},{1,0},{2,3},{3,2},{4,5},{5,4},{6,7},{7,6},{8,9},{9,8},{10,11... | collective-permute-start | bytes 393224 | tf_op jit(solution)/shard_map/ppermute | solution.py:622
  85.2 2.9 %collective-permute-start.25 = (f32[40,512]{1,0:T(8,128)S(1)}, f32[40,512]{1,0:T(8,128)S(1)}, u32[]{:S(2)}, u32[]{:S(2)}) collective-permute-start(f32[40,512]{1,0:T(8,128)S(1)} %get-tuple-element.304), channel_id=1, source_target_pairs={{0,4},{1,5},{2,6},{3,7},{4,0},{5,1},{6,2},{7,3},{8,12},{9,13},{10,... | collective-permute-start | bytes 245768 | tf_op jit(solution)/shard_map/ppermute | solution.py:622
  88.0 1.5 %collective-permute-start.26 = (f32[40,512]{1,0:T(8,128)S(1)}, f32[40,512]{1,0:T(8,128)S(1)}, u32[]{:S(2)}, u32[]{:S(2)}) collective-permute-start(f32[40,512]{1,0:T(8,128)S(1)} %get-tuple-element.305), channel_id=1, source_target_pairs={{0,6},{1,7},{2,4},{3,5},{4,2},{5,3},{6,0},{7,1},{8,14},{9,15},{10,... | collective-permute-start | bytes 245768 | tf_op jit(solution)/shard_map/ppermute | solution.py:622
  89.5 1.6 %collective-permute-start.34 = (f32[64,512]{1,0:T(8,128)S(1)}, f32[64,512]{1,0:T(8,128)S(1)}, u32[]{:S(2)}, u32[]{:S(2)}) collective-permute-start(f32[64,512]{1,0:T(8,128)S(1)} %lines_summed.2.refs_0_), channel_id=1, source_target_pairs={{0,16},{1,17},{2,18},{3,19},{4,20},{5,21},{6,22},{7,23},{8,24},{9,... | collective-permute-start | bytes 393224 | tf_op jit(solution)/shard_map/ppermute | solution.py:622
  91.7 1.5 %collective-permute-done.25.refs_2_ = f32[40,512]{1,0:T(8,128)S(1)} collective-permute-done((f32[40,512]{1,0:T(8,128)S(1)}, f32[40,512]{1,0:T(8,128)S(1)}, u32[]{:S(2)}, u32[]{:S(2)}) %collective-permute-start.25) | collective-permute-done | bytes 81952 | tf_op jit(solution)/shard_map/ppermute | solution.py:622
  97.9 2.1 %collective-permute-start.29 = (f32[32,512]{1,0:T(8,128)S(1)}, f32[32,512]{1,0:T(8,128)S(1)}, u32[]{:S(2)}, u32[]{:S(2)}) collective-permute-start(f32[32,512]{1,0:T(8,128)S(1)} %get-tuple-element.309.refs_0_), channel_id=1, source_target_pairs={{0,6},{1,7},{2,4},{3,5},{4,2},{5,3},{6,0},{7,1},{8,14},{9,15},{10,... | collective-permute-start | bytes 196616 | tf_op jit(solution)/shard_map/ppermute | solution.py:622
  100.7 2.2 %collective-permute-done.28.refs_2_ = f32[32,512]{1,0:T(8,128)S(1)} collective-permute-done((f32[32,512]{1,0:T(8,128)S(1)}, f32[32,512]{1,0:T(8,128)S(1)}, u32[]{:S(2)}, u32[]{:S(2)}) %collective-permute-start.28) | collective-permute-done | bytes 65568 | tf_op jit(solution)/shard_map/ppermute | solution.py:622
  102.8 1.3 %collective-permute-done.29.refs_3_ = f32[32,512]{1,0:T(8,128)S(1)} collective-permute-done((f32[32,512]{1,0:T(8,128)S(1)}, f32[32,512]{1,0:T(8,128)S(1)}, u32[]{:S(2)}, u32[]{:S(2)}) %collective-permute-start.29) | collective-permute-done | bytes 65568 | tf_op jit(solution)/shard_map/ppermute | solution.py:622
  106.6 1.5 %collective-permute-start.37 = (f32[128,512]{1,0:T(8,128)S(1)}, f32[128,512]{1,0:T(8,128)S(1)}, u32[]{:S(2)}, u32[]{:S(2)}) collective-permute-start(f32[128,512]{1,0:T(8,128)S(1)} %get-tuple-element.800), channel_id=1, source_target_pairs={{0,16},{1,17},{2,18},{3,19},{4,20},{5,21},{6,22},{7,23},{8,24},{9,... | collective-permute-start | bytes 786440 | tf_op jit(solution)/shard_map/ppermute | solution.py:622
  109.3 2.0 %collective-permute-start.40 = (f32[64,512]{1,0:T(8,128)S(1)}, f32[64,512]{1,0:T(8,128)S(1)}, u32[]{:S(2)}, u32[]{:S(2)}) collective-permute-start(f32[64,512]{1,0:T(8,128)S(1)} %get-tuple-element.801), channel_id=1, source_target_pairs={{0,4},{1,5},{2,6},{3,7},{4,0},{5,1},{6,2},{7,3},{8,12},{9,13},{10,... | collective-permute-start | bytes 393224 | tf_op jit(solution)/shard_map/ppermute | solution.py:622
  111.5 2.1 %collective-permute-start.41 = (f32[64,512]{1,0:T(8,128)S(1)}, f32[64,512]{1,0:T(8,128)S(1)}, u32[]{:S(2)}, u32[]{:S(2)}) collective-permute-start(f32[64,512]{1,0:T(8,128)S(1)} %get-tuple-element.801), channel_id=1, source_target_pairs={{0,6},{1,7},{2,4},{3,5},{4,2},{5,3},{6,0},{7,1},{8,14},{9,15},{10,... | collective-permute-start | bytes 393224 | tf_op jit(solution)/shard_map/ppermute | solution.py:622
  113.6 5.0 %collective-permute-done.40.refs_6_ = f32[64,512]{1,0:T(8,128)S(1)} collective-permute-done((f32[64,512]{1,0:T(8,128)S(1)}, f32[64,512]{1,0:T(8,128)S(1)}, u32[]{:S(2)}, u32[]{:S(2)}) %collective-permute-start.40) | collective-permute-done | bytes 131104 | tf_op jit(solution)/shard_map/ppermute | solution.py:622
  121.2 1.7 %collective-permute-done.42.block = f32[768,512]{1,0:T(8,128)S(1)} collective-permute-done((f32[768,512]{1,0:T(8,128)S(1)}, f32[768,512]{1,0:T(8,128)S(1)}, u32[]{:S(2)}, u32[]{:S(2)}) %collective-permute-start.42) | collective-permute-done | bytes 1572896 | tf_op jit(solution)/shard_map/ppermute | solution.py:622
  (66 shorter events, 14.9 us)
Async XLA Ops:
  0.6 14.0 %copy-start.22 = (s32[2048]{0:T(1024)S(1)}, s32[2048]{0:T(1024)}, u32[]{:S(2)}) copy-start(s32[2048]{0:T(1024)} %param.16) | copy-start | bytes 24580
  0.6 14.0 %copy-start.24 = (s32[2048]{0:T(1024)S(1)}, s32[2048]{0:T(1024)}, u32[]{:S(2)}) copy-start(s32[2048]{0:T(1024)} %param.15) | copy-start | bytes 24580
  13.3 14.3 %collective-permute-start.18 = (f32[200,512]{1,0:T(8,128)S(1)}, f32[200,512]{1,0:T(8,128)S(1)}, u32[]{:S(2)}, u32[]{:S(2)}) collective-permute-start(f32[200,512]{1,0:T(8,128)S(1)} %get-tuple-element.286), channel_id=1, source_target_pairs={{1,0},{2,1},{3,2},{4,3},{5,4},{6,5},{7,6},{9,8},{10,9},{11,10},{12... | collective-permute-start | bytes 1228808 | tf_op jit(solution)/shard_map/ppermute | solution.py:731
  32.8 14.7 %collective-permute-start.19 = (f32[192,512]{1,0:T(8,128)S(1)}, f32[192,512]{1,0:T(8,128)S(1)}, u32[]{:S(2)}, u32[]{:S(2)}) collective-permute-start(f32[192,512]{1,0:T(8,128)S(1)} %get-tuple-element.289), channel_id=1, source_target_pairs={{0,1},{1,2},{2,3},{3,4},{4,5},{5,6},{6,7},{8,9},{9,10},{10,11},{11... | collective-permute-start | bytes 1179656 | tf_op jit(solution)/shard_map/ppermute | solution.py:731
  37.4 10.1 %copy-start = (bf16[2048,512]{1,0:T(8,128)(2,1)S(1)}, bf16[2048,512]{1,0:T(8,128)(2,1)}, u32[]{:S(2)}) copy-start(bf16[2048,512]{1,0:T(8,128)(2,1)} %x_ref.3) | copy-start | bytes 6291460
  37.4 10.1 %copy-start.8 = (bf16[2048,512]{1,0:T(8,128)(2,1)S(1)}, bf16[2048,512]{1,0:T(8,128)(2,1)}, u32[]{:S(2)}) copy-start(bf16[2048,512]{1,0:T(8,128)(2,1)} %get-tuple-element.285.indicator_ref.indicator) | copy-start | bytes 6291460
  37.4 10.1 %copy-start.9 = (f32[2048,512]{1,0:T(8,128)S(1)}, f32[2048,512]{1,0:T(8,128)}, u32[]{:S(2)}) copy-start(f32[2048,512]{1,0:T(8,128)} %get-tuple-element.295.slope_in) | copy-start | bytes 12582916
  37.4 10.1 %copy-start.10 = (f32[2048,512]{1,0:T(8,128)S(1)}, f32[2048,512]{1,0:T(8,128)}, u32[]{:S(2)}) copy-start(f32[2048,512]{1,0:T(8,128)} %get-tuple-element.293.slope_mid) | copy-start | bytes 12582916
  58.8 3.8 %collective-permute-start.20 = (f32[776,512]{1,0:T(8,128)}, f32[776,512]{1,0:T(8,128)}, u32[]{:S(2)}, u32[]{:S(2)}) collective-permute-start(f32[776,512]{1,0:T(8,128)} %get-tuple-element.297), channel_id=1, source_target_pairs={{0,8},{1,9},{2,10},{3,11},{4,12},{5,13},{6,14},{7,15},{8,0},{9,1},... | collective-permute-start | bytes 4767752 | tf_op jit(solution)/shard_map/ppermute | solution.py:622
  65.3 9.6 %collective-permute-start.21 = (f32[136,512]{1,0:T(8,128)S(1)}, f32[136,512]{1,0:T(8,128)S(1)}, u32[]{:S(2)}, u32[]{:S(2)}) collective-permute-start(f32[136,512]{1,0:T(8,128)S(1)} %get-tuple-element.299), channel_id=1, source_target_pairs={{0,1},{1,0},{2,3},{3,2},{4,5},{5,4},{6,7},{7,6},{8,9},{9,8},{10,11... | collective-permute-start | bytes 835592 | tf_op jit(solution)/shard_map/ppermute | solution.py:622
  66.9 13.4 %collective-permute-start.22 = (f32[136,512]{1,0:T(8,128)S(1)}, f32[136,512]{1,0:T(8,128)S(1)}, u32[]{:S(2)}, u32[]{:S(2)}) collective-permute-start(f32[136,512]{1,0:T(8,128)S(1)} %get-tuple-element.300), channel_id=1, source_target_pairs={{0,16},{1,17},{2,18},{3,19},{4,20},{5,21},{6,22},{7,23},{8,24},{9,... | collective-permute-start | bytes 835592 | tf_op jit(solution)/shard_map/ppermute | solution.py:622
  68.4 13.2 %collective-permute-start.23 = (f32[136,512]{1,0:T(8,128)S(1)}, f32[136,512]{1,0:T(8,128)S(1)}, u32[]{:S(2)}, u32[]{:S(2)}) collective-permute-start(f32[136,512]{1,0:T(8,128)S(1)} %get-tuple-element.301), channel_id=1, source_target_pairs={{0,17},{1,16},{2,19},{3,18},{4,21},{5,20},{6,23},{7,22},{8,25},{9,... | collective-permute-start | bytes 835592 | tf_op jit(solution)/shard_map/ppermute | solution.py:622
  69.0 14.1 %collective-permute-start.30 = (f32[64,512]{1,0:T(8,128)S(1)}, f32[64,512]{1,0:T(8,128)S(1)}, u32[]{:S(2)}, u32[]{:S(2)}) collective-permute-start(f32[64,512]{1,0:T(8,128)S(1)} %get-tuple-element.311), channel_id=1, source_target_pairs={{0,2},{1,3},{2,0},{3,1},{4,6},{5,7},{6,4},{7,5},{8,10},{9,11},{10,... | collective-permute-start | bytes 393224 | tf_op jit(solution)/shard_map/ppermute | solution.py:622
  70.7 12.3 %collective-permute-start.31 = (f32[64,512]{1,0:T(8,128)S(1)}, f32[64,512]{1,0:T(8,128)S(1)}, u32[]{:S(2)}, u32[]{:S(2)}) collective-permute-start(f32[64,512]{1,0:T(8,128)S(1)} %get-tuple-element.312), channel_id=1, source_target_pairs={{0,4},{1,5},{2,6},{3,7},{4,0},{5,1},{6,2},{7,3},{8,12},{9,13},{10,... | collective-permute-start | bytes 393224 | tf_op jit(solution)/shard_map/ppermute | solution.py:622
  74.9 8.2 %collective-permute-start.32 = (f32[64,512]{1,0:T(8,128)S(1)}, f32[64,512]{1,0:T(8,128)S(1)}, u32[]{:S(2)}, u32[]{:S(2)}) collective-permute-start(f32[64,512]{1,0:T(8,128)S(1)} %get-tuple-element.313), channel_id=1, source_target_pairs={{0,6},{1,7},{2,4},{3,5},{4,2},{5,3},{6,0},{7,1},{8,14},{9,15},{10,... | collective-permute-start | bytes 393224 | tf_op jit(solution)/shard_map/ppermute | solution.py:622
  81.7 9.5 %collective-permute-start.24 = (f32[40,512]{1,0:T(8,128)S(1)}, f32[40,512]{1,0:T(8,128)S(1)}, u32[]{:S(2)}, u32[]{:S(2)}) collective-permute-start(f32[40,512]{1,0:T(8,128)S(1)} %get-tuple-element.303), channel_id=1, source_target_pairs={{0,2},{1,3},{2,0},{3,1},{4,6},{5,7},{6,4},{7,5},{8,10},{9,11},{10,... | collective-permute-start | bytes 245768 | tf_op jit(solution)/shard_map/ppermute | solution.py:622
  83.7 14.3 %collective-permute-start.33 = (f32[64,512]{1,0:T(8,128)S(1)}, f32[64,512]{1,0:T(8,128)S(1)}, u32[]{:S(2)}, u32[]{:S(2)}) collective-permute-start(f32[64,512]{1,0:T(8,128)S(1)} %lines_summed.2.refs_0_), channel_id=1, source_target_pairs={{0,1},{1,0},{2,3},{3,2},{4,5},{5,4},{6,7},{7,6},{8,9},{9,8},{10,11... | collective-permute-start | bytes 393224 | tf_op jit(solution)/shard_map/ppermute | solution.py:622
  85.2 8.0 %collective-permute-start.25 = (f32[40,512]{1,0:T(8,128)S(1)}, f32[40,512]{1,0:T(8,128)S(1)}, u32[]{:S(2)}, u32[]{:S(2)}) collective-permute-start(f32[40,512]{1,0:T(8,128)S(1)} %get-tuple-element.304), channel_id=1, source_target_pairs={{0,4},{1,5},{2,6},{3,7},{4,0},{5,1},{6,2},{7,3},{8,12},{9,13},{10,... | collective-permute-start | bytes 245768 | tf_op jit(solution)/shard_map/ppermute | solution.py:622
  88.0 6.3 %collective-permute-start.26 = (f32[40,512]{1,0:T(8,128)S(1)}, f32[40,512]{1,0:T(8,128)S(1)}, u32[]{:S(2)}, u32[]{:S(2)}) collective-permute-start(f32[40,512]{1,0:T(8,128)S(1)} %get-tuple-element.305), channel_id=1, source_target_pairs={{0,6},{1,7},{2,4},{3,5},{4,2},{5,3},{6,0},{7,1},{8,14},{9,15},{10,... | collective-permute-start | bytes 245768 | tf_op jit(solution)/shard_map/ppermute | solution.py:622
  89.5 10.5 %collective-permute-start.34 = (f32[64,512]{1,0:T(8,128)S(1)}, f32[64,512]{1,0:T(8,128)S(1)}, u32[]{:S(2)}, u32[]{:S(2)}) collective-permute-start(f32[64,512]{1,0:T(8,128)S(1)} %lines_summed.2.refs_0_), channel_id=1, source_target_pairs={{0,16},{1,17},{2,18},{3,19},{4,20},{5,21},{6,22},{7,23},{8,24},{9,... | collective-permute-start | bytes 393224 | tf_op jit(solution)/shard_map/ppermute | solution.py:622
  91.1 8.9 %collective-permute-start.35 = (f32[64,512]{1,0:T(8,128)S(1)}, f32[64,512]{1,0:T(8,128)S(1)}, u32[]{:S(2)}, u32[]{:S(2)}) collective-permute-start(f32[64,512]{1,0:T(8,128)S(1)} %lines_summed.2.refs_0_), channel_id=1, source_target_pairs={{0,17},{1,16},{2,19},{3,18},{4,21},{5,20},{6,23},{7,22},{8,25},{9,... | collective-permute-start | bytes 393224 | tf_op jit(solution)/shard_map/ppermute | solution.py:622
  95.6 5.1 %collective-permute-start.27 = (f32[32,512]{1,0:T(8,128)S(1)}, f32[32,512]{1,0:T(8,128)S(1)}, u32[]{:S(2)}, u32[]{:S(2)}) collective-permute-start(f32[32,512]{1,0:T(8,128)S(1)} %get-tuple-element.309.refs_0_), channel_id=1, source_target_pairs={{0,2},{1,3},{2,0},{3,1},{4,6},{5,7},{6,4},{7,5},{8,10},{9,11},{10,... | collective-permute-start | bytes 196616 | tf_op jit(solution)/shard_map/ppermute | solution.py:622
  96.8 6.0 %collective-permute-start.28 = (f32[32,512]{1,0:T(8,128)S(1)}, f32[32,512]{1,0:T(8,128)S(1)}, u32[]{:S(2)}, u32[]{:S(2)}) collective-permute-start(f32[32,512]{1,0:T(8,128)S(1)} %get-tuple-element.309.refs_0_), channel_id=1, source_target_pairs={{0,4},{1,5},{2,6},{3,7},{4,0},{5,1},{6,2},{7,3},{8,12},{9,13},{10,... | collective-permute-start | bytes 196616 | tf_op jit(solution)/shard_map/ppermute | solution.py:622
  97.9 6.2 %collective-permute-start.29 = (f32[32,512]{1,0:T(8,128)S(1)}, f32[32,512]{1,0:T(8,128)S(1)}, u32[]{:S(2)}, u32[]{:S(2)}) collective-permute-start(f32[32,512]{1,0:T(8,128)S(1)} %get-tuple-element.309.refs_0_), channel_id=1, source_target_pairs={{0,6},{1,7},{2,4},{3,5},{4,2},{5,3},{6,0},{7,1},{8,14},{9,15},{10,... | collective-permute-start | bytes 196616 | tf_op jit(solution)/shard_map/ppermute | solution.py:622
  104.1 14.5 %copy-start.15 = (s32[2]{0:T(128)S(1)}, s32[2]{0:T(128)}, u32[]{:S(2)}) copy-start(s32[2]{0:T(128)} %copy-done.14) | copy-start | bytes 28
  105.0 6.4 %collective-permute-start.39 = (f32[64,512]{1,0:T(8,128)S(1)}, f32[64,512]{1,0:T(8,128)S(1)}, u32[]{:S(2)}, u32[]{:S(2)}) collective-permute-start(f32[64,512]{1,0:T(8,128)S(1)} %get-tuple-element.801), channel_id=1, source_target_pairs={{0,2},{1,3},{2,0},{3,1},{4,6},{5,7},{6,4},{7,5},{8,10},{9,11},{10,... | collective-permute-start | bytes 393224 | tf_op jit(solution)/shard_map/ppermute | solution.py:622
  105.8 12.8 %collective-permute-start.36 = (f32[128,512]{1,0:T(8,128)S(1)}, f32[128,512]{1,0:T(8,128)S(1)}, u32[]{:S(2)}, u32[]{:S(2)}) collective-permute-start(f32[128,512]{1,0:T(8,128)S(1)} %get-tuple-element.800), channel_id=1, source_target_pairs={{0,1},{1,0},{2,3},{3,2},{4,5},{5,4},{6,7},{7,6},{8,9},{9,8},{10,11... | collective-permute-start | bytes 786440 | tf_op jit(solution)/shard_map/ppermute | solution.py:622
  106.6 12.0 %collective-permute-start.37 = (f32[128,512]{1,0:T(8,128)S(1)}, f32[128,512]{1,0:T(8,128)S(1)}, u32[]{:S(2)}, u32[]{:S(2)}) collective-permute-start(f32[128,512]{1,0:T(8,128)S(1)} %get-tuple-element.800), channel_id=1, source_target_pairs={{0,16},{1,17},{2,18},{3,19},{4,20},{5,21},{6,22},{7,23},{8,24},{9,... | collective-permute-start | bytes 786440 | tf_op jit(solution)/shard_map/ppermute | solution.py:622
  108.1 10.5 %collective-permute-start.38 = (f32[128,512]{1,0:T(8,128)S(1)}, f32[128,512]{1,0:T(8,128)S(1)}, u32[]{:S(2)}, u32[]{:S(2)}) collective-permute-start(f32[128,512]{1,0:T(8,128)S(1)} %get-tuple-element.800), channel_id=1, source_target_pairs={{0,17},{1,16},{2,19},{3,18},{4,21},{5,20},{6,23},{7,22},{8,25},{9,... | collective-permute-start | bytes 786440 | tf_op jit(solution)/shard_map/ppermute | solution.py:622
  109.3 9.3 %collective-permute-start.40 = (f32[64,512]{1,0:T(8,128)S(1)}, f32[64,512]{1,0:T(8,128)S(1)}, u32[]{:S(2)}, u32[]{:S(2)}) collective-permute-start(f32[64,512]{1,0:T(8,128)S(1)} %get-tuple-element.801), channel_id=1, source_target_pairs={{0,4},{1,5},{2,6},{3,7},{4,0},{5,1},{6,2},{7,3},{8,12},{9,13},{10,... | collective-permute-start | bytes 393224 | tf_op jit(solution)/shard_map/ppermute | solution.py:622
  111.5 7.1 %collective-permute-start.41 = (f32[64,512]{1,0:T(8,128)S(1)}, f32[64,512]{1,0:T(8,128)S(1)}, u32[]{:S(2)}, u32[]{:S(2)}) collective-permute-start(f32[64,512]{1,0:T(8,128)S(1)} %get-tuple-element.801), channel_id=1, source_target_pairs={{0,6},{1,7},{2,4},{3,5},{4,2},{5,3},{6,0},{7,1},{8,14},{9,15},{10,... | collective-permute-start | bytes 393224 | tf_op jit(solution)/shard_map/ppermute | solution.py:622
  119.4 3.5 %collective-permute-start.42 = (f32[768,512]{1,0:T(8,128)S(1)}, f32[768,512]{1,0:T(8,128)S(1)}, u32[]{:S(2)}, u32[]{:S(2)}) collective-permute-start(f32[768,512]{1,0:T(8,128)S(1)} %collect_second.1.block), channel_id=1, source_target_pairs={{0,8},{1,9},{2,10},{3,11},{4,12},{5,13},{6,14},{7,15},{8,0},{9,1},... | collective-permute-start | bytes 4718600 | tf_op jit(solution)/shard_map/ppermute | solution.py:622
  (7 other events, 67.1 us)

commit v6 on v5

--- a/solution.py
+++ b/solution.py
@@ -163,11 +163,14 @@
         hit = iota((GROUP, tile), 0) + t * GROUP == rank
         place = jnp.max(jnp.where(hit, entry, 0.0), axis=1, keepdims=True)
         place = jnp.broadcast_to(place, (GROUP, LANES))
-        parts = [place[k : k + LANES, :].T[0:1] for k in range(0, GROUP, LANES)]
-        spot = (send.shape[0] - sent, GROUP)
+        if sent < GROUP:
+            place = jnp.concatenate([place[:sent]] * 2, axis=0)
+        width = place.shape[0]
+        parts = [place[k : k + LANES, :].T[0:1] for k in range(0, width, LANES)]
+        spot = (send.shape[0] - sent, width)
         place = jnp.broadcast_to(jnp.concatenate(parts, axis=1), spot)
         place = jnp.where(iota(spot, 0) == t, place, 0.0)
-        send[sent:, 0:GROUP] = jnp.maximum(send[sent:, 0:GROUP], place)
+        send[sent:, 0:width] = jnp.maximum(send[sent:, 0:width], place)
         at = group_rows(t, sent)
         hit = ones_where(hit)[: min(GROUP, sent)]
         send[at, :] += dot(twice(hit, tile), weight[...])
@@ -331,17 +334,17 @@
 
 def split_sum(source, parts, cap):
     sent = sent_rows(cap)
-    for t in range(cap // GROUP):
-        rows = min(GROUP, sent - t * GROUP)
-        value = source[t * GROUP : t * GROUP + rows, :]
-        if rows < GROUP:
-            value = jnp.concatenate([value, jnp.zeros((GROUP - rows, value.shape[1]), F32)], axis=0)
-        put_parts(parts, t, value)
-
-
-def group_sum(mask, parts, t):
+    group = min(GROUP, sent)
+    for t in range(sent // group):
+        put_parts(parts, t, source[t * group : (t + 1) * group, :])
+
+
+def group_sum(column, test, parts, cap, t):
+    sent = sent_rows(cap)
+    if sent < GROUP:
+        return dot(ones_where(test(widen(column, 2 * sent), 2 * sent)), parts[...])
     at = pl.ds(pl.multiple_of(t * 2 * GROUP, 2 * GROUP), 2 * GROUP)
-    return dot(twice(mask, GROUP), parts[at, :])
+    return dot(twice(ones_where(test(widen(column, GROUP), GROUP)), GROUP), parts[at, :])
 
 
 def hazard_kernel(
@@ -356,13 +359,15 @@
     def _():
         split_sum(got, parts, cap)
 
-    first = widen(as_column(first_ref[...]).astype(F32), GROUP)
+    first = as_column(first_ref[...]).astype(F32)
     divisor = risk[own, :]
     sent = sent_rows(cap)
 
     def beyond(t, total):
-        entry = got[pl.ds(sent + t, 1), 0:GROUP]
-        return total + group_sum(ones_where(entry <= first), parts, t)
+        def test(column, width):
+            return got[pl.ds(sent + t, 1), 0:width] <= column
+
+        return total + group_sum(first, test, parts, cap, t)
 
     divisor = lax.fori_loop(0, cap // GROUP, beyond, divisor)
     put_parts(hazard, step, indicator_ref[...].astype(F32) / divisor)
@@ -390,7 +395,7 @@
         ],
         out_specs=[whole(), whole()],
         out_shape=[pltpu.VMEM((2 * rows, width), BF16), like((sent_rows(cap), width), F32)],
-        scratch_shapes=[pltpu.VMEM((2 * cap, width), BF16)],
+        scratch_shapes=[pltpu.VMEM((2 * sent_rows(cap), width), BF16)],
         compiler_params=params(20),
         name="hazards",
     )(first, first, in_vmem(risk), in_hbm(indicator), got)
@@ -412,10 +417,17 @@
         grad_mid[...] = jnp.zeros_like(grad_mid)
         grad_out[...] = jnp.zeros_like(grad_out)
 
-    rank = widen(as_column(rank_ref[...]), GROUP)
+    rank = as_column(rank_ref[...])
+    sent = sent_rows(cap)
 
     def behind(t, total):
-        return total + group_sum(ones_where(rank == iota((tile, GROUP), 1) + t * GROUP), parts, t)
+        def test(column, width):
+            lane = iota((tile, width), 1)
+            if sent < GROUP:
+                lane = jnp.where(lane < sent, lane, lane - sent)
+            return column == lane + t * GROUP
+
+        return total + group_sum(rank, test, parts, cap, t)
 
     exposure = lax.fori_loop(0, cap // GROUP, behind, exposure_ref[own, :])
     part = tile // 2
@@ -476,7 +488,7 @@
             pltpu.HBM((rows, width), BF16), pltpu.HBM(halves, F32),
             jax.ShapeDtypeStruct(halves, F32),
         ],
-        scratch_shapes=[pltpu.VMEM((2 * cap, out_width), BF16)]
+        scratch_shapes=[pltpu.VMEM((2 * sent_rows(cap), out_width), BF16)]
         + [pltpu.VMEM(w.shape, F32) for w in weights],
         compiler_params=params(20),
         name="backward",
@@ -657,11 +669,10 @@
     a, b = line_hops(a), plane_hops([b] * plane)
     ((b,),) = spread([b], [(0, 0, size_b, 0, 0, 1)], none, "rest_summed")
     size_a = size_a // line
-    (a,), (note,), (flag,) = spread(
-        [a],
-        [(0, 0, size_a, 0, 0, 1), (0, size_a, tail, 0, 0, 1), (0, size_a + 1, 1, 0, 0, 0)],
-        none, "body_summed",
-    )
+    (a,), (note,) = spread(
+        [a], [(0, 0, size_a, 0, 0, 1), (0, size_a, tail, 0, 0, 1)], none, "body_summed"
+    )
+    ((flag,),) = spread([[note]], [(0, 1, 1, 0, 0, 0)], none, "flag")
     (a,) = collect(
         [(line_hops([a] * line), 0, 0)], [body // plane], in_line.reshape(1), "collect_first"
     )

time: 125 us -> 125 us (level)
  Pallas kernels: 57.2 us -> 59 us
  waiting for transfers between devices: 25.7 us -> 24 us
    ppermute x23, waiting for transfers between devices: 22.7 us -> 21.4 us  [hop(): return lax.ppermute(block, ('strata', 'chain'), route)]
    pallas_call x5 -> x6, Pallas kernels: 5.16 us -> 6.48 us  [spread(): pl.pallas_call(partial(spread_kernel, [len(term) for term in terms], stre...]
  transfers between devices with their start and end apart: 25 -> 25, of which waited for: 12 -> 12; matrix products, arithmetic and copies ran while one was open for 1% -> 1% of each run, Pallas kernels for 19% -> 21%
where the time goes in v6:
time: 125 us; the launch traced here: 124 us
  Pallas kernels  59 us (47%)
  starting transfers between devices  37.4 us (30%)
  waiting for transfers between devices  24 us (19%)
  other arithmetic  1.38 us (1%)
    ppermute x23, starting transfers between devices, hop(): return lax.ppermute(block, ('strata', 'chain'), route)  31.5 us
    ppermute x23, waiting for transfers between devices, hop(): return lax.ppermute(block, ('strata', 'chain'), route)  21.4 us
    pallas_call x1, Pallas kernels, trunk(): pl.pallas_call(partial(trunk_kernel, cap), grid=(rows // TILE,), in_specs...  12.6 us
    pallas_call x1, Pallas kernels, backward(): pl.pallas_call(partial(backward_kernel, cap, factor), grid=(rows // TILE,...  11.1 us
    pallas_call x1, Pallas kernels, own_exposure(): pl.pallas_call(own_exposure_kernel, grid=(rows // TILE,), in_specs=[pl.Bl...  10.3 us
    pallas_call x1, Pallas kernels, own_risk(): pl.pallas_call(own_risk_kernel, grid=(rows // TILE,), in_specs=[pl.BlockS...  10.2 us
    pallas_call x6, Pallas kernels, spread(): pl.pallas_call(partial(spread_kernel, [len(term) for term in terms], stre...  6.48 us
    ppermute x2, starting transfers between devices, from_behind(): return lax.ppermute(block, axis, route)  5.85 us
  transfers between devices with their start and end apart: 25, of which 12 were waited for; matrix products, arithmetic and copies ran while one was open for 1% of the time, Pallas kernels for 21%

profile of v6, /device:TPU:0, one launch (start us, length us, event | category | flops | bytes accessed | tf_op | source)
XLA Modules:
  0.0 124.1 jit_solution(3640489297428009114)
XLA Ops:
  0.7 12.6 %trunk.6 = (bf16[2048,512]{1,0:T(8,128)(2,1)}, bf16[2048,512]{1,0:T(8,128)(2,1)}, f32[2048,512]{1,0:T(8,128)}, f32[2048,512]{1,0:T(8,128)}, bf16[2048,512]{1,0:T...) custom-call(s32[1]{0:T(128)} %bitcast.3.block_start, ...), custom_call_target="tpu_custom_call" | custom-call | tf_op jit(solution)/shard_map/trunk/pallas_call | solution.py:196
  13.2 1.3 %collective-permute-start.18 = (f32[200,512]{1,0:T(8,128)S(1)}, f32[200,512]{1,0:T(8,128)S(1)}, u32[]{:S(2)}, u32[]{:S(2)}) collective-permute-start(f32[200,512]{1,0:T(8,128)S(1)} %get-tuple-element.281), channel_id=1, source_target_pairs={{1,0},{2,1},{3,2},{4,3},{5,4},{6,5},{7,6},{9,8},{10,9},{11,10},{12... | collective-permute-start | bytes 1228808 | tf_op jit(solution)/shard_map/ppermute | solution.py:742
  14.7 10.2 %own_risk.2.risk = f32[2048,512]{1,0:T(8,128)S(1)} custom-call(s32[16]{0:T(128)S(1)} %slice.9.starts, s32[1,2048]{1,0:T(1,128)S(1)} %bitcast.37, s32[1,2048]{1,0:T(1,128)S(1)} %bitcast.33, bf16[4096,512]{1,0:T(8,128)(2,1)} %get-tuple-element.279.weight), custom_call_target="tpu_custom_call" | custom-call | flops 8589934592 | bytes 33554432 | tf_op jit(solution)/shard_map/own_risk/pallas_call | solution.py:263
  24.9 2.6 %collective-permute-done.18.got = f32[200,512]{1,0:T(8,128)S(1)} collective-permute-done((f32[200,512]{1,0:T(8,128)S(1)}, f32[200,512]{1,0:T(8,128)S(1)}, u32[]{:S(2)}, u32[]{:S(2)}) %collective-permute-start.18) | collective-permute-done | bytes 409632 | tf_op jit(solution)/shard_map/ppermute | solution.py:742
  27.5 5.2 %hazards.6 = (bf16[4096,512]{1,0:T(8,128)(2,1)S(1)}, f32[192,512]{1,0:T(8,128)S(1)}) custom-call(s32[1,2048]{1,0:T(1,128)S(1)} %bitcast.34, s32[1,2048]{1,0:T(1,128)S(1)} %bitcast.35, f32[2048,512]{1,0:T(8,128)S(1)} %own_risk.2.risk, bf16[2048,512]{1,0:T(8,128)(2,1)} %get-tuple-element.280.indicator_ref.indicator, f32[200,512]{1,0:T(8,128)S(1)} %collective-permute-done.18.got), custom_call_target="tpu_custom_call" | custom-call | tf_op jit(solution)/shard_map/hazards/pallas_call | solution.py:390
  32.7 4.6 %collective-permute-start.19 = (f32[192,512]{1,0:T(8,128)S(1)}, f32[192,512]{1,0:T(8,128)S(1)}, u32[]{:S(2)}, u32[]{:S(2)}) collective-permute-start(f32[192,512]{1,0:T(8,128)S(1)} %get-tuple-element.284), channel_id=1, source_target_pairs={{0,1},{1,2},{2,3},{3,4},{4,5},{5,6},{6,7},{8,9},{9,10},{10,11},{11... | collective-permute-start | bytes 1179656 | tf_op jit(solution)/shard_map/ppermute | solution.py:742
  37.4 10.3 %own_exposure.6 = (f32[2048,512]{1,0:T(8,128)S(1)}, f32[8,512]{1,0:T(8,128)S(1)}) custom-call(s32[16]{0:T(128)S(1)} %slice.9.starts, s32[1,2048]{1,0:T(1,128)S(1)} %bitcast.36, s32[1,2048]{1,0:T(1,128)S(1)} %bitcast.38, bf16[4096,512]{1,0:T(8,128)(2,1)S(1)} %get-tuple-element.282.hazard), custom_call_target="tpu_custom_call" | custom-call | flops 8589934592 | bytes 33554432 | tf_op jit(solution)/shard_map/own_exposure/pallas_call | solution.py:321
  47.9 11.1 %backward.6 = (bf16[2048,512]{1,0:T(8,128)(2,1)}, f32[776,512]{1,0:T(8,128)}, f32[776,512]{1,0:T(8,128)}) custom-call(s32[1]{0:T(128)} %bitcast.2.half, s32[1,2048]{1,0:T(1,128)S(1)} %get-tuple-element.278.rank_ref, f32[2048,512]{1,0:T(8,128)S(1)} %get-tuple-element.283.exposure_ref, f32[192,512]{1,0:T(8,128)S(1)} %collective-permute-done.19.got, ...), custom_call_target="tpu_custom_call" | custom-call | tf_op jit(solution)/shard_map/backward/pallas_call | solution.py:480
  59.1 3.7 %collective-permute-done.20.refs_1_ = f32[776,512]{1,0:T(8,128)} collective-permute-done((f32[776,512]{1,0:T(8,128)}, f32[776,512]{1,0:T(8,128)}, u32[]{:S(2)}, u32[]{:S(2)}) %collective-permute-start.20) | collective-permute-done | bytes 1589280 | tf_op jit(solution)/shard_map/ppermute | solution.py:634
  62.8 2.7 %spread_first.6 = (f32[136,512]{1,0:T(8,128)S(1)}, f32[136,512]{1,0:T(8,128)S(1)}, f32[136,512]{1,0:T(8,128)S(1)}, f32[136,512]{1,0:T(8,128)S(1)}, f32[64,512]{1...) custom-call(s32[2]{0:T(128)S(1)} %pad_add_fusion.1.me, ...), custom_call_target="tpu_custom_call" | custom-call | tf_op jit(solution)/shard_map/spread_first/pallas_call | solution.py:568
  65.5 1.6 %collective-permute-start.21 = (f32[136,512]{1,0:T(8,128)S(1)}, f32[136,512]{1,0:T(8,128)S(1)}, u32[]{:S(2)}, u32[]{:S(2)}) collective-permute-start(f32[136,512]{1,0:T(8,128)S(1)} %get-tuple-element.294), channel_id=1, source_target_pairs={{0,1},{1,0},{2,3},{3,2},{4,5},{5,4},{6,7},{7,6},{8,9},{9,8},{10,11... | collective-permute-start | bytes 835592 | tf_op jit(solution)/shard_map/ppermute | solution.py:634
  67.1 1.8 %collective-permute-start.22 = (f32[136,512]{1,0:T(8,128)S(1)}, f32[136,512]{1,0:T(8,128)S(1)}, u32[]{:S(2)}, u32[]{:S(2)}) collective-permute-start(f32[136,512]{1,0:T(8,128)S(1)} %get-tuple-element.295), channel_id=1, source_target_pairs={{0,16},{1,17},{2,18},{3,19},{4,20},{5,21},{6,22},{7,23},{8,24},{9,... | collective-permute-start | bytes 835592 | tf_op jit(solution)/shard_map/ppermute | solution.py:634
  69.1 1.5 %collective-permute-start.30 = (f32[64,512]{1,0:T(8,128)S(1)}, f32[64,512]{1,0:T(8,128)S(1)}, u32[]{:S(2)}, u32[]{:S(2)}) collective-permute-start(f32[64,512]{1,0:T(8,128)S(1)} %get-tuple-element.305), channel_id=1, source_target_pairs={{0,2},{1,3},{2,0},{3,1},{4,6},{5,7},{6,4},{7,5},{8,10},{9,11},{10,... | collective-permute-start | bytes 393224 | tf_op jit(solution)/shard_map/ppermute | solution.py:634
  70.6 1.8 %collective-permute-start.31 = (f32[64,512]{1,0:T(8,128)S(1)}, f32[64,512]{1,0:T(8,128)S(1)}, u32[]{:S(2)}, u32[]{:S(2)}) collective-permute-start(f32[64,512]{1,0:T(8,128)S(1)} %get-tuple-element.306), channel_id=1, source_target_pairs={{0,4},{1,5},{2,6},{3,7},{4,0},{5,1},{6,2},{7,3},{8,12},{9,13},{10,... | collective-permute-start | bytes 393224 | tf_op jit(solution)/shard_map/ppermute | solution.py:634
  72.5 2.7 %collective-permute-done.21.refs_1_ = f32[136,512]{1,0:T(8,128)S(1)} collective-permute-done((f32[136,512]{1,0:T(8,128)S(1)}, f32[136,512]{1,0:T(8,128)S(1)}, u32[]{:S(2)}, u32[]{:S(2)}) %collective-permute-start.21) | collective-permute-done | bytes 278560 | tf_op jit(solution)/shard_map/ppermute | solution.py:634
  75.1 2.8 %collective-permute-start.32 = (f32[64,512]{1,0:T(8,128)S(1)}, f32[64,512]{1,0:T(8,128)S(1)}, u32[]{:S(2)}, u32[]{:S(2)}) collective-permute-start(f32[64,512]{1,0:T(8,128)S(1)} %get-tuple-element.307), channel_id=1, source_target_pairs={{0,6},{1,7},{2,4},{3,5},{4,2},{5,3},{6,0},{7,1},{8,14},{9,15},{10,... | collective-permute-start | bytes 393224 | tf_op jit(solution)/shard_map/ppermute | solution.py:634
  77.9 2.9 %collective-permute-done.22.refs_2_ = f32[136,512]{1,0:T(8,128)S(1)} collective-permute-done((f32[136,512]{1,0:T(8,128)S(1)}, f32[136,512]{1,0:T(8,128)S(1)}, u32[]{:S(2)}, u32[]{:S(2)}) %collective-permute-start.22) | collective-permute-done | bytes 278560 | tf_op jit(solution)/shard_map/ppermute | solution.py:634
  81.6 1.6 %collective-permute-start.24 = (f32[40,512]{1,0:T(8,128)S(1)}, f32[40,512]{1,0:T(8,128)S(1)}, u32[]{:S(2)}, u32[]{:S(2)}) collective-permute-start(f32[40,512]{1,0:T(8,128)S(1)} %get-tuple-element.298), channel_id=1, source_target_pairs={{0,2},{1,3},{2,0},{3,1},{4,6},{5,7},{6,4},{7,5},{8,10},{9,11},{10,... | collective-permute-start | bytes 245768 | tf_op jit(solution)/shard_map/ppermute | solution.py:634
  84.8 3.1 %collective-permute-start.25 = (f32[40,512]{1,0:T(8,128)S(1)}, f32[40,512]{1,0:T(8,128)S(1)}, u32[]{:S(2)}, u32[]{:S(2)}) collective-permute-start(f32[40,512]{1,0:T(8,128)S(1)} %get-tuple-element.299), channel_id=1, source_target_pairs={{0,4},{1,5},{2,6},{3,7},{4,0},{5,1},{6,2},{7,3},{8,12},{9,13},{10,... | collective-permute-start | bytes 245768 | tf_op jit(solution)/shard_map/ppermute | solution.py:634
  87.9 1.4 %collective-permute-start.26 = (f32[40,512]{1,0:T(8,128)S(1)}, f32[40,512]{1,0:T(8,128)S(1)}, u32[]{:S(2)}, u32[]{:S(2)}) collective-permute-start(f32[40,512]{1,0:T(8,128)S(1)} %get-tuple-element.300), channel_id=1, source_target_pairs={{0,6},{1,7},{2,4},{3,5},{4,2},{5,3},{6,0},{7,1},{8,14},{9,15},{10,... | collective-permute-start | bytes 245768 | tf_op jit(solution)/shard_map/ppermute | solution.py:634
  89.2 1.6 %collective-permute-start.34 = (f32[64,512]{1,0:T(8,128)S(1)}, f32[64,512]{1,0:T(8,128)S(1)}, u32[]{:S(2)}, u32[]{:S(2)}) collective-permute-start(f32[64,512]{1,0:T(8,128)S(1)} %lines_summed.2.refs_0_), channel_id=1, source_target_pairs={{0,16},{1,17},{2,18},{3,19},{4,20},{5,21},{6,22},{7,23},{8,24},{9,... | collective-permute-start | bytes 393224 | tf_op jit(solution)/shard_map/ppermute | solution.py:634
  91.6 1.4 %collective-permute-done.25.refs_2_ = f32[40,512]{1,0:T(8,128)S(1)} collective-permute-done((f32[40,512]{1,0:T(8,128)S(1)}, f32[40,512]{1,0:T(8,128)S(1)}, u32[]{:S(2)}, u32[]{:S(2)}) %collective-permute-start.25) | collective-permute-done | bytes 81952 | tf_op jit(solution)/shard_map/ppermute | solution.py:634
  93.0 1.2 collective-permute-done.26.refs_3_
  97.6 2.1 %collective-permute-start.29 = (f32[32,512]{1,0:T(8,128)S(1)}, f32[32,512]{1,0:T(8,128)S(1)}, u32[]{:S(2)}, u32[]{:S(2)}) collective-permute-start(f32[32,512]{1,0:T(8,128)S(1)} %get-tuple-element.303.refs_0_), channel_id=1, source_target_pairs={{0,6},{1,7},{2,4},{3,5},{4,2},{5,3},{6,0},{7,1},{8,14},{9,15},{10,... | collective-permute-start | bytes 196616 | tf_op jit(solution)/shard_map/ppermute | solution.py:634
  100.3 1.4 %flag.6 = s32[1]{0:T(128)} custom-call(s32[3]{0:T(128)S(1)} %broadcast_3_me.2.me, f32[8,512]{1,0:T(8,128)} %get-tuple-element.570.refs_0_), custom_call_target="tpu_custom_call" | custom-call | tf_op jit(solution)/shard_map/flag/pallas_call | solution.py:568
  102.6 1.2 collective-permute-done.29.refs_3_
  106.3 1.4 %collective-permute-start.37 = (f32[128,512]{1,0:T(8,128)S(1)}, f32[128,512]{1,0:T(8,128)S(1)}, u32[]{:S(2)}, u32[]{:S(2)}) collective-permute-start(f32[128,512]{1,0:T(8,128)S(1)} %get-tuple-element.790), channel_id=1, source_target_pairs={{0,16},{1,17},{2,18},{3,19},{4,20},{5,21},{6,22},{7,23},{8,24},{9,... | collective-permute-start | bytes 786440 | tf_op jit(solution)/shard_map/ppermute | solution.py:634
  107.7 1.3 %collective-permute-start.38 = (f32[128,512]{1,0:T(8,128)S(1)}, f32[128,512]{1,0:T(8,128)S(1)}, u32[]{:S(2)}, u32[]{:S(2)}) collective-permute-start(f32[128,512]{1,0:T(8,128)S(1)} %get-tuple-element.790), channel_id=1, source_target_pairs={{0,17},{1,16},{2,19},{3,18},{4,21},{5,20},{6,23},{7,22},{8,25},{9,... | collective-permute-start | bytes 786440 | tf_op jit(solution)/shard_map/ppermute | solution.py:634
  109.0 1.8 %collective-permute-start.40 = (f32[64,512]{1,0:T(8,128)S(1)}, f32[64,512]{1,0:T(8,128)S(1)}, u32[]{:S(2)}, u32[]{:S(2)}) collective-permute-start(f32[64,512]{1,0:T(8,128)S(1)} %get-tuple-element.791), channel_id=1, source_target_pairs={{0,4},{1,5},{2,6},{3,7},{4,0},{5,1},{6,2},{7,3},{8,12},{9,13},{10,... | collective-permute-start | bytes 393224 | tf_op jit(solution)/shard_map/ppermute | solution.py:634
  111.0 1.9 %collective-permute-start.41 = (f32[64,512]{1,0:T(8,128)S(1)}, f32[64,512]{1,0:T(8,128)S(1)}, u32[]{:S(2)}, u32[]{:S(2)}) collective-permute-start(f32[64,512]{1,0:T(8,128)S(1)} %get-tuple-element.791), channel_id=1, source_target_pairs={{0,6},{1,7},{2,4},{3,5},{4,2},{5,3},{6,0},{7,1},{8,14},{9,15},{10,... | collective-permute-start | bytes 393224 | tf_op jit(solution)/shard_map/ppermute | solution.py:634
  112.9 5.6 %collective-permute-done.40.refs_6_ = f32[64,512]{1,0:T(8,128)S(1)} collective-permute-done((f32[64,512]{1,0:T(8,128)S(1)}, f32[64,512]{1,0:T(8,128)S(1)}, u32[]{:S(2)}, u32[]{:S(2)}) %collective-permute-start.40) | collective-permute-done | bytes 131104 | tf_op jit(solution)/shard_map/ppermute | solution.py:634
  119.3 1.3 %slice_multiply_fusion = f32[1,512]{1,0:T(1,128)} fusion(f32[8,512]{1,0:T(8,128)} %get-tuple-element.788), kind=kLoop, calls=%fused_computation.5 | loop fusion | flops 512 | bytes 4096 | tf_op jit(solution)/shard_map/div | solution.py:796
  (67 shorter events, 15.2 us)
Async XLA Ops:
  0.6 13.9 %copy-start.22 = (s32[2048]{0:T(1024)S(1)}, s32[2048]{0:T(1024)}, u32[]{:S(2)}) copy-start(s32[2048]{0:T(1024)} %param.16) | copy-start | bytes 24580
  0.6 13.9 %copy-start.24 = (s32[2048]{0:T(1024)S(1)}, s32[2048]{0:T(1024)}, u32[]{:S(2)}) copy-start(s32[2048]{0:T(1024)} %param.15) | copy-start | bytes 24580
  13.2 14.3 %collective-permute-start.18 = (f32[200,512]{1,0:T(8,128)S(1)}, f32[200,512]{1,0:T(8,128)S(1)}, u32[]{:S(2)}, u32[]{:S(2)}) collective-permute-start(f32[200,512]{1,0:T(8,128)S(1)} %get-tuple-element.281), channel_id=1, source_target_pairs={{1,0},{2,1},{3,2},{4,3},{5,4},{6,5},{7,6},{9,8},{10,9},{11,10},{12... | collective-permute-start | bytes 1228808 | tf_op jit(solution)/shard_map/ppermute | solution.py:742
  32.7 15.0 %collective-permute-start.19 = (f32[192,512]{1,0:T(8,128)S(1)}, f32[192,512]{1,0:T(8,128)S(1)}, u32[]{:S(2)}, u32[]{:S(2)}) collective-permute-start(f32[192,512]{1,0:T(8,128)S(1)} %get-tuple-element.284), channel_id=1, source_target_pairs={{0,1},{1,2},{2,3},{3,4},{4,5},{5,6},{6,7},{8,9},{9,10},{10,11},{11... | collective-permute-start | bytes 1179656 | tf_op jit(solution)/shard_map/ppermute | solution.py:742
  37.3 10.5 %copy-start = (bf16[2048,512]{1,0:T(8,128)(2,1)S(1)}, bf16[2048,512]{1,0:T(8,128)(2,1)}, u32[]{:S(2)}) copy-start(bf16[2048,512]{1,0:T(8,128)(2,1)} %x_ref.3) | copy-start | bytes 6291460
  37.3 10.5 %copy-start.8 = (bf16[2048,512]{1,0:T(8,128)(2,1)S(1)}, bf16[2048,512]{1,0:T(8,128)(2,1)}, u32[]{:S(2)}) copy-start(bf16[2048,512]{1,0:T(8,128)(2,1)} %get-tuple-element.280.indicator_ref.indicator) | copy-start | bytes 6291460
  37.3 10.5 %copy-start.9 = (f32[2048,512]{1,0:T(8,128)S(1)}, f32[2048,512]{1,0:T(8,128)}, u32[]{:S(2)}) copy-start(f32[2048,512]{1,0:T(8,128)} %get-tuple-element.290.slope_in) | copy-start | bytes 12582916
  37.3 10.5 %copy-start.10 = (f32[2048,512]{1,0:T(8,128)S(1)}, f32[2048,512]{1,0:T(8,128)}, u32[]{:S(2)}) copy-start(f32[2048,512]{1,0:T(8,128)} %get-tuple-element.288.slope_mid) | copy-start | bytes 12582916
  59.0 3.8 %collective-permute-start.20 = (f32[776,512]{1,0:T(8,128)}, f32[776,512]{1,0:T(8,128)}, u32[]{:S(2)}, u32[]{:S(2)}) collective-permute-start(f32[776,512]{1,0:T(8,128)} %get-tuple-element.292), channel_id=1, source_target_pairs={{0,8},{1,9},{2,10},{3,11},{4,12},{5,13},{6,14},{7,15},{8,0},{9,1},... | collective-permute-start | bytes 4767752 | tf_op jit(solution)/shard_map/ppermute | solution.py:634
  65.5 9.6 %collective-permute-start.21 = (f32[136,512]{1,0:T(8,128)S(1)}, f32[136,512]{1,0:T(8,128)S(1)}, u32[]{:S(2)}, u32[]{:S(2)}) collective-permute-start(f32[136,512]{1,0:T(8,128)S(1)} %get-tuple-element.294), channel_id=1, source_target_pairs={{0,1},{1,0},{2,3},{3,2},{4,5},{5,4},{6,7},{7,6},{8,9},{9,8},{10,11... | collective-permute-start | bytes 835592 | tf_op jit(solution)/shard_map/ppermute | solution.py:634
  67.1 13.7 %collective-permute-start.22 = (f32[136,512]{1,0:T(8,128)S(1)}, f32[136,512]{1,0:T(8,128)S(1)}, u32[]{:S(2)}, u32[]{:S(2)}) collective-permute-start(f32[136,512]{1,0:T(8,128)S(1)} %get-tuple-element.295), channel_id=1, source_target_pairs={{0,16},{1,17},{2,18},{3,19},{4,20},{5,21},{6,22},{7,23},{8,24},{9,... | collective-permute-start | bytes 835592 | tf_op jit(solution)/shard_map/ppermute | solution.py:634
  68.9 12.6 %collective-permute-start.23 = (f32[136,512]{1,0:T(8,128)S(1)}, f32[136,512]{1,0:T(8,128)S(1)}, u32[]{:S(2)}, u32[]{:S(2)}) collective-permute-start(f32[136,512]{1,0:T(8,128)S(1)} %get-tuple-element.296), channel_id=1, source_target_pairs={{0,17},{1,16},{2,19},{3,18},{4,21},{5,20},{6,23},{7,22},{8,25},{9,... | collective-permute-start | bytes 835592 | tf_op jit(solution)/shard_map/ppermute | solution.py:634
  69.1 14.1 %collective-permute-start.30 = (f32[64,512]{1,0:T(8,128)S(1)}, f32[64,512]{1,0:T(8,128)S(1)}, u32[]{:S(2)}, u32[]{:S(2)}) collective-permute-start(f32[64,512]{1,0:T(8,128)S(1)} %get-tuple-element.305), channel_id=1, source_target_pairs={{0,2},{1,3},{2,0},{3,1},{4,6},{5,7},{6,4},{7,5},{8,10},{9,11},{10,... | collective-permute-start | bytes 393224 | tf_op jit(solution)/shard_map/ppermute | solution.py:634
  70.6 12.6 %collective-permute-start.31 = (f32[64,512]{1,0:T(8,128)S(1)}, f32[64,512]{1,0:T(8,128)S(1)}, u32[]{:S(2)}, u32[]{:S(2)}) collective-permute-start(f32[64,512]{1,0:T(8,128)S(1)} %get-tuple-element.306), channel_id=1, source_target_pairs={{0,4},{1,5},{2,6},{3,7},{4,0},{5,1},{6,2},{7,3},{8,12},{9,13},{10,... | collective-permute-start | bytes 393224 | tf_op jit(solution)/shard_map/ppermute | solution.py:634
  75.1 8.1 %collective-permute-start.32 = (f32[64,512]{1,0:T(8,128)S(1)}, f32[64,512]{1,0:T(8,128)S(1)}, u32[]{:S(2)}, u32[]{:S(2)}) collective-permute-start(f32[64,512]{1,0:T(8,128)S(1)} %get-tuple-element.307), channel_id=1, source_target_pairs={{0,6},{1,7},{2,4},{3,5},{4,2},{5,3},{6,0},{7,1},{8,14},{9,15},{10,... | collective-permute-start | bytes 393224 | tf_op jit(solution)/shard_map/ppermute | solution.py:634
  81.6 9.3 %collective-permute-start.24 = (f32[40,512]{1,0:T(8,128)S(1)}, f32[40,512]{1,0:T(8,128)S(1)}, u32[]{:S(2)}, u32[]{:S(2)}) collective-permute-start(f32[40,512]{1,0:T(8,128)S(1)} %get-tuple-element.298), channel_id=1, source_target_pairs={{0,2},{1,3},{2,0},{3,1},{4,6},{5,7},{6,4},{7,5},{8,10},{9,11},{10,... | collective-permute-start | bytes 245768 | tf_op jit(solution)/shard_map/ppermute | solution.py:634
  83.8 13.8 %collective-permute-start.33 = (f32[64,512]{1,0:T(8,128)S(1)}, f32[64,512]{1,0:T(8,128)S(1)}, u32[]{:S(2)}, u32[]{:S(2)}) collective-permute-start(f32[64,512]{1,0:T(8,128)S(1)} %lines_summed.2.refs_0_), channel_id=1, source_target_pairs={{0,1},{1,0},{2,3},{3,2},{4,5},{5,4},{6,7},{7,6},{8,9},{9,8},{10,11... | collective-permute-start | bytes 393224 | tf_op jit(solution)/shard_map/ppermute | solution.py:634
  84.8 8.2 %collective-permute-start.25 = (f32[40,512]{1,0:T(8,128)S(1)}, f32[40,512]{1,0:T(8,128)S(1)}, u32[]{:S(2)}, u32[]{:S(2)}) collective-permute-start(f32[40,512]{1,0:T(8,128)S(1)} %get-tuple-element.299), channel_id=1, source_target_pairs={{0,4},{1,5},{2,6},{3,7},{4,0},{5,1},{6,2},{7,3},{8,12},{9,13},{10,... | collective-permute-start | bytes 245768 | tf_op jit(solution)/shard_map/ppermute | solution.py:634
  87.9 6.3 %collective-permute-start.26 = (f32[40,512]{1,0:T(8,128)S(1)}, f32[40,512]{1,0:T(8,128)S(1)}, u32[]{:S(2)}, u32[]{:S(2)}) collective-permute-start(f32[40,512]{1,0:T(8,128)S(1)} %get-tuple-element.300), channel_id=1, source_target_pairs={{0,6},{1,7},{2,4},{3,5},{4,2},{5,3},{6,0},{7,1},{8,14},{9,15},{10,... | collective-permute-start | bytes 245768 | tf_op jit(solution)/shard_map/ppermute | solution.py:634
  89.2 10.5 %collective-permute-start.34 = (f32[64,512]{1,0:T(8,128)S(1)}, f32[64,512]{1,0:T(8,128)S(1)}, u32[]{:S(2)}, u32[]{:S(2)}) collective-permute-start(f32[64,512]{1,0:T(8,128)S(1)} %lines_summed.2.refs_0_), channel_id=1, source_target_pairs={{0,16},{1,17},{2,18},{3,19},{4,20},{5,21},{6,22},{7,23},{8,24},{9,... | collective-permute-start | bytes 393224 | tf_op jit(solution)/shard_map/ppermute | solution.py:634
  90.9 8.9 %collective-permute-start.35 = (f32[64,512]{1,0:T(8,128)S(1)}, f32[64,512]{1,0:T(8,128)S(1)}, u32[]{:S(2)}, u32[]{:S(2)}) collective-permute-start(f32[64,512]{1,0:T(8,128)S(1)} %lines_summed.2.refs_0_), channel_id=1, source_target_pairs={{0,17},{1,16},{2,19},{3,18},{4,21},{5,20},{6,23},{7,22},{8,25},{9,... | collective-permute-start | bytes 393224 | tf_op jit(solution)/shard_map/ppermute | solution.py:634
  95.4 6.4 %collective-permute-start.27 = (f32[32,512]{1,0:T(8,128)S(1)}, f32[32,512]{1,0:T(8,128)S(1)}, u32[]{:S(2)}, u32[]{:S(2)}) collective-permute-start(f32[32,512]{1,0:T(8,128)S(1)} %get-tuple-element.303.refs_0_), channel_id=1, source_target_pairs={{0,2},{1,3},{2,0},{3,1},{4,6},{5,7},{6,4},{7,5},{8,10},{9,11},{10,... | collective-permute-start | bytes 196616 | tf_op jit(solution)/shard_map/ppermute | solution.py:634
  96.4 6.1 %collective-permute-start.28 = (f32[32,512]{1,0:T(8,128)S(1)}, f32[32,512]{1,0:T(8,128)S(1)}, u32[]{:S(2)}, u32[]{:S(2)}) collective-permute-start(f32[32,512]{1,0:T(8,128)S(1)} %get-tuple-element.303.refs_0_), channel_id=1, source_target_pairs={{0,4},{1,5},{2,6},{3,7},{4,0},{5,1},{6,2},{7,3},{8,12},{9,13},{10,... | collective-permute-start | bytes 196616 | tf_op jit(solution)/shard_map/ppermute | solution.py:634
  97.6 6.2 %collective-permute-start.29 = (f32[32,512]{1,0:T(8,128)S(1)}, f32[32,512]{1,0:T(8,128)S(1)}, u32[]{:S(2)}, u32[]{:S(2)}) collective-permute-start(f32[32,512]{1,0:T(8,128)S(1)} %get-tuple-element.303.refs_0_), channel_id=1, source_target_pairs={{0,6},{1,7},{2,4},{3,5},{4,2},{5,3},{6,0},{7,1},{8,14},{9,15},{10,... | collective-permute-start | bytes 196616 | tf_op jit(solution)/shard_map/ppermute | solution.py:634
  103.8 14.7 %copy-start.15 = (s32[2]{0:T(128)S(1)}, s32[2]{0:T(128)}, u32[]{:S(2)}) copy-start(s32[2]{0:T(128)} %copy-done.14) | copy-start | bytes 28
  104.7 6.3 %collective-permute-start.39 = (f32[64,512]{1,0:T(8,128)S(1)}, f32[64,512]{1,0:T(8,128)S(1)}, u32[]{:S(2)}, u32[]{:S(2)}) collective-permute-start(f32[64,512]{1,0:T(8,128)S(1)} %get-tuple-element.791), channel_id=1, source_target_pairs={{0,2},{1,3},{2,0},{3,1},{4,6},{5,7},{6,4},{7,5},{8,10},{9,11},{10,... | collective-permute-start | bytes 393224 | tf_op jit(solution)/shard_map/ppermute | solution.py:634
  105.5 12.9 %collective-permute-start.36 = (f32[128,512]{1,0:T(8,128)S(1)}, f32[128,512]{1,0:T(8,128)S(1)}, u32[]{:S(2)}, u32[]{:S(2)}) collective-permute-start(f32[128,512]{1,0:T(8,128)S(1)} %get-tuple-element.790), channel_id=1, source_target_pairs={{0,1},{1,0},{2,3},{3,2},{4,5},{5,4},{6,7},{7,6},{8,9},{9,8},{10,11... | collective-permute-start | bytes 786440 | tf_op jit(solution)/shard_map/ppermute | solution.py:634
  106.3 12.1 %collective-permute-start.37 = (f32[128,512]{1,0:T(8,128)S(1)}, f32[128,512]{1,0:T(8,128)S(1)}, u32[]{:S(2)}, u32[]{:S(2)}) collective-permute-start(f32[128,512]{1,0:T(8,128)S(1)} %get-tuple-element.790), channel_id=1, source_target_pairs={{0,16},{1,17},{2,18},{3,19},{4,20},{5,21},{6,22},{7,23},{8,24},{9,... | collective-permute-start | bytes 786440 | tf_op jit(solution)/shard_map/ppermute | solution.py:634
  107.7 10.7 %collective-permute-start.38 = (f32[128,512]{1,0:T(8,128)S(1)}, f32[128,512]{1,0:T(8,128)S(1)}, u32[]{:S(2)}, u32[]{:S(2)}) collective-permute-start(f32[128,512]{1,0:T(8,128)S(1)} %get-tuple-element.790), channel_id=1, source_target_pairs={{0,17},{1,16},{2,19},{3,18},{4,21},{5,20},{6,23},{7,22},{8,25},{9,... | collective-permute-start | bytes 786440 | tf_op jit(solution)/shard_map/ppermute | solution.py:634
  109.0 9.4 %collective-permute-start.40 = (f32[64,512]{1,0:T(8,128)S(1)}, f32[64,512]{1,0:T(8,128)S(1)}, u32[]{:S(2)}, u32[]{:S(2)}) collective-permute-start(f32[64,512]{1,0:T(8,128)S(1)} %get-tuple-element.791), channel_id=1, source_target_pairs={{0,4},{1,5},{2,6},{3,7},{4,0},{5,1},{6,2},{7,3},{8,12},{9,13},{10,... | collective-permute-start | bytes 393224 | tf_op jit(solution)/shard_map/ppermute | solution.py:634
  111.0 7.5 %collective-permute-start.41 = (f32[64,512]{1,0:T(8,128)S(1)}, f32[64,512]{1,0:T(8,128)S(1)}, u32[]{:S(2)}, u32[]{:S(2)}) collective-permute-start(f32[64,512]{1,0:T(8,128)S(1)} %get-tuple-element.791), channel_id=1, source_target_pairs={{0,6},{1,7},{2,4},{3,5},{4,2},{5,3},{6,0},{7,1},{8,14},{9,15},{10,... | collective-permute-start | bytes 393224 | tf_op jit(solution)/shard_map/ppermute | solution.py:634
  119.3 3.5 %collective-permute-start.42 = (f32[768,512]{1,0:T(8,128)S(1)}, f32[768,512]{1,0:T(8,128)S(1)}, u32[]{:S(2)}, u32[]{:S(2)}) collective-permute-start(f32[768,512]{1,0:T(8,128)S(1)} %collect_second.1.block), channel_id=1, source_target_pairs={{0,8},{1,9},{2,10},{3,11},{4,12},{5,13},{6,14},{7,15},{8,0},{9,1},... | collective-permute-start | bytes 4718600 | tf_op jit(solution)/shard_map/ppermute | solution.py:634
  (7 other events, 69.2 us)
